TPU v7x, 256 devices: a whole 4x4x8 slice. The times are simulated.
256 devices in a mesh: space: 128 (over y, x, z), coarse: 2 (over core).
Axes of the slice: x: 4, y: 4, z: 8, core: 2. Of those that a mesh axis runs over, the one named last changes fastest.
Arguments:
- cells: float32 [131072, 128], P('space'), may hold values from -6 to 6
- w_send: float32 [128, 128], replicated, may hold values from -0.5 to 0.5
- w_recv: float32 [128, 128], replicated, may hold values from -0.5 to 0.5
- w_msg: float32 [128, 128], replicated, may hold values from -0.5 to 0.5
- w_coarse: float32 [128, 128], replicated, may hold values from -0.5 to 0.5
- w_self: float32 [128, 128], replicated, may hold values from -0.5 to 0.5
- w_agg: float32 [128, 128], replicated, may hold values from -0.5 to 0.5
- w_up: float32 [128, 128], replicated, may hold values from -0.5 to 0.5
- w_out: float32 [128, 128], replicated, may hold values from -0.5 to 0.5
- upstream: float32 [131072, 128], P('space'), may hold values from -6 to 6
- senders: int32 [786432], P(('space', 'coarse')), may hold values from 0 to 2047
- receivers: int32 [786432], P(('space', 'coarse')), may hold values from 0 to 1023
- send_map: int32 [128, 4, 256], P('space'), may hold values from 0 to 1023
- pool_map: int32 [131072], P('space'), may hold values from 0 to 2047, as said below
- coarse_senders: int32 [12288], P('coarse'), may hold values from 0 to 2047
- coarse_receivers: int32 [12288], P('coarse'), may hold values from 0 to 1023
Outputs:
- d_cells: float32 [131072, 128], P('space')
- weight_grads: float32 [8, 128, 128], replicated
Inputs may be any that keep to these rules, and one draw needn't show every extreme that they name: `pool_map`: the cells of block d map to coarse nodes d * 16 to d * 16 + 2 * 16 - 1, taken modulo 2048.
All inputs are finite; a program needn't handle non-finite values.
Results may differ from a plain program's by a relative error of at most 0.00014.
Values sent between devices are 32-bit elements; how exact they have to be, the bound alone decides.
No kernel may reach another device: no remote copies, remote signals or barrier semaphores. Data moves between devices by JAX's collectives and lax.ppermute only.
A program may use at most 128 MiB of HBM per device.

v0:
```python
import jax
import jax.numpy as jnp
from jax import lax
from jax.sharding import PartitionSpec as P

OFFSETS = (1, -1, 2, -2)
EPSILON = 1e-05


def passed_along(array, axis, by):
    peers = lax.axis_size(axis)
    pairs = [(i, i + by) for i in range(peers) if 0 <= i + by < peers]
    return lax.ppermute(array, axis, pairs)


def matmul(left, right):
    return jnp.dot(left, right, precision=lax.Precision.HIGHEST)


def layer_norm(values):
    centered = values - jnp.mean(values, axis=-1, keepdims=True)
    variance = jnp.mean(centered * centered, axis=-1, keepdims=True)
    return centered * lax.rsqrt(variance + EPSILON)


def edge_messages(cell_table, cell_rows, w_first, w_second, w_third, edge_senders, edge_receivers):
    pre_act = matmul(cell_table[edge_senders], w_first) + matmul(
        cell_rows[edge_receivers], w_second
    )
    message = layer_norm(matmul(jax.nn.silu(pre_act), w_third))
    return jax.ops.segment_sum(message, edge_receivers, num_segments=cell_rows.shape[0])


def node_update(cell_rows, aggregate, lifted, w_self, w_agg, w_up, w_out):
    inner_sum = matmul(cell_rows, w_self) + matmul(aggregate, w_agg) + matmul(lifted, w_up)
    return cell_rows + layer_norm(matmul(jax.nn.silu(inner_sum), w_out))


def coarse_update(pooled_all, own_rows, w_coarse, coarse_senders, coarse_receivers):
    gathered = jax.ops.segment_sum(
        pooled_all[coarse_senders], coarse_receivers, num_segments=own_rows.shape[0]
    )
    return own_rows + jax.nn.silu(matmul(own_rows + gathered, w_coarse))


def shards(
    cells,
    w_send,
    w_recv,
    w_msg,
    w_coarse,
    w_self,
    w_agg,
    w_up,
    w_out,
    upstream,
    senders,
    receivers,
    send_map,
    pool_map,
    coarse_senders,
    coarse_receivers,
):
    cell_count = cells.shape[0]
    space_count = lax.axis_size("space")
    pair_count = lax.axis_size("coarse")
    space_place = lax.axis_index("space")
    pair_place = lax.axis_index("coarse")
    coarse_total = coarse_senders.shape[0] * pair_count // 6
    coarse_block = coarse_total // space_count
    own_count = coarse_total // pair_count
    slot_count = send_map.shape[2]
    pool_scale = (coarse_block / cell_count) ** 0.5
    grad_scale = (cell_count * space_count) ** (-0.5)
    received = []
    for group_index, offset in enumerate(OFFSETS):
        outgoing = cells[send_map[0, group_index]]
        received.append(passed_along(outgoing, "space", offset))
    cell_table = jnp.concatenate([cells] + received, axis=0)
    edge_senders, edge_receivers = (senders, receivers)

    def edge_part(table_values, cell_values, w_first, w_second, w_third):
        return edge_messages(
            table_values, cell_values, w_first, w_second, w_third, edge_senders, edge_receivers
        )

    partial_agg, edge_pullback = jax.vjp(edge_part, cell_table, cells, w_send, w_recv, w_msg)
    aggregate = lax.psum(partial_agg, "coarse")
    dense_sum = jax.ops.segment_sum(cells, pool_map, num_segments=coarse_total)
    pooled = lax.psum(dense_sum, "space") * pool_scale
    own_start = pair_place * own_count

    def coarse_part(pooled_all, weight_values):
        own_rows = lax.dynamic_slice_in_dim(pooled_all, own_start, own_count, 0)
        return coarse_update(pooled_all, own_rows, weight_values, coarse_senders, coarse_receivers)

    own_new, coarse_pullback = jax.vjp(coarse_part, pooled, w_coarse)
    coarse_new = lax.all_gather(own_new, "coarse", axis=0, tiled=True)
    lifted = coarse_new[pool_map]
    updated, node_pullback = jax.vjp(
        node_update, cells, aggregate, lifted, w_self, w_agg, w_up, w_out
    )
    d_direct, d_aggregate, d_lifted, g_self, g_agg, g_up, g_out = node_pullback(upstream)
    d_dense = jax.ops.segment_sum(d_lifted, pool_map, num_segments=coarse_total)
    d_coarse = lax.psum(d_dense, "space")
    pair_first = (pair_place == 0).astype(jnp.float32)
    space_first = (space_place == 0).astype(jnp.float32)
    d_own = lax.dynamic_slice_in_dim(d_coarse, own_start, own_count, 0)
    d_pooled_part, g_coarse = coarse_pullback(d_own)
    d_pooled = lax.psum(d_pooled_part, "coarse")
    d_from_pool = d_pooled[pool_map] * pool_scale
    d_table, d_cells_edge, g_send, g_recv, g_msg = edge_pullback(d_aggregate)
    d_table = d_table.at[:cell_count].add(d_cells_edge)
    d_table = lax.psum(d_table, "coarse")
    d_cells = d_direct + d_from_pool + d_table[:cell_count]
    for group_index, offset in enumerate(OFFSETS):
        start_row = cell_count + group_index * slot_count
        halo_grad = d_table[start_row : start_row + slot_count]
        returned = passed_along(halo_grad, "space", -offset)
        d_cells = d_cells.at[send_map[0, group_index]].add(returned)
    edge_share = 1.0
    grad_terms = jnp.stack(
        [
            g_send * edge_share,
            g_recv * edge_share,
            g_msg * edge_share,
            g_coarse * space_first,
            g_self * pair_first,
            g_agg * pair_first,
            g_up * pair_first,
            g_out * pair_first,
        ]
    )
    weight_grads = lax.psum(grad_terms, ("space", "coarse")) * grad_scale
    return (d_cells, weight_grads)


def solution(mesh):
    in_specs = (
        P("space", None),
        P(),
        P(),
        P(),
        P(),
        P(),
        P(),
        P(),
        P(),
        P("space", None),
        P(("space", "coarse")),
        P(("space", "coarse")),
        P("space", None, None),
        P("space"),
        P("coarse"),
        P("coarse"),
    )
    out_specs = (P("space", None), P())
    return jax.shard_map(shards, mesh=mesh, in_specs=in_specs, out_specs=out_specs, check_vma=False)
```

profile of v0, /device:TPU:1, one launch (start us, length us, event | category | flops | bytes accessed | tf_op | source)
XLA Modules:
  0.0 936.2 jit_solution(6418907680306569464)
XLA Ops:
  10.4 4.4 collective-permute-start
  17.6 5.5 collective-permute-start.2
  25.2 7.0 scatter_custom_fusion.1
  33.5 8.1 gather_fusion.5
  45.6 8.1 gather_fusion.4
  61.4 3.0 copy.22
  64.4 18.0 %scatter_custom_fusion = f32[1024,128]{1,0:T(8,128)} fusion(s32[3072]{0:T(1024)S(1)} %copy-done.37, f32[3072,128]{1,0:T(8,128)} %copy.22, f32[]{:T(128)} %constant.77.clone.1), kind=kCustom, calls=%fused_computation.98 | custom fusion | flops 393216 | bytes 524800 | tf_op jit(solution)/shard_map/jvp()/scatter-add | solution.py:31
  82.7 172.5 %all-reduce.9.cloned.1.call-done = f32[2048,128]{1,0:T(8,128)} async-done(((f32[2048,128]{1,0:T(8,128)}), f32[2048,128]{1,0:T(8,128)}) %all-reduce.9.cloned.1.call-update) | async-done | bytes 1048592 | tf_op jit(solution)/shard_map/psum | solution.py:90
  258.3 66.5 %scatter_custom_fusion.2 = f32[1024,128]{1,0:T(8,128)} fusion(f32[1024,128]{1,0:T(8,128)} %copy.33, s32[6144]{0:T(1024)S(1)} %copy-done.35, f32[2048,128]{1,0:T(8,128)} %copy-done.10, s32[6144]{0:T(1024)S(1)} %get-tuple-element.27), kind=kCustom, calls=%fused_computation.23 | custom fusion | flops 786432 | bytes 524288 | tf_op jit(solution)/shard_map/jvp()/scatter-add | solution.py:40
  332.1 12.5 %all-gather.2.cloned.1.call-done = f32[2048,128]{1,0:T(8,128)} async-done(((f32[1024,128]{1,0:T(8,128)}), f32[2048,128]{1,0:T(8,128)}) %all-gather.2.cloned.1.call-update) | async-done | bytes 1048592 | tf_op jit(solution)/shard_map/all_gather | solution.py:98
  344.6 4.0 gather_fusion.6
  355.2 11.8 %gather_fusion.8 = f32[3072,128]{1,0:T(8,128)} fusion(f32[1024,128]{1,0:T(8,128)S(1)} %fusion.82, s32[3072]{0:T(1024)} %get-tuple-element.30), kind=kCustom, calls=%fused_computation.10 | custom fusion | bytes 3158016 | tf_op jit(solution)/shard_map/transpose(jvp())/gather | solution.py:31
  367.0 3.1 copy.25
  381.6 7.6 scatter_custom_fusion.3
  390.3 18.2 %scatter_custom_fusion.5 = f32[2048,128]{1,0:T(8,128)} fusion(s32[3072]{0:T(1024)} %get-tuple-element.31, f32[3072,128]{1,0:T(8,128)} %fusion.83, f32[]{:T(128)} %constant.77.clone.1), kind=kCustom, calls=%fused_computation.84 | custom fusion | flops 393216 | bytes 1049088 | tf_op jit(solution)/shard_map/transpose(jvp())/scatter-add | solution.py:27
  409.6 17.9 %scatter_fusion = f32[1024,128]{1,0:T(8,128)S(1)} fusion(f32[1024,128]{1,0:T(8,128)S(1)} %slice.82, s32[3072]{0:T(1024)S(1)} %copy-done.38, f32[3072,128]{1,0:T(8,128)} %fusion.84), kind=kCustom, calls=%fused_computation.17 | custom fusion | flops 393216 | bytes 4730880 | tf_op jit(solution)/shard_map/transpose(jvp())/scatter-add | solution.py:28
  428.4 4.2 fusion.33
  438.2 168.0 %all-reduce.11.cloned.1.call-done = f32[2048,128]{1,0:T(8,128)} async-done(((f32[2048,128]{1,0:T(8,128)}), f32[2048,128]{1,0:T(8,128)}) %all-reduce.11.cloned.1.call-update) | async-done | bytes 1048592 | tf_op jit(solution)/shard_map/psum | solution.py:105
  614.9 53.0 %scatter_custom_fusion.4 = f32[2048,128]{1,0:T(8,128)S(1)} fusion(s32[6144]{0:T(1024)} %get-tuple-element.26, f32[]{:T(128)} %constant.77.clone.1, pred[6144]{0:T(1024)(128)(4,1)S(1)} %copy-done.40, f32[1024,128]{1,0:T(8,128)S(1)} %fusion.72, s32[6144]{0:T(1024)S(1)} %copy-done.36), kind=kCustom, calls=%fused_computation.25 | custom fusion | flops 1572864 | bytes 1604608 | tf_op jit(solution)/shard_map/transpose(jvp())/scatter-add | solution.py:41
  669.1 196.4 %all-reduce.13.cloned.1.call-done = f32[8,128,128]{2,1,0:T(8,128)} async-done(((f32[8,128,128]{2,1,0:T(8,128)}), f32[8,128,128]{2,1,0:T(8,128)}) %all-reduce.13.cloned.1.call-update) | async-done | bytes 524304 | tf_op jit(solution)/shard_map/psum | solution.py:134
  867.4 33.8 %all-reduce.15.cloned.1.call-done = (f32[2048,128]{1,0:T(8,128)}, f32[2048,128]{1,0:T(8,128)}) async-done(((f32[2048,128]{1,0:T(8,128)}, f32[2048,128]{1,0:T(8,128)}), (f32[2048,128]{1,0:T(8,128)}, f32[2048,128]{1,0:T(8,128)})) %all-reduce.15.cloned.1.call-update) | async-done | bytes 2097168 | tf_op jit(solution)/shard_map/psum | solution.py:114
  901.2 4.1 gather_fusion.7
  907.5 4.6 collective-permute-start.5
  913.4 4.9 collective-permute-start.7
  (209 shorter events, 83.3 us)
Async XLA Ops:
  7.2 50.7 %copy-start = (f32[128,128]{1,0:T(8,128)S(1)}, f32[128,128]{1,0:T(8,128)}, u32[]{:S(2)}) copy-start(f32[128,128]{1,0:T(8,128)} %param.21) | copy-start | bytes 196612
  7.2 248.0 %all-reduce.9.cloned.1.call-start = ((), (), s32[]{:S(2)}) async-start(), calls=%async_computation.1 | async-start | bytes 2097152 | tf_op jit(solution)/shard_map/psum | solution.py:90
  10.4 35.1 %collective-permute-start = (f32[256,128]{1,0:T(8,128)S(1)}, f32[256,128]{1,0:T(8,128)S(1)}, u32[]{:S(2)}, u32[]{:S(2)}) collective-permute-start(f32[256,128]{1,0:T(8,128)S(1)} %gather_fusion), channel_id=1, source_target_pairs={{0,2},{2,4},{4,6},{6,8},{8,10},{10,12},{12,14},{14,16},{16,18},{18... | collective-permute-start | bytes 393224 | tf_op jit(solution)/shard_map/ppermute | solution.py:13
  14.8 10.4 %copy-start.51 = (s32[1024]{0:T(1024)S(1)}, s32[1024]{0:T(1024)}, u32[]{:S(2)}) copy-start(s32[1024]{0:T(1024)} %param.31) | copy-start | bytes 12292
  15.6 30.0 %collective-permute-start.1 = (f32[256,128]{1,0:T(8,128)S(1)}, f32[256,128]{1,0:T(8,128)S(1)}, u32[]{:S(2)}, u32[]{:S(2)}) collective-permute-start(f32[256,128]{1,0:T(8,128)S(1)} %gather_fusion.1), channel_id=1, source_target_pairs={{2,0},{4,2},{6,4},{8,6},{10,8},{12,10},{14,12},{16,14},{18,16},{20... | collective-permute-start | bytes 393224 | tf_op jit(solution)/shard_map/ppermute | solution.py:13
  17.6 27.9 %collective-permute-start.2 = (f32[256,128]{1,0:T(8,128)S(1)}, f32[256,128]{1,0:T(8,128)S(1)}, u32[]{:S(2)}, u32[]{:S(2)}) collective-permute-start(f32[256,128]{1,0:T(8,128)S(1)} %gather_fusion.2), channel_id=1, source_target_pairs={{0,4},{2,6},{4,8},{6,10},{8,12},{10,14},{12,16},{14,18},{16,20},{1... | collective-permute-start | bytes 393224 | tf_op jit(solution)/shard_map/ppermute | solution.py:13
  23.2 9.7 %copy-start.37 = (s32[3072]{0:T(1024)S(1)}, s32[3072]{0:T(1024)}, u32[]{:S(2)}) copy-start(s32[3072]{0:T(1024)} %param.29) | copy-start | bytes 36868
  23.9 21.7 %collective-permute-start.3 = (f32[256,128]{1,0:T(8,128)S(1)}, f32[256,128]{1,0:T(8,128)S(1)}, u32[]{:S(2)}, u32[]{:S(2)}) collective-permute-start(f32[256,128]{1,0:T(8,128)S(1)} %gather_fusion.3), channel_id=1, source_target_pairs={{4,0},{6,2},{8,4},{10,6},{12,8},{14,10},{16,12},{18,14},{20,16},{2... | collective-permute-start | bytes 393224 | tf_op jit(solution)/shard_map/ppermute | solution.py:13
  32.2 297.4 %all-reduce.7.cloned.1.call-start = ((), (), s32[]{:S(2)}) async-start(), calls=%async_computation | async-start | bytes 1048576 | tf_op jit(solution)/shard_map/psum | solution.py:88
  45.6 9.3 copy-start.25
  82.5 262.2 %all-gather.2.cloned.1.call-start = ((), (), s32[]{:S(2)}) async-start(), calls=%async_computation.2 | async-start | bytes 1572864 | tf_op jit(solution)/shard_map/all_gather | solution.py:98
  327.5 278.7 %all-reduce.11.cloned.1.call-start = ((), (), s32[]{:S(2)}) async-start(), calls=%async_computation.3 | async-start | bytes 2097152 | tf_op jit(solution)/shard_map/psum | solution.py:105
  332.1 16.6 %copy-start.28 = (f32[128,128]{1,0:T(8,128)S(1)}, f32[128,128]{1,0:T(8,128)}, u32[]{:S(2)}) copy-start(f32[128,128]{1,0:T(8,128)} %param.25) | copy-start | bytes 196612
  389.2 20.4 %copy-start.38 = (s32[3072]{0:T(1024)S(1)}, s32[3072]{0:T(1024)}, u32[]{:S(2)}) copy-start(s32[3072]{0:T(1024)} %get-tuple-element.28) | copy-start | bytes 36868
  389.2 476.3 %all-reduce.13.cloned.1.call-start = ((), (), s32[]{:S(2)}) async-start(), calls=%async_computation.4 | async-start | bytes 1048576 | tf_op jit(solution)/shard_map/psum | solution.py:134
  435.4 170.9 %copy-start.56 = (f32[1024,128]{1,0:T(8,128)S(1)}, f32[1024,128]{1,0:T(8,128)}, u32[]{:S(2)}) copy-start(f32[1024,128]{1,0:T(8,128)} %get-tuple-element.42) | copy-start | bytes 1572868
  612.9 55.1 %copy-start.26 = (f32[2048,128]{1,0:T(8,128)S(1)}, f32[2048,128]{1,0:T(8,128)}, u32[]{:S(2)}) copy-start(f32[2048,128]{1,0:T(8,128)} %all-reduce.11.cloned.1.call-done) | copy-start | bytes 3145732
  612.9 288.3 %all-reduce.15.cloned.1.call-start = ((), (), s32[]{:S(2)}) async-start(), calls=%async_computation.5 | async-start | bytes 4194304 | tf_op jit(solution)/shard_map/psum | solution.py:114
  901.2 17.2 %copy-start.13 = (f32[1024,128]{1,0:T(8,128)S(1)}, f32[1024,128]{1,0:T(8,128)}, u32[]{:S(2)}) copy-start(f32[1024,128]{1,0:T(8,128)} %param.27) | copy-start | bytes 1572868
  906.1 12.9 %copy-start.50 = (s32[256,1]{0,1:T(1,128)S(1)}, s32[256,1]{0,1:T(1,128)}, u32[]{:S(2)}) copy-start(s32[256,1]{0,1:T(1,128)} %copy-done.49) | copy-start | bytes 3076
  906.1 12.9 %collective-permute-start.4 = (f32[256,128]{1,0:T(8,128)S(1)}, f32[256,128]{1,0:T(8,128)}, u32[]{:S(2)}, u32[]{:S(2)}) collective-permute-start(f32[256,128]{1,0:T(8,128)S(1)} %get-tuple-element.25), channel_id=1, source_target_pairs={{2,0},{4,2},{6,4},{8,6},{10,8},{12,10},{14,12},{16,14},{18,16},{20... | collective-permute-start | bytes 393224 | tf_op jit(solution)/shard_map/ppermute | solution.py:13
  907.5 14.0 %collective-permute-start.5 = (f32[256,128]{1,0:T(8,128)}, f32[256,128]{1,0:T(8,128)}, u32[]{:S(2)}, u32[]{:S(2)}) collective-permute-start(f32[256,128]{1,0:T(8,128)} %get-tuple-element.24), channel_id=1, source_target_pairs={{0,2},{2,4},{4,6},{6,8},{8,10},{10,12},{12,14},{14,16},{16,18},{18... | collective-permute-start | bytes 393224 | tf_op jit(solution)/shard_map/ppermute | solution.py:13
  912.1 11.9 %collective-permute-start.6 = (f32[256,128]{1,0:T(8,128)}, f32[256,128]{1,0:T(8,128)S(1)}, u32[]{:S(2)}, u32[]{:S(2)}) collective-permute-start(f32[256,128]{1,0:T(8,128)} %get-tuple-element.23), channel_id=1, source_target_pairs={{4,0},{6,2},{8,4},{10,6},{12,8},{14,10},{16,12},{18,14},{20,16},{2... | collective-permute-start | bytes 393224 | tf_op jit(solution)/shard_map/ppermute | solution.py:13
  913.4 12.8 %collective-permute-start.7 = (f32[256,128]{1,0:T(8,128)}, f32[256,128]{1,0:T(8,128)S(1)}, u32[]{:S(2)}, u32[]{:S(2)}) collective-permute-start(f32[256,128]{1,0:T(8,128)} %get-tuple-element.22), channel_id=1, source_target_pairs={{0,4},{2,6},{4,8},{6,10},{8,12},{10,14},{12,16},{14,18},{16,20},{1... | collective-permute-start | bytes 393224 | tf_op jit(solution)/shard_map/ppermute | solution.py:13
  (47 other events, 137.3 us)
Sparse Core Ops, SparseCore 0:
  32.4 222.7 all-reduce.8
  258.4 32.1 all-reduce.6
  327.7 16.9 all-gather.1
  389.3 216.8 all-reduce.10
  613.0 252.4 all-reduce.12
  868.2 32.9 all-reduce.14
where the time goes:
time: 955 us; the launch traced here: 936 us
  waiting for transfers between devices  583 us (61%)
  other arithmetic  209 us (22%)
  local copies, waits for them, and re-layouts  57.4 us (6%)
  matrix products  45.4 us (5%)
  starting transfers between devices  25.1 us (3%)
  between operations  15.4 us (2%)
    psum x1, waiting for transfers between devices, shards(): weight_grads = lax.psum(grad_terms, ('space', 'coarse')) * grad_scale  196 us
    psum x1, waiting for transfers between devices, shards(): pooled = lax.psum(dense_sum, 'space') * pool_scale  173 us
    psum x1, waiting for transfers between devices, shards(): d_coarse = lax.psum(d_dense, 'space')  168 us
    scatter-add x1, other arithmetic, coarse_update(): jax.ops.segment_sum(pooled_all[coarse_senders], coarse_receivers, num_seg...  66.5 us
    scatter-add x1, other arithmetic, coarse_update(): pooled_all[coarse_senders]  53 us
    dot_general x24, matrix products, matmul(): return jnp.dot(left, right, precision=lax.Precision.HIGHEST)  45.4 us
    psum x1, waiting for transfers between devices, shards(): d_table = lax.psum(d_table, 'coarse')  33.8 us
    ppermute x8, starting transfers between devices, passed_along(): return lax.ppermute(array, axis, pairs)  24.7 us
  transfers between devices with their start and end apart: 14, of which 5 were waited for; matrix products, arithmetic and copies ran while one was open for 26% of the time, Pallas kernels for 0%

commit v1 on v0

v1 whole, which is shorter than its diff:
```python
import functools

import jax
import jax.numpy as jnp
from jax import lax
from jax.experimental import pallas as pl
from jax.experimental.pallas import tpu as pltpu
from jax.sharding import PartitionSpec as P

EPSILON = 1e-05
LANES = 128
TILE = 512
F32 = jnp.float32
BF16 = jnp.bfloat16
VMEM_LIMIT = 48 * 1024 * 1024


def split(values):
    high = values.astype(BF16)
    low = (values - high.astype(F32)).astype(BF16)
    return jnp.concatenate([high, low], axis=1)


def fold(values):
    return values[:, :LANES] + values[:, LANES:]


def weight_pair(weight):
    pair = split(weight)
    return jnp.concatenate([pair, pair], axis=0)


def weight_pair_t(weight):
    high = weight.astype(BF16)
    low = (weight - high.astype(F32)).astype(BF16)
    stacked = jnp.concatenate([high, low], axis=0)
    return jnp.concatenate([stacked, stacked], axis=1)


def mm(left, right):
    return lax.dot_general(left, right, (((1,), (0,)), ((), ())), preferred_element_type=F32)


def mm_t(left, right):
    return lax.dot_general(left, right, (((1,), (1,)), ((), ())), preferred_element_type=F32)


def tm_m(left, right):
    return lax.dot_general(left, right, (((0,), (0,)), ((), ())), preferred_element_type=F32)


def outer(left_pair, right_pair):
    full = tm_m(left_pair, right_pair)
    return fold(full[:LANES] + full[LANES:])


def as_column(row):
    return jnp.transpose(jnp.broadcast_to(row, (LANES, LANES)))


def one_hot_rows(row, count):
    column = jnp.concatenate([as_column(row).astype(jnp.int16)] * (count // LANES), axis=1)
    place = lax.broadcasted_iota(jnp.int16, (LANES, count), 1)
    return jnp.where(column == place, jnp.ones((), BF16), jnp.zeros((), BF16))


def one_hot_columns(row, first, count):
    wide = jnp.broadcast_to(row - first, (16, LANES)).astype(jnp.int16)
    wide = jnp.concatenate([wide] * (count // 16), axis=0)
    place = lax.broadcasted_iota(jnp.int16, (count, LANES), 0)
    return jnp.where(wide == place, jnp.ones((), BF16), jnp.zeros((), BF16))


def norm_parts(values):
    centered = values - jnp.mean(values, axis=-1, keepdims=True)
    variance = jnp.mean(centered * centered, axis=-1, keepdims=True)
    scale = lax.rsqrt(variance + EPSILON)
    return centered * scale, scale


def norm_back(normed, scale, cotangent):
    shared = cotangent - normed * jnp.mean(cotangent * normed, axis=-1, keepdims=True)
    return scale * (shared - jnp.mean(shared, axis=-1, keepdims=True))


def sigmoid(values):
    return 1.0 / (1.0 + jnp.exp(-values))


def silu_slope(values, gate):
    return gate * (1.0 + values * (1.0 - gate))


def relative_pool(row, place, coarse_block, coarse_total):
    shifted = row - place * coarse_block
    return jnp.where(shifted < 0, shifted + coarse_total, shifted)


def pack_kernel(sizes, place_ref, cells_ref, send_ref, pool_ref, near_ref, far_ref, pool_out):
    coarse_block, coarse_total, scale = sizes
    core = place_ref[1]
    count = cells_ref.shape[0]
    pair = split(cells_ref[...])
    hot = []
    for chunk in range(count // LANES):
        row = relative_pool(pool_ref[chunk : chunk + 1, :], place_ref[0], coarse_block, coarse_total)
        hot.append(one_hot_columns(row, 0, 2 * coarse_block))
    pool_out[...] = fold(mm(jnp.concatenate(hot, axis=1), pair)) * scale
    per = send_ref.shape[0] // 4
    for group, out in ((0, near_ref), (1, far_ref)):
        for chunk in range(per):
            row = send_ref[pl.ds(group * 2 * per + core * per + chunk, 1), :]
            out[chunk * LANES : (chunk + 1) * LANES, :] = fold(mm(one_hot_rows(row, count), pair))


def sender_row(row, core, count, slots):
    return jnp.where(row >= count, row ^ (core * slots), row)


def edge_kernel(
    place_ref,
    cells_ref,
    near_ref,
    near_other_ref,
    far_ref,
    far_other_ref,
    w_send_ref,
    w_recv_ref,
    w_msg_ref,
    send_ref,
    recv_ref,
    pre_ref,
    hidden_ref,
    agg_ref,
    table,
    hot,
    normed,
):
    core = place_ref[1]
    count = cells_ref.shape[0]
    slots = near_ref.shape[0]
    nodes = 2 * count + 4 * slots
    edges = pre_ref.shape[0]
    w_send = weight_pair(w_send_ref[...])
    cells_pair = split(cells_ref[...])
    table[:count, :] = split(fold(mm(cells_pair, w_send)))
    for spot, part in enumerate((near_ref, near_other_ref, far_ref, far_other_ref)):
        start = count + spot * slots
        table[start : start + slots, :] = split(fold(mm(split(part[...]), w_send)))
    table[nodes - count :, :] = split(fold(mm(cells_pair, weight_pair(w_recv_ref[...]))))
    w_msg = weight_pair(w_msg_ref[...])
    chunks = TILE // LANES

    def tile(step, carry):
        start = pl.multiple_of(step * TILE, TILE)
        for chunk in range(chunks):
            place = step * chunks + chunk
            row = sender_row(send_ref[pl.ds(place, 1), :], core, count, slots)
            hot[chunk * LANES : (chunk + 1) * LANES, : nodes - count] = one_hot_rows(row, nodes - count)
            row = recv_ref[pl.ds(place, 1), :]
            hot[chunk * LANES : (chunk + 1) * LANES, nodes - count :] = one_hot_rows(row, count)
        pre = fold(mm(hot[...], table[...]))
        pre_ref[pl.ds(start, TILE), :] = pre
        hidden = fold(mm(split(pre * sigmoid(pre)), w_msg))
        hidden_ref[pl.ds(start, TILE), :] = hidden
        normed[pl.ds(start, TILE), :] = split(norm_parts(hidden)[0])
        return carry

    lax.fori_loop(0, edges // TILE, tile, 0)
    part = 256

    def gather_tile(step, carry):
        first = step * part
        across = [
            one_hot_columns(recv_ref[chunk : chunk + 1, :], first, part)
            for chunk in range(edges // LANES)
        ]
        agg_ref[pl.ds(pl.multiple_of(first, part), part), :] = fold(
            mm(jnp.concatenate(across, axis=1), normed[...])
        )
        return carry

    lax.fori_loop(0, count // part, gather_tile, 0)


def count_kernel(
    sizes, place_ref, send_ref, send_other_ref, recv_ref, recv_other_ref, into_ref, from_ref
):
    coarse_block, coarse_total = sizes
    core = place_ref[1]
    rows = 2 * coarse_block
    half = coarse_block // 2
    own = coarse_total // 2
    into_ref[...] = jnp.zeros_like(into_ref)
    from_ref[...] = jnp.zeros_like(from_ref)
    groups = into_ref.shape[0]
    chunks = send_ref.shape[0]
    batch = 8

    def parts(node):
        near = relative_pool(node, place_ref[0], coarse_block, coarse_total)
        inside = node & (coarse_block - 1)
        column = (node // coarse_block) * half + (inside & (half - 1))
        held = (inside // half) == core
        return near, column, held

    def tally(near, column, held):
        wanted = jnp.where(held & (near < rows), (column // LANES) * rows + near, -1)
        return wanted, column & (LANES - 1)

    for senders, receivers, owner in (
        (send_ref, recv_ref, core),
        (send_other_ref, recv_other_ref, 1 - core),
    ):

        def step(index, carry, senders=senders, receivers=receivers, owner=owner):
            first, second, third, fourth = [], [], [], []
            for chunk in range(batch):
                place = index * batch + chunk
                sender = senders[pl.ds(place, 1), :]
                receiver = receivers[pl.ds(place, 1), :] + owner * own
                sender_near, sender_column, sender_held = parts(sender)
                receiver_near, receiver_column, receiver_held = parts(receiver)
                wanted, low = tally(receiver_near, sender_column, sender_held)
                first.append(one_hot_columns(wanted, 0, groups))
                second.append(one_hot_columns(low, 0, LANES))
                wanted, low = tally(sender_near, receiver_column, receiver_held)
                third.append(one_hot_columns(wanted, 0, groups))
                fourth.append(one_hot_columns(low, 0, LANES))
            into_ref[...] += mm_t(jnp.concatenate(first, axis=1), jnp.concatenate(second, axis=1))
            from_ref[...] += mm_t(jnp.concatenate(third, axis=1), jnp.concatenate(fourth, axis=1))
            return carry

        lax.fori_loop(0, chunks // batch, step, 0)


def weigh_counts(count_ref, values_ref, rows):
    total = jnp.zeros((rows, LANES), F32)
    for group in range(count_ref.shape[0] // rows):
        total += jnp.dot(
            count_ref[group * rows : (group + 1) * rows, :],
            values_ref[group * LANES : (group + 1) * LANES, :],
            precision=lax.Precision.HIGHEST,
            preferred_element_type=F32,
        )
    return total


def coarse_sum_kernel(sizes, place_ref, count_ref, values_ref, sums_ref):
    coarse_block, blocks = sizes
    rows = 2 * coarse_block
    half = coarse_block // 2
    place, core = place_ref[0], place_ref[1]
    after = lax.rem(place + 1, blocks)
    sums_ref[:rows, :] = weigh_counts(count_ref, values_ref, rows)
    sums_ref[rows:, :] = jnp.zeros((rows, LANES), F32)
    for spot, block in ((0, place), (1, after)):
        own = values_ref[pl.ds(pl.multiple_of(block * half, half), half), :]
        sums_ref[pl.ds(pl.multiple_of(rows + spot * coarse_block + core * half, half), half), :] = own


def coarse_back_sum_kernel(rows, count_ref, values_ref, sums_ref):
    sums_ref[...] = weigh_counts(count_ref, values_ref, rows)


def node_kernel(
    sizes,
    place_ref,
    cells_ref,
    agg_ref,
    agg_other_ref,
    sums_ref,
    sums_other_ref,
    upstream_ref,
    pool_ref,
    w_coarse_ref,
    w_self_ref,
    w_agg_ref,
    w_up_ref,
    w_out_ref,
    d_agg_ref,
    d_direct_ref,
    d_coarse_ref,
    coarse_in_ref,
    grads_ref,
    g_self,
    g_agg,
    g_out,
    lifted_back,
):
    coarse_block, coarse_total = sizes
    rows = 2 * coarse_block
    count = cells_ref.shape[0]
    sums = sums_ref[...] + sums_other_ref[...]
    pooled = sums[rows:]
    coarse_in = pooled + sums[:rows]
    coarse_in_ref[...] = coarse_in
    coarse_pre = fold(mm(split(coarse_in), weight_pair(w_coarse_ref[...])))
    coarse_new = pooled + coarse_pre * sigmoid(coarse_pre)
    raised = fold(mm(split(coarse_new), weight_pair(w_up_ref[...])))
    raised = split(jnp.concatenate([raised, jnp.zeros((LANES - rows, LANES), F32)], axis=0))
    w_self, w_agg, w_out = w_self_ref[...], w_agg_ref[...], w_out_ref[...]
    self_pair, agg_pair, out_pair = weight_pair(w_self), weight_pair(w_agg), weight_pair(w_out)
    self_back, agg_back, out_back = weight_pair_t(w_self), weight_pair_t(w_agg), weight_pair_t(w_out)
    part = 256
    g_self[...] = jnp.zeros_like(g_self)
    g_agg[...] = jnp.zeros_like(g_agg)
    g_out[...] = jnp.zeros_like(g_out)
    lifted_back[...] = jnp.zeros_like(lifted_back)

    def tile(step, carry):
        at = pl.ds(pl.multiple_of(step * part, part), part)
        cells_pair = split(cells_ref[at, :])
        agg_pair_rows = split(agg_ref[at, :] + agg_other_ref[at, :])
        down, across = [], []
        for chunk in range(part // LANES):
            row = pool_ref[pl.ds(step * (part // LANES) + chunk, 1), :]
            row = relative_pool(row, place_ref[0], coarse_block, coarse_total)
            down.append(one_hot_rows(row, LANES))
            across.append(one_hot_columns(row, 0, rows))
        inner = fold(
            mm(cells_pair, self_pair)
            + mm(agg_pair_rows, agg_pair)
            + mm(jnp.concatenate(down, axis=0), raised)
        )
        gate = sigmoid(inner)
        active = split(inner * gate)
        normed, scale = norm_parts(fold(mm(active, out_pair)))
        upstream = upstream_ref[at, :]
        d_hidden = split(norm_back(normed, scale, upstream))
        g_out[...] += tm_m(active, d_hidden)
        d_inner = fold(mm_t(d_hidden, out_back)) * silu_slope(inner, gate)
        d_pair = split(d_inner)
        d_agg_ref[at, :] = fold(mm_t(d_pair, agg_back))
        d_direct_ref[at, :] = upstream + fold(mm_t(d_pair, self_back))
        g_self[...] += tm_m(cells_pair, d_pair)
        g_agg[...] += tm_m(agg_pair_rows, d_pair)
        lifted_back[...] += mm(jnp.concatenate(across, axis=1), d_pair)
        return carry

    lax.fori_loop(0, count // part, tile, 0)

    def combine(full):
        return fold(full[:LANES] + full[LANES:])

    inner_sums = split(fold(lifted_back[...]))
    d_coarse_ref[...] = fold(mm_t(inner_sums, weight_pair_t(w_up_ref[...])))
    grads_ref[0] = combine(g_self[...])
    grads_ref[1] = combine(g_agg[...])
    grads_ref[2] = outer(split(coarse_new), inner_sums)
    grads_ref[3] = combine(g_out[...])


def coarse_back_kernel(
    coarse_block, place_ref, own_ref, before_ref, coarse_in_ref, w_coarse_ref, base_ref, send_ref, g_ref
):
    half = coarse_block // 2
    core = place_ref[1]
    coarse_in = split(coarse_in_ref[:coarse_block, :])
    weight = w_coarse_ref[...]
    pre = fold(mm(coarse_in, weight_pair(weight)))
    d_coarse = own_ref[:coarse_block, :] + before_ref[...]
    d_pre = split(d_coarse * silu_slope(pre, sigmoid(pre)))
    d_in = fold(mm_t(d_pre, weight_pair_t(weight)))
    base_ref[...] = d_coarse + d_in
    send_ref[...] = jnp.where(core == 0, d_in[:half], d_in[half:])
    g_ref[...] = outer(coarse_in, d_pre)


def edge_back_kernel(
    place_ref,
    cells_ref,
    near_ref,
    near_other_ref,
    far_ref,
    far_other_ref,
    w_send_ref,
    w_recv_ref,
    w_msg_ref,
    send_ref,
    recv_ref,
    pre_ref,
    hidden_ref,
    d_agg_ref,
    near_back,
    near_other_back,
    far_back,
    far_other_back,
    d_cells_ref,
    grads_ref,
    d_agg,
    hot,
    d_pre,
    d_table,
    g_msg,
):
    core = place_ref[1]
    count = cells_ref.shape[0]
    slots = near_ref.shape[0]
    nodes = 2 * count + 4 * slots
    edges = pre_ref.shape[0]
    chunks = TILE // LANES
    d_agg[...] = split(d_agg_ref[...])
    msg_back = weight_pair_t(w_msg_ref[...])
    g_msg[...] = jnp.zeros_like(g_msg)

    def tile(step, carry):
        at = pl.ds(pl.multiple_of(step * TILE, TILE), TILE)
        for chunk in range(chunks):
            row = recv_ref[pl.ds(step * chunks + chunk, 1), :]
            hot[chunk * LANES : (chunk + 1) * LANES, :] = one_hot_rows(row, count)
        normed, scale = norm_parts(hidden_ref[at, :])
        d_hidden = split(norm_back(normed, scale, fold(mm(hot[...], d_agg[...]))))
        pre = pre_ref[at, :]
        gate = sigmoid(pre)
        g_msg[...] += tm_m(split(pre * gate), d_hidden)
        d_pre[at, :] = split(fold(mm_t(d_hidden, msg_back)) * silu_slope(pre, gate))
        return carry

    lax.fori_loop(0, edges // TILE, tile, 0)
    part = 256

    def scatter_tile(step, carry):
        first = step * part
        own = first < nodes - count
        across = []
        for chunk in range(edges // LANES):
            sender = sender_row(send_ref[chunk : chunk + 1, :], core, count, slots)
            receiver = recv_ref[chunk : chunk + 1, :] + (nodes - count)
            across.append(one_hot_columns(jnp.where(own, sender, receiver), first, part))
        d_table[pl.ds(pl.multiple_of(first, part), part), :] = split(
            fold(mm(jnp.concatenate(across, axis=1), d_pre[...]))
        )
        return carry

    lax.fori_loop(0, nodes // part, scatter_tile, 0)
    send_back = weight_pair_t(w_send_ref[...])
    cells_pair = split(cells_ref[...])
    g_send = tm_m(cells_pair, d_table[:count, :])
    for spot, (part_ref, back) in enumerate(
        (
            (near_ref, near_back),
            (near_other_ref, near_other_back),
            (far_ref, far_back),
            (far_other_ref, far_other_back),
        )
    ):
        start = count + spot * slots
        piece = d_table[start : start + slots, :]
        back[...] = fold(mm_t(piece, send_back))
        g_send += tm_m(split(part_ref[...]), piece)
    from_recv = d_table[nodes - count :, :]
    d_cells_ref[...] = fold(
        mm_t(d_table[:count, :], send_back) + mm_t(from_recv, weight_pair_t(w_recv_ref[...]))
    )

    def combine(full):
        return fold(full[:LANES] + full[LANES:])

    grads_ref[0] = combine(g_send)
    grads_ref[1] = outer(cells_pair, from_recv)
    grads_ref[2] = combine(g_msg[...])


def finish_kernel(
    sizes,
    place_ref,
    direct_ref,
    own_ref,
    other_ref,
    near_ref,
    near_other_ref,
    far_ref,
    far_other_ref,
    base_ref,
    base_after_ref,
    sums_ref,
    sums_other_ref,
    send_ref,
    pool_ref,
    out_ref,
):
    coarse_block, coarse_total, scale = sizes
    rows = 2 * coarse_block
    core = place_ref[1]
    count = direct_ref.shape[0]
    pooled = jnp.concatenate([base_ref[...], base_after_ref[...]], axis=0)
    pooled = (pooled + sums_ref[...] + sums_other_ref[...]) * scale
    pooled = split(jnp.concatenate([pooled, jnp.zeros((LANES - rows, LANES), F32)], axis=0))
    returned = split(
        jnp.concatenate([near_ref[...], near_other_ref[...], far_ref[...], far_other_ref[...]], axis=0)
    )
    per = send_ref.shape[0] // 4
    part = 256

    def tile(step, carry):
        first = step * part
        at = pl.ds(pl.multiple_of(first, part), part)
        across = []
        for group, place in ((0, core), (0, 1 - core), (1, core), (1, 1 - core)):
            for chunk in range(per):
                row = send_ref[pl.ds(group * 2 * per + place * per + chunk, 1), :]
                across.append(one_hot_columns(row, first, part))
        down = []
        for chunk in range(part // LANES):
            row = pool_ref[pl.ds(step * (part // LANES) + chunk, 1), :]
            row = relative_pool(row, place_ref[0], coarse_block, coarse_total)
            down.append(one_hot_rows(row, LANES))
        added = mm(jnp.concatenate(across, axis=1), returned) + mm(
            jnp.concatenate(down, axis=0), pooled
        )
        out_ref[at, :] = direct_ref[at, :] + own_ref[at, :] + other_ref[at, :] + fold(added)
        return carry

    lax.fori_loop(0, count // part, tile, 0)


def call(kernel, outs, scratch, flops, name, *operands):
    whole = pl.BlockSpec(memory_space=pltpu.VMEM)
    specs = [pl.BlockSpec(memory_space=pltpu.SMEM) if o.ndim == 1 else whole for o in operands]
    size = sum(o.size * 4 for o in operands) + sum(o.size * 4 for o in outs)
    return pl.pallas_call(
        kernel,
        out_shape=outs,
        in_specs=specs,
        out_specs=[whole] * len(outs),
        scratch_shapes=scratch,
        compiler_params=pltpu.CompilerParams(vmem_limit_bytes=VMEM_LIMIT),
        cost_estimate=pl.CostEstimate(flops=int(flops), bytes_accessed=int(size), transcendentals=0),
        name=name,
    )(*operands)


def full(*shape):
    return jax.ShapeDtypeStruct(shape, F32)


def shards(
    cells,
    w_send,
    w_recv,
    w_msg,
    w_coarse,
    w_self,
    w_agg,
    w_up,
    w_out,
    upstream,
    senders,
    receivers,
    send_map,
    pool_map,
    coarse_senders,
    coarse_receivers,
):
    count, latent = cells.shape
    blocks = lax.axis_size("space")
    place = jnp.stack([lax.axis_index("space"), lax.axis_index("coarse")]).astype(jnp.int32)
    coarse_total = coarse_senders.shape[0] * 2 // 6
    coarse_block = coarse_total // blocks
    rows = 2 * coarse_block
    half = coarse_block // 2
    slots = send_map.shape[2]
    edges = senders.shape[0]
    nodes = 2 * count + 4 * slots
    pool_scale = (coarse_block / count) ** 0.5
    grad_scale = (count * blocks) ** (-0.5)
    sizes = (coarse_block, coarse_total)

    def lanes(array):
        return array.reshape(-1, LANES)

    send_rows, recv_rows = lanes(senders), lanes(receivers)
    map_rows, pool_rows = lanes(send_map), lanes(pool_map)
    coarse_send, coarse_recv = lanes(coarse_senders), lanes(coarse_receivers)

    def other_core(array):
        return lax.ppermute(array, "coarse", [(0, 1), (1, 0)])

    def along(array, by):
        pairs = []
        for block in range(blocks):
            for core, step in ((0, by), (1, -by)):
                if 0 <= block + step < blocks:
                    pairs.append((2 * block + core, 2 * (block + step) + core))
        return lax.ppermute(array, ("space", "coarse"), pairs)

    def around(array, by):
        return lax.ppermute(array, "space", [(i, (i + by) % blocks) for i in range(blocks)])

    def everywhere(array):
        copies = jnp.broadcast_to(array[None], (blocks,) + array.shape)
        return lax.all_to_all(copies.reshape(-1, latent), "space", 0, 0, tiled=True)

    near, far, pool_part = call(
        functools.partial(pack_kernel, sizes + (pool_scale,)),
        [full(slots, latent), full(slots, latent), full(rows, latent)],
        [],
        2 * 2 * 2 * slots * count * 256,
        "pack",
        place,
        cells,
        map_rows,
        pool_rows,
    )
    pooled_own = pool_part[:coarse_block] + around(pool_part[coarse_block:], 1)
    pooled_half = lax.dynamic_slice_in_dim(pooled_own, place[1] * half, half, 0)
    pooled = everywhere(pooled_half)
    near, far = along(near, 1), along(far, 2)
    near_other, far_other = other_core(near), other_core(far)
    edge_both = other_core(jnp.concatenate([coarse_send, coarse_recv], axis=0))
    chunks = coarse_send.shape[0]
    groups = (blocks * half // LANES) * rows
    count_into, count_from = call(
        functools.partial(count_kernel, sizes),
        [full(groups, LANES), full(groups, LANES)],
        [],
        4 * 2 * groups * LANES * 12 * chunks * LANES,
        "count",
        place,
        coarse_send,
        edge_both[:chunks],
        coarse_recv,
        edge_both[chunks:],
    )
    pre, hidden, agg = call(
        edge_kernel,
        [full(edges, latent), full(edges, latent), full(count, latent)],
        [
            pltpu.VMEM((nodes, 2 * latent), BF16),
            pltpu.VMEM((TILE, nodes), BF16),
            pltpu.VMEM((edges, 2 * latent), BF16),
        ],
        2 * 2 * edges * (nodes + count) * 256,
        "edges",
        place,
        cells,
        near,
        near_other,
        far,
        far_other,
        w_send,
        w_recv,
        w_msg,
        send_rows,
        recv_rows,
    )
    agg_other = other_core(agg)
    (sums,) = call(
        functools.partial(coarse_sum_kernel, (coarse_block, blocks)),
        [full(2 * rows, latent)],
        [],
        6 * 2 * rows * blocks * half * latent,
        "coarse_sum",
        place,
        count_into,
        pooled,
    )
    sums_other = other_core(sums)
    square = pltpu.VMEM((2 * latent, 2 * latent), F32)
    d_agg, d_direct, d_coarse, coarse_in, node_grads = call(
        functools.partial(node_kernel, sizes),
        [
            full(count, latent),
            full(count, latent),
            full(rows, latent),
            full(rows, latent),
            full(4, latent, latent),
        ],
        [square, square, square, pltpu.VMEM((rows, 2 * latent), F32)],
        2 * 2 * 11 * count * 256 * 256,
        "nodes",
        place,
        cells,
        agg,
        agg_other,
        sums,
        sums_other,
        upstream,
        pool_rows,
        w_coarse,
        w_self,
        w_agg,
        w_up,
        w_out,
    )
    d_before = around(d_coarse[coarse_block:], 1)
    base, d_in_half, coarse_grad = call(
        functools.partial(coarse_back_kernel, coarse_block),
        [full(coarse_block, latent), full(half, latent), full(latent, latent)],
        [],
        1e6,
        "coarse_back",
        place,
        d_coarse,
        d_before,
        coarse_in,
        w_coarse,
    )
    base_after = around(base, -1)
    d_in = everywhere(d_in_half)
    near_back, near_other_back, far_back, far_other_back, d_cells_own, edge_grads = call(
        edge_back_kernel,
        [full(slots, latent)] * 4 + [full(count, latent), full(3, latent, latent)],
        [
            pltpu.VMEM((count, 2 * latent), BF16),
            pltpu.VMEM((TILE, count), BF16),
            pltpu.VMEM((edges, 2 * latent), BF16),
            pltpu.VMEM((nodes, 2 * latent), BF16),
            square,
        ],
        2 * 2 * edges * (nodes + count) * 256,
        "edges_back",
        place,
        cells,
        near,
        near_other,
        far,
        far_other,
        w_send,
        w_recv,
        w_msg,
        send_rows,
        recv_rows,
        pre,
        hidden,
        d_agg,
    )
    edge_grads = edge_grads + other_core(edge_grads)
    first = place[1] == 0
    mine = jnp.where(
        first, jnp.concatenate([edge_grads, coarse_grad[None]], axis=0), node_grads
    ).reshape(-1, latent)
    pieces = lax.all_to_all(mine, "space", 0, 0, tiled=True)
    reduced = jnp.sum(pieces.reshape(blocks, -1, latent), axis=0) * grad_scale
    own_grads = everywhere(reduced).reshape(-1, latent, latent)
    weight_grads = lax.all_gather(own_grads, "coarse", axis=0, tiled=True)

    near_back = near_back + other_core(near_other_back)
    far_back = far_back + other_core(far_other_back)
    near_back, far_back = along(near_back, -1), along(far_back, -2)
    d_cells_other = other_core(d_cells_own)
    (back_sums,) = call(
        functools.partial(coarse_back_sum_kernel, rows),
        [full(rows, latent)],
        [],
        6 * 2 * rows * blocks * half * latent,
        "coarse_back_sum",
        count_from,
        d_in,
    )
    (d_cells,) = call(
        functools.partial(finish_kernel, sizes + (pool_scale,)),
        [full(count, latent)],
        [],
        2 * 2 * count * 4 * slots * 256,
        "finish",
        place,
        d_direct,
        d_cells_own,
        d_cells_other,
        near_back,
        other_core(near_back),
        far_back,
        other_core(far_back),
        base,
        base_after,
        back_sums,
        other_core(back_sums),
        map_rows,
        pool_rows,
    )
    return d_cells, weight_grads


def solution(mesh):
    in_specs = (
        P("space", None),
        P(),
        P(),
        P(),
        P(),
        P(),
        P(),
        P(),
        P(),
        P("space", None),
        P(("space", "coarse")),
        P(("space", "coarse")),
        P("space", None, None),
        P("space"),
        P("coarse"),
        P("coarse"),
    )
    out_specs = (P("space", None), P())
    return jax.shard_map(shards, mesh=mesh, in_specs=in_specs, out_specs=out_specs, check_vma=False)
```

time: 955 us -> 178 us (0.19)
  the two profiles are of different devices: /device:TPU:1 before, /device:TPU:25 now
where the time goes in v1:
time: 178 us
  starting transfers between devices  66.7 us (37%)
  Pallas kernels  46.8 us (26%)
  waiting for transfers between devices  28 us (16%)
  blocking collectives  24 us (13%)
  local copies, waits for them, and re-layouts  10.6 us (6%)
    pallas_call x9, Pallas kernels, call(): pl.pallas_call(kernel, out_shape=outs, in_specs=specs, out_specs=[whole]...  46.8 us
    all_to_all x3, starting transfers between devices, everywhere(): return lax.all_to_all(copies.reshape(-1, latent), 'space', 0, 0, tiled=True)  26.6 us
    all_to_all x1, blocking collectives, shards(): pieces = lax.all_to_all(mine, 'space', 0, 0, tiled=True)  20.9 us
    ppermute x4, starting transfers between devices, along(): return lax.ppermute(array, ('space', 'coarse'), pairs)  19.1 us
    all_to_all x3, waiting for transfers between devices, everywhere(): return lax.all_to_all(copies.reshape(-1, latent), 'space', 0, 0, tiled=True)  13.1 us
    ppermute x12, starting transfers between devices, other_core(): return lax.ppermute(array, 'coarse', [(0, 1), (1, 0)])  11.3 us
    ppermute x3, starting transfers between devices, around(): lax.ppermute(array, 'space', [(i, (i + by) % blocks) for i in range(block...  9.67 us
    unnamed x61, local copies, waits for them, and re-layouts  7.45 us
  transfers between devices with their start and end apart: 22, of which 9 were waited for; matrix products, arithmetic and copies ran while one was open for 1% of the time, Pallas kernels for 13%

profile of v1, /device:TPU:25, one launch (start us, length us, event | category | flops | bytes accessed | tf_op | source)
XLA Modules:
  0.0 177.6 jit_solution(15612094292134739269)
XLA Ops:
  4.3 1.7 collective-permute-start.6
  6.0 8.2 %collective-permute-start = (f32[256,128]{1,0:T(8,128)S(1)}, f32[256,128]{1,0:T(8,128)S(1)}, u32[]{:S(2)}, u32[]{:S(2)}) collective-permute-start(f32[256,128]{1,0:T(8,128)S(1)} %get-tuple-element.24), channel_id=1, source_target_pairs={{0,2},{2,4},{3,1},{4,6},{5,3},{6,8},{7,5},{8,10},{9,7},{10,12},{11... | collective-permute-start | bytes 393224 | tf_op jit(solution)/shard_map/ppermute | solution.py:586
  14.2 3.8 %collective-permute-start.2 = (f32[256,128]{1,0:T(8,128)S(1)}, f32[256,128]{1,0:T(8,128)S(1)}, u32[]{:S(2)}, u32[]{:S(2)}) collective-permute-start(f32[256,128]{1,0:T(8,128)S(1)} %get-tuple-element.25), channel_id=1, source_target_pairs={{0,4},{2,6},{4,8},{5,1},{6,10},{7,3},{8,12},{9,5},{10,14},{11,7},{... | collective-permute-start | bytes 393224 | tf_op jit(solution)/shard_map/ppermute | solution.py:586
  19.0 8.9 %all-to-all-start = ((f32[128,8,128]{2,1,0:T(8,128)}), f32[128,8,128]{2,1,0:T(8,128)S(1)}, u32[]{:S(2)}, u32[]{:S(2)}) async-start(f32[128,8,128]{2,1,0:T(8,128)} %broadcast_in_dim.8), calls=%async_computation | async-start | bytes 1048576 | tf_op jit(solution)/shard_map/all_to_all | solution.py:593
  30.1 11.8 %edges.1 = (f32[3072,128]{1,0:T(8,128)S(1)}, f32[3072,128]{1,0:T(8,128)S(1)}, f32[1024,128]{1,0:T(8,128)S(1)}) custom-call(s32[2]{0:T(128)S(1)} %pad_add_fusion.1.place_ref, f32[1024,128]{1,0:T(8,128)S(1)} %copy-done.5, f32[256,128]{1,0:T(8,128)S(1)} %collective-permute-done.near_ref, f32[256,128]{1,0:T(8,128)S(1)} %collective-permute-done.1.near_other_ref, ...), custom_call_target="tpu_custom_call" | custom-call | flops 12884901888 | bytes 4939784 | tf_op jit(solution)/shard_map/edges/pallas_call | solution.py:522
  44.4 6.5 %count.1 = (f32[256,128]{1,0:T(8,128)S(1)}, f32[256,128]{1,0:T(8,128)S(1)}) custom-call(s32[2]{0:T(128)S(1)} %pad_add_fusion.1.place_ref, s32[48,128]{1,0:T(8,128)S(1)} %bitcast.16, s32[48,128]{1,0:T(8,128)S(1)} %get-tuple-element.47.send_other_ref, s32[48,128]{1,0:T(8,128)S(1)} %bitcast.18, s32[48,128]{1,0:T(8,128)S(1)} %get-tuple-element.46.recv_other_ref), custom_call_target="tpu_custom_call" | custom-call | flops 19327352832 | bytes 360456 | tf_op jit(solution)/shard_map/count/pallas_call | solution.py:522
  56.0 6.3 %nodes.1 = (f32[1024,128]{1,0:T(8,128)S(1)}, f32[1024,128]{1,0:T(8,128)S(1)}, f32[32,128]{1,0:T(8,128)S(1)}, f32[32,128]{1,0:T(8,128)S(1)}, f32[4,128,128]{2,1,0:T(8,128)S(1)}) custom-call(s32[2]{0:T(128)S(1)} %pad_add_fusion.1.place_ref, f32[1024,128]{1,0:T(8,128)S(1)} %copy-done.5, f32[1024,128]{1,0:T(8,128)S(1)} %get-tuple-element.26.agg_ref, ...), custom_call_target="tpu_custom_call" | custom-call | flops 2952790016 | bytes 3837960 | tf_op jit(solution)/shard_map/nodes/pallas_call | solution.py:522
  62.4 15.7 %edges_back.1 = (f32[256,128]{1,0:T(8,128)S(1)}, f32[256,128]{1,0:T(8,128)S(1)}, f32[256,128]{1,0:T(8,128)S(1)}, f32[256,128]{1,0:T(8,128)S(1)}, f32[1024,128]{1,0:T(8,128)S(1)}, /*index=5*/f32[3,128,128]{2,1,0:T(8,128)S(1)}) custom-call(s32[2]{0:T(128)S(1)} %pad_add_fusion.1.place_ref, f32[1024,128]{1,0:T(8,128)S(1)} %copy-done.5, ...), custom_call_target="tpu_custom_call" | custom-call | flops 12884901888 | bytes 6184968 | tf_op jit(solution)/shard_map/edges_back/pallas_call | solution.py:522
  78.5 1.2 collective-permute-start.15
  79.7 5.5 %collective-permute-done.15.before_ref = f32[16,128]{1,0:T(8,128)S(1)} collective-permute-done((f32[16,128]{1,0:T(8,128)S(1)}, f32[16,128]{1,0:T(8,128)S(1)}, u32[]{:S(2)}, u32[]{:S(2)}) %collective-permute-start.15) | collective-permute-done | bytes 8224 | tf_op jit(solution)/shard_map/ppermute | solution.py:589
  86.2 20.9 %all_to_all.31 = f32[128,4,128]{2,1,0:T(4,128)S(1)} all-to-all(f32[128,4,128]{2,1,0:T(4,128)S(1)} %bitcast.27), channel_id=1, replica_groups=mesh['space'=128,'coarse'=2] {'space'}, dimensions={0} | all-to-all | bytes 524288 | tf_op jit(solution)/shard_map/all_to_all | solution.py:734
  108.0 9.2 %all-to-all-start.1 = ((f32[128,8,128]{2,1,0:T(8,128)}), f32[128,8,128]{2,1,0:T(8,128)S(1)}, u32[]{:S(2)}, u32[]{:S(2)}) async-start(f32[128,8,128]{2,1,0:T(8,128)} %broadcast_in_dim.9), calls=%async_computation.1 | async-start | bytes 1048576 | tf_op jit(solution)/shard_map/all_to_all | solution.py:593
  117.2 2.6 %collective-permute-start.8 = (f32[1024,128]{1,0:T(8,128)S(1)}, f32[1024,128]{1,0:T(8,128)S(1)}, u32[]{:S(2)}, u32[]{:S(2)}) collective-permute-start(f32[1024,128]{1,0:T(8,128)S(1)} %get-tuple-element.33.own_ref), channel_id=1, source_target_pairs={{0,1},{1,0},{2,3},{3,2},{4,5},{5,4},{6,7},{7,6},{8,9},{9,8},{10,11... | collective-permute-start | bytes 1572872 | tf_op jit(solution)/shard_map/ppermute | solution.py:578
  119.9 13.1 %all-to-all-done.1 = f32[128,8,128]{2,1,0:T(8,128)S(1)} async-done(((f32[128,8,128]{2,1,0:T(8,128)}), f32[128,8,128]{2,1,0:T(8,128)S(1)}, u32[]{:S(2)}, u32[]{:S(2)}) %all-to-all-start.1) | async-done | bytes 524320 | tf_op jit(solution)/shard_map/all_to_all | solution.py:593
  133.8 8.5 %all-to-all-start.3 = ((f32[128,4,128]{2,1,0:T(4,128)}), f32[128,4,128]{2,1,0:T(4,128)S(1)}, u32[]{:S(2)}, u32[]{:S(2)}) async-start(f32[128,4,128]{2,1,0:T(4,128)} %broadcast_in_dim.11), calls=%async_computation.3 | async-start | bytes 524288 | tf_op jit(solution)/shard_map/all_to_all | solution.py:593
  142.3 4.0 %collective-permute-start.9 = (f32[256,128]{1,0:T(8,128)S(1)}, f32[256,128]{1,0:T(8,128)S(1)}, u32[]{:S(2)}, u32[]{:S(2)}) collective-permute-start(f32[256,128]{1,0:T(8,128)S(1)} %get-tuple-element.35), channel_id=1, source_target_pairs={{0,1},{1,0},{2,3},{3,2},{4,5},{5,4},{6,7},{7,6},{8,9},{9,8},{10,11... | collective-permute-start | bytes 393224 | tf_op jit(solution)/shard_map/ppermute | solution.py:578
  147.3 3.1 %collective-permute-start.10 = (f32[256,128]{1,0:T(8,128)S(1)}, f32[256,128]{1,0:T(8,128)S(1)}, u32[]{:S(2)}, u32[]{:S(2)}) collective-permute-start(f32[256,128]{1,0:T(8,128)S(1)} %add.17), channel_id=1, source_target_pairs={{1,3},{2,0},{3,5},{4,2},{5,7},{6,4},{7,9},{8,6},{9,11},{10,8},{11,... | collective-permute-start | bytes 393224 | tf_op jit(solution)/shard_map/ppermute | solution.py:586
  150.4 4.0 %collective-permute-start.13 = (f32[256,128]{1,0:T(8,128)S(1)}, f32[256,128]{1,0:T(8,128)S(1)}, u32[]{:S(2)}, u32[]{:S(2)}) collective-permute-start(f32[256,128]{1,0:T(8,128)S(1)} %add.18), channel_id=1, source_target_pairs={{1,5},{3,7},{4,0},{5,9},{6,2},{7,11},{8,4},{9,13},{10,6},{11,15},{... | collective-permute-start | bytes 393224 | tf_op jit(solution)/shard_map/ppermute | solution.py:586
  154.5 2.9 %collective-permute-done.10.near_ref = f32[256,128]{1,0:T(8,128)S(1)} collective-permute-done((f32[256,128]{1,0:T(8,128)S(1)}, f32[256,128]{1,0:T(8,128)S(1)}, u32[]{:S(2)}, u32[]{:S(2)}) %collective-permute-start.10) | collective-permute-done | bytes 131104 | tf_op jit(solution)/shard_map/ppermute | solution.py:586
  157.3 1.7 collective-permute-start.11
  159.0 2.7 %collective-permute-done.13.far_ref = f32[256,128]{1,0:T(8,128)S(1)} collective-permute-done((f32[256,128]{1,0:T(8,128)S(1)}, f32[256,128]{1,0:T(8,128)S(1)}, u32[]{:S(2)}, u32[]{:S(2)}) %collective-permute-start.13) | collective-permute-done | bytes 131104 | tf_op jit(solution)/shard_map/ppermute | solution.py:586
  163.1 6.8 %collective-permute-start.16 = (f32[16,128]{1,0:T(8,128)S(1)}, f32[16,128]{1,0:T(8,128)S(1)}, u32[]{:S(2)}, u32[]{:S(2)}) collective-permute-start(f32[16,128]{1,0:T(8,128)S(1)} %get-tuple-element.40.base_ref), channel_id=1, source_target_pairs={{0,254},{2,0},{4,2},{6,4},{8,6},{10,8},{12,10},{14,12},{16,14},{18... | collective-permute-start | bytes 24584 | tf_op jit(solution)/shard_map/ppermute | solution.py:589
  170.7 3.0 %finish.1 = f32[1024,128]{1,0:T(8,128)} custom-call(s32[2]{0:T(128)S(1)} %pad_add_fusion.1.place_ref, f32[1024,128]{1,0:T(8,128)S(1)} %copy-done.25, f32[1024,128]{1,0:T(8,128)S(1)} %get-tuple-element.33.own_ref, f32[1024,128]{1,0:T(8,128)S(1)} %collective-permute-done.8.other_ref, f32[256,128]{1,0:T(8,128)S(1)} %collective-permute-done.10.near_ref, ...), custom_call_target="tpu_custom_call" | custom-call | flops 1073741824 | bytes 2678792 | tf_op jit(solution)/shard_map/finish/pallas_call | solution.py:522
  173.7 3.1 %all_gather.3 = f32[8,128,128]{2,1,0:T(8,128)S(1)} all-gather(f32[4,128,128]{2,1,0:T(8,128)S(1)} %bitcast.26), channel_id=1, replica_groups=mesh['space'=128,'coarse'=2] {'coarse'}, dimensions={0}, use_global_device_ids=true | all-gather | bytes 786432 | tf_op jit(solution)/shard_map/all_gather | solution.py:737
  (108 shorter events, 21.2 us)
Async XLA Ops:
  3.2 26.9 %copy-start.18 = (s32[3072]{0:T(1024)S(1)}, s32[3072]{0:T(1024)}, u32[]{:S(2)}) copy-start(s32[3072]{0:T(1024)} %param.26) | copy-start | bytes 36868
  4.3 13.9 %collective-permute-start.6 = (f32[16,128]{1,0:T(8,128)S(1)}, f32[16,128]{1,0:T(8,128)S(1)}, u32[]{:S(2)}, u32[]{:S(2)}) collective-permute-start(f32[16,128]{1,0:T(8,128)S(1)} %get-tuple-element.49), channel_id=1, source_target_pairs={{0,2},{2,4},{4,6},{6,8},{8,10},{10,12},{12,14},{14,16},{16,18},{18... | collective-permute-start | bytes 24584 | tf_op jit(solution)/shard_map/ppermute | solution.py:589
  6.0 22.0 %collective-permute-start = (f32[256,128]{1,0:T(8,128)S(1)}, f32[256,128]{1,0:T(8,128)S(1)}, u32[]{:S(2)}, u32[]{:S(2)}) collective-permute-start(f32[256,128]{1,0:T(8,128)S(1)} %get-tuple-element.24), channel_id=1, source_target_pairs={{0,2},{2,4},{3,1},{4,6},{5,3},{6,8},{7,5},{8,10},{9,7},{10,12},{11... | collective-permute-start | bytes 393224 | tf_op jit(solution)/shard_map/ppermute | solution.py:586
  14.2 14.4 %collective-permute-start.2 = (f32[256,128]{1,0:T(8,128)S(1)}, f32[256,128]{1,0:T(8,128)S(1)}, u32[]{:S(2)}, u32[]{:S(2)}) collective-permute-start(f32[256,128]{1,0:T(8,128)S(1)} %get-tuple-element.25), channel_id=1, source_target_pairs={{0,4},{2,6},{4,8},{5,1},{6,10},{7,3},{8,12},{9,5},{10,14},{11,7},{... | collective-permute-start | bytes 393224 | tf_op jit(solution)/shard_map/ppermute | solution.py:586
  18.1 10.7 %collective-permute-start.5 = (s32[96,128]{1,0:T(8,128)S(1)}, s32[96,128]{1,0:T(8,128)S(1)}, u32[]{:S(2)}, u32[]{:S(2)}) collective-permute-start(s32[96,128]{1,0:T(8,128)S(1)} %pad_add_fusion), channel_id=1, source_target_pairs={{0,1},{1,0},{2,3},{3,2},{4,5},{5,4},{6,7},{7,6},{8,9},{9,8},{10,11... | collective-permute-start | bytes 147464 | tf_op jit(solution)/shard_map/ppermute | solution.py:578
  19.0 31.9 %all-to-all-start = ((f32[128,8,128]{2,1,0:T(8,128)}), f32[128,8,128]{2,1,0:T(8,128)S(1)}, u32[]{:S(2)}, u32[]{:S(2)}) async-start(f32[128,8,128]{2,1,0:T(8,128)} %broadcast_in_dim.8), calls=%async_computation | async-start | bytes 1048576 | tf_op jit(solution)/shard_map/all_to_all | solution.py:593
  28.0 1.7 collective-permute-start.1
  28.7 1.3 collective-permute-start.3
  44.2 8.4 %collective-permute-start.4 = (f32[1024,128]{1,0:T(8,128)S(1)}, f32[1024,128]{1,0:T(8,128)S(1)}, u32[]{:S(2)}, u32[]{:S(2)}) collective-permute-start(f32[1024,128]{1,0:T(8,128)S(1)} %get-tuple-element.26.agg_ref), channel_id=1, source_target_pairs={{0,1},{1,0},{2,3},{3,2},{4,5},{5,4},{6,7},{7,6},{8,9},{9,8},{10,11... | collective-permute-start | bytes 1572872 | tf_op jit(solution)/shard_map/ppermute | solution.py:578
  52.0 1.4 collective-permute-start.7
  78.1 8.1 %collective-permute-start.18 = (f32[3,128,128]{2,1,0:T(8,128)S(1)}, f32[3,128,128]{2,1,0:T(8,128)S(1)}, u32[]{:S(2)}, u32[]{:S(2)}) collective-permute-start(f32[3,128,128]{2,1,0:T(8,128)S(1)} %get-tuple-element.43), channel_id=1, source_target_pairs={{0,1},{1,0},{2,3},{3,2},{4,5},{5,4},{6,7},{7,6},{8,9},{9,8},{10,11... | collective-permute-start | bytes 589832 | tf_op jit(solution)/shard_map/ppermute | solution.py:578
  78.5 6.7 %collective-permute-start.15 = (f32[16,128]{1,0:T(8,128)S(1)}, f32[16,128]{1,0:T(8,128)S(1)}, u32[]{:S(2)}, u32[]{:S(2)}) collective-permute-start(f32[16,128]{1,0:T(8,128)S(1)} %slice.19), channel_id=1, source_target_pairs={{0,2},{2,4},{4,6},{6,8},{8,10},{10,12},{12,14},{14,16},{16,18},{18... | collective-permute-start | bytes 24584 | tf_op jit(solution)/shard_map/ppermute | solution.py:589
  108.0 62.7 %copy-start.25 = (f32[1024,128]{1,0:T(8,128)S(1)}, f32[1024,128]{1,0:T(8,128)}, u32[]{:S(2)}) copy-start(f32[1024,128]{1,0:T(8,128)} %copy-done.24) | copy-start | bytes 1572868
  108.0 25.1 %all-to-all-start.1 = ((f32[128,8,128]{2,1,0:T(8,128)}), f32[128,8,128]{2,1,0:T(8,128)S(1)}, u32[]{:S(2)}, u32[]{:S(2)}) async-start(f32[128,8,128]{2,1,0:T(8,128)} %broadcast_in_dim.9), calls=%async_computation.1 | async-start | bytes 1048576 | tf_op jit(solution)/shard_map/all_to_all | solution.py:593
  117.2 53.5 %collective-permute-start.8 = (f32[1024,128]{1,0:T(8,128)S(1)}, f32[1024,128]{1,0:T(8,128)S(1)}, u32[]{:S(2)}, u32[]{:S(2)}) collective-permute-start(f32[1024,128]{1,0:T(8,128)S(1)} %get-tuple-element.33.own_ref), channel_id=1, source_target_pairs={{0,1},{1,0},{2,3},{3,2},{4,5},{5,4},{6,7},{7,6},{8,9},{9,8},{10,11... | collective-permute-start | bytes 1572872 | tf_op jit(solution)/shard_map/ppermute | solution.py:578
  133.8 39.9 %all-to-all-start.3 = ((f32[128,4,128]{2,1,0:T(4,128)}), f32[128,4,128]{2,1,0:T(4,128)S(1)}, u32[]{:S(2)}, u32[]{:S(2)}) async-start(f32[128,4,128]{2,1,0:T(4,128)} %broadcast_in_dim.11), calls=%async_computation.3 | async-start | bytes 524288 | tf_op jit(solution)/shard_map/all_to_all | solution.py:593
  142.3 5.0 %collective-permute-start.9 = (f32[256,128]{1,0:T(8,128)S(1)}, f32[256,128]{1,0:T(8,128)S(1)}, u32[]{:S(2)}, u32[]{:S(2)}) collective-permute-start(f32[256,128]{1,0:T(8,128)S(1)} %get-tuple-element.35), channel_id=1, source_target_pairs={{0,1},{1,0},{2,3},{3,2},{4,5},{5,4},{6,7},{7,6},{8,9},{9,8},{10,11... | collective-permute-start | bytes 393224 | tf_op jit(solution)/shard_map/ppermute | solution.py:578
  146.3 4.1 %collective-permute-start.12 = (f32[256,128]{1,0:T(8,128)S(1)}, f32[256,128]{1,0:T(8,128)S(1)}, u32[]{:S(2)}, u32[]{:S(2)}) collective-permute-start(f32[256,128]{1,0:T(8,128)S(1)} %get-tuple-element.37), channel_id=1, source_target_pairs={{0,1},{1,0},{2,3},{3,2},{4,5},{5,4},{6,7},{7,6},{8,9},{9,8},{10,11... | collective-permute-start | bytes 393224 | tf_op jit(solution)/shard_map/ppermute | solution.py:578
  147.3 10.0 %collective-permute-start.10 = (f32[256,128]{1,0:T(8,128)S(1)}, f32[256,128]{1,0:T(8,128)S(1)}, u32[]{:S(2)}, u32[]{:S(2)}) collective-permute-start(f32[256,128]{1,0:T(8,128)S(1)} %add.17), channel_id=1, source_target_pairs={{1,3},{2,0},{3,5},{4,2},{5,7},{6,4},{7,9},{8,6},{9,11},{10,8},{11,... | collective-permute-start | bytes 393224 | tf_op jit(solution)/shard_map/ppermute | solution.py:586
  150.4 11.3 %collective-permute-start.13 = (f32[256,128]{1,0:T(8,128)S(1)}, f32[256,128]{1,0:T(8,128)S(1)}, u32[]{:S(2)}, u32[]{:S(2)}) collective-permute-start(f32[256,128]{1,0:T(8,128)S(1)} %add.18), channel_id=1, source_target_pairs={{1,5},{3,7},{4,0},{5,9},{6,2},{7,11},{8,4},{9,13},{10,6},{11,15},{... | collective-permute-start | bytes 393224 | tf_op jit(solution)/shard_map/ppermute | solution.py:586
  157.3 13.3 %collective-permute-start.11 = (f32[256,128]{1,0:T(8,128)S(1)}, f32[256,128]{1,0:T(8,128)S(1)}, u32[]{:S(2)}, u32[]{:S(2)}) collective-permute-start(f32[256,128]{1,0:T(8,128)S(1)} %collective-permute-done.10.near_ref), channel_id=1, source_target_pairs={{0,1},{1,0},{2,3},{3,2},{4,5},{5,4},{6,7},{7,6},{8,9},{9,8},{10,11... | collective-permute-start | bytes 393224 | tf_op jit(solution)/shard_map/ppermute | solution.py:578
  161.8 8.9 %collective-permute-start.14 = (f32[256,128]{1,0:T(8,128)S(1)}, f32[256,128]{1,0:T(8,128)S(1)}, u32[]{:S(2)}, u32[]{:S(2)}) collective-permute-start(f32[256,128]{1,0:T(8,128)S(1)} %collective-permute-done.13.far_ref), channel_id=1, source_target_pairs={{0,1},{1,0},{2,3},{3,2},{4,5},{5,4},{6,7},{7,6},{8,9},{9,8},{10,11... | collective-permute-start | bytes 393224 | tf_op jit(solution)/shard_map/ppermute | solution.py:578
  163.1 7.6 %collective-permute-start.17 = (f32[32,128]{1,0:T(8,128)S(1)}, f32[32,128]{1,0:T(8,128)S(1)}, u32[]{:S(2)}, u32[]{:S(2)}) collective-permute-start(f32[32,128]{1,0:T(8,128)S(1)} %coarse_back_sum.1.sums_ref), channel_id=1, source_target_pairs={{0,1},{1,0},{2,3},{3,2},{4,5},{5,4},{6,7},{7,6},{8,9},{9,8},{10,11... | collective-permute-start | bytes 49160 | tf_op jit(solution)/shard_map/ppermute | solution.py:578
  163.1 7.6 %collective-permute-start.16 = (f32[16,128]{1,0:T(8,128)S(1)}, f32[16,128]{1,0:T(8,128)S(1)}, u32[]{:S(2)}, u32[]{:S(2)}) collective-permute-start(f32[16,128]{1,0:T(8,128)S(1)} %get-tuple-element.40.base_ref), channel_id=1, source_target_pairs={{0,254},{2,0},{4,2},{6,4},{8,6},{10,8},{12,10},{14,12},{16,14},{18... | collective-permute-start | bytes 24584 | tf_op jit(solution)/shard_map/ppermute | solution.py:589
  (28 other events, 319.8 us)

commit v2 on v1

--- a/solution.py
+++ b/solution.py
@@ -9,10 +9,9 @@
 
 EPSILON = 1e-05
 LANES = 128
-TILE = 512
+TILE = 1024
 F32 = jnp.float32
 BF16 = jnp.bfloat16
-VMEM_LIMIT = 48 * 1024 * 1024
 
 
 def split(values):
@@ -94,6 +93,12 @@
 def relative_pool(row, place, coarse_block, coarse_total):
     shifted = row - place * coarse_block
     return jnp.where(shifted < 0, shifted + coarse_total, shifted)
+
+
+def map_row(send_ref, group, core, chunk):
+    at = slice(chunk * LANES, (chunk + 1) * LANES)
+    first, second = send_ref[0, 2 * group : 2 * group + 1, at], send_ref[0, 2 * group + 1 : 2 * group + 2, at]
+    return jnp.where(core == 0, first, second)
 
 
 def pack_kernel(sizes, place_ref, cells_ref, send_ref, pool_ref, near_ref, far_ref, pool_out):
@@ -106,10 +111,9 @@
         row = relative_pool(pool_ref[chunk : chunk + 1, :], place_ref[0], coarse_block, coarse_total)
         hot.append(one_hot_columns(row, 0, 2 * coarse_block))
     pool_out[...] = fold(mm(jnp.concatenate(hot, axis=1), pair)) * scale
-    per = send_ref.shape[0] // 4
     for group, out in ((0, near_ref), (1, far_ref)):
-        for chunk in range(per):
-            row = send_ref[pl.ds(group * 2 * per + core * per + chunk, 1), :]
+        for chunk in range(out.shape[0] // LANES):
+            row = map_row(send_ref, group, core, chunk)
             out[chunk * LANES : (chunk + 1) * LANES, :] = fold(mm(one_hot_rows(row, count), pair))
 
 
@@ -167,7 +171,7 @@
         return carry
 
     lax.fori_loop(0, edges // TILE, tile, 0)
-    part = 256
+    part = 512
 
     def gather_tile(step, carry):
         first = step * part
@@ -184,29 +188,18 @@
 
 
 def count_kernel(
-    sizes, place_ref, send_ref, send_other_ref, recv_ref, recv_other_ref, into_ref, from_ref
+    sizes, into, place_ref, send_ref, send_other_ref, recv_ref, recv_other_ref, *rest
 ):
+    count_ref = rest[-1]
     coarse_block, coarse_total = sizes
     core = place_ref[1]
     rows = 2 * coarse_block
     half = coarse_block // 2
     own = coarse_total // 2
-    into_ref[...] = jnp.zeros_like(into_ref)
-    from_ref[...] = jnp.zeros_like(from_ref)
-    groups = into_ref.shape[0]
+    count_ref[...] = jnp.zeros_like(count_ref)
+    groups = count_ref.shape[0]
     chunks = send_ref.shape[0]
     batch = 8
-
-    def parts(node):
-        near = relative_pool(node, place_ref[0], coarse_block, coarse_total)
-        inside = node & (coarse_block - 1)
-        column = (node // coarse_block) * half + (inside & (half - 1))
-        held = (inside // half) == core
-        return near, column, held
-
-    def tally(near, column, held):
-        wanted = jnp.where(held & (near < rows), (column // LANES) * rows + near, -1)
-        return wanted, column & (LANES - 1)
 
     for senders, receivers, owner in (
         (send_ref, recv_ref, core),
@@ -214,21 +207,21 @@
     ):
 
         def step(index, carry, senders=senders, receivers=receivers, owner=owner):
-            first, second, third, fourth = [], [], [], []
+            first, second = [], []
             for chunk in range(batch):
                 place = index * batch + chunk
                 sender = senders[pl.ds(place, 1), :]
                 receiver = receivers[pl.ds(place, 1), :] + owner * own
-                sender_near, sender_column, sender_held = parts(sender)
-                receiver_near, receiver_column, receiver_held = parts(receiver)
-                wanted, low = tally(receiver_near, sender_column, sender_held)
-                first.append(one_hot_columns(wanted, 0, groups))
-                second.append(one_hot_columns(low, 0, LANES))
-                wanted, low = tally(sender_near, receiver_column, receiver_held)
-                third.append(one_hot_columns(wanted, 0, groups))
-                fourth.append(one_hot_columns(low, 0, LANES))
-            into_ref[...] += mm_t(jnp.concatenate(first, axis=1), jnp.concatenate(second, axis=1))
-            from_ref[...] += mm_t(jnp.concatenate(third, axis=1), jnp.concatenate(fourth, axis=1))
+                near, distant = (receiver, sender) if into else (sender, receiver)
+                near = relative_pool(near, place_ref[0], coarse_block, coarse_total)
+                inside = distant & (coarse_block - 1)
+                column = (distant // coarse_block) * half + (inside & (half - 1))
+                wanted = ((inside // half) == core) & (near < rows)
+                first.append(
+                    one_hot_columns(jnp.where(wanted, (column // LANES) * rows + near, -1), 0, groups)
+                )
+                second.append(one_hot_columns(column & (LANES - 1), 0, LANES))
+            count_ref[...] += mm_t(jnp.concatenate(first, axis=1), jnp.concatenate(second, axis=1))
             return carry
 
         lax.fori_loop(0, chunks // batch, step, 0)
@@ -259,8 +252,33 @@
         sums_ref[pl.ds(pl.multiple_of(rows + spot * coarse_block + core * half, half), half), :] = own
 
 
-def coarse_back_sum_kernel(rows, count_ref, values_ref, sums_ref):
-    sums_ref[...] = weigh_counts(count_ref, values_ref, rows)
+def coarse_back_sum_kernel(sizes, place_ref, count_ref, packed_ref, sums_ref, values):
+    coarse_block, blocks = sizes
+    rows = 2 * coarse_block
+    half = coarse_block // 2
+    packed = packed_ref[...]
+    low = lax.broadcasted_iota(jnp.int32, packed[:, :8].shape, 1) < 4
+    second = jnp.where(low, packed[:, 16:], packed[:, 8:16])
+    second = jnp.concatenate([second[:, 4:], second[:, :4]], axis=1)
+    values[...] = jnp.concatenate([packed[:, :8], second], axis=1)
+    flat = values[...].reshape(-1, LANES)
+    core = place_ref[1]
+    spread = lax.broadcasted_iota(jnp.int32, (coarse_block, LANES), 0) // half == core
+    own = []
+    for block in (place_ref[0], lax.rem(place_ref[0] + 1, blocks)):
+        pair = values[block // 2]
+        mine = jnp.where(lax.rem(block, 2) == 0, pair[:half], pair[half:])
+        own.append(jnp.where(spread, jnp.concatenate([mine, mine], axis=0), 0.0))
+    total = jnp.concatenate(own, axis=0)
+    total += jnp.zeros((rows, LANES), F32)
+    for group in range(count_ref.shape[0] // rows):
+        total += jnp.dot(
+            count_ref[group * rows : (group + 1) * rows, :],
+            flat[group * LANES : (group + 1) * LANES, :],
+            precision=lax.Precision.HIGHEST,
+            preferred_element_type=F32,
+        )
+    sums_ref[...] = total
 
 
 def node_kernel(
@@ -352,52 +370,65 @@
 
 
 def coarse_back_kernel(
-    coarse_block, place_ref, own_ref, before_ref, coarse_in_ref, w_coarse_ref, base_ref, send_ref, g_ref
+    coarse_block, place_ref, own_ref, before_ref, coarse_in_ref, w_coarse_ref, d_in_ref, g_ref
 ):
-    half = coarse_block // 2
-    core = place_ref[1]
     coarse_in = split(coarse_in_ref[:coarse_block, :])
     weight = w_coarse_ref[...]
     pre = fold(mm(coarse_in, weight_pair(weight)))
     d_coarse = own_ref[:coarse_block, :] + before_ref[...]
     d_pre = split(d_coarse * silu_slope(pre, sigmoid(pre)))
     d_in = fold(mm_t(d_pre, weight_pair_t(weight)))
-    base_ref[...] = d_coarse + d_in
-    send_ref[...] = jnp.where(core == 0, d_in[:half], d_in[half:])
+    d_in_ref[...] = d_in
     g_ref[...] = outer(coarse_in, d_pre)
 
 
+def assemble_kernel(place_ref, d_in_ref, edge_ref, edge_other_ref, coarse_ref, node_ref, out_ref):
+    core = place_ref[1]
+    d_in = d_in_ref[pl.ds(pl.multiple_of(core * 8, 8), 8), :]
+    turned = jnp.concatenate([d_in[4:], d_in[:4]], axis=0)[None]
+    out_ref[:, :8, :] = jnp.broadcast_to(d_in[None], (out_ref.shape[0], 8, LANES))
+    low = lax.broadcasted_iota(jnp.int32, (1, 8, LANES), 1) < 4
+
+    def put(spot, grads):
+        per = grads.shape[0] // 8
+        pairs = grads.reshape(per, 8, LANES)
+        at = pl.ds(spot * per, per)
+        out_ref[at, 8:16, :] = jnp.where(low, pairs, turned)
+        out_ref[at, 16:, :] = jnp.where(low, turned, pairs)
+
+    @pl.when(core == 0)
+    def _():
+        for spot in range(3):
+            put(spot, edge_ref[spot] + edge_other_ref[spot])
+        put(3, coarse_ref[...])
+
+    @pl.when(core != 0)
+    def _():
+        for spot in range(4):
+            put(spot, node_ref[spot])
+
+
+def reduce_kernel(scale, packed_ref, count_ref, near_ref, far_ref, out_ref):
+    middle, last = packed_ref[:, 8:16, :], packed_ref[:, 16:, :]
+    low = lax.broadcasted_iota(jnp.int32, middle.shape, 1) < 4
+    total = jnp.sum(jnp.where(low, middle, last), axis=0) * scale
+    total = total + jnp.concatenate([total[4:], total[:4]], axis=0)
+    out_ref[...] = jnp.broadcast_to(total[None], out_ref.shape)
+
+
 def edge_back_kernel(
-    place_ref,
-    cells_ref,
-    near_ref,
-    near_other_ref,
-    far_ref,
-    far_other_ref,
-    w_send_ref,
-    w_recv_ref,
     w_msg_ref,
-    send_ref,
     recv_ref,
     pre_ref,
     hidden_ref,
     d_agg_ref,
-    near_back,
-    near_other_back,
-    far_back,
-    far_other_back,
-    d_cells_ref,
-    grads_ref,
+    d_pre,
+    g_ref,
     d_agg,
     hot,
-    d_pre,
-    d_table,
     g_msg,
 ):
-    core = place_ref[1]
-    count = cells_ref.shape[0]
-    slots = near_ref.shape[0]
-    nodes = 2 * count + 4 * slots
+    count = d_agg_ref.shape[0]
     edges = pre_ref.shape[0]
     chunks = TILE // LANES
     d_agg[...] = split(d_agg_ref[...])
@@ -418,7 +449,32 @@
         return carry
 
     lax.fori_loop(0, edges // TILE, tile, 0)
-    part = 256
+    full_sum = g_msg[...]
+    g_ref[...] = fold(full_sum[:LANES] + full_sum[LANES:])
+
+
+def edge_table_kernel(
+    place_ref,
+    cells_ref,
+    near_ref,
+    near_other_ref,
+    far_ref,
+    far_other_ref,
+    send_ref,
+    recv_ref,
+    d_pre,
+    g_msg,
+    d_in_ref,
+    d_after_ref,
+    d_table,
+    grads_ref,
+):
+    core = place_ref[1]
+    count = cells_ref.shape[0]
+    slots = near_ref.shape[0]
+    nodes = 2 * count + 4 * slots
+    edges = d_pre.shape[0]
+    part = 1024
 
     def scatter_tile(step, carry):
         first = step * part
@@ -434,32 +490,37 @@
         return carry
 
     lax.fori_loop(0, nodes // part, scatter_tile, 0)
-    send_back = weight_pair_t(w_send_ref[...])
     cells_pair = split(cells_ref[...])
     g_send = tm_m(cells_pair, d_table[:count, :])
-    for spot, (part_ref, back) in enumerate(
-        (
-            (near_ref, near_back),
-            (near_other_ref, near_other_back),
-            (far_ref, far_back),
-            (far_other_ref, far_other_back),
-        )
-    ):
+    for spot, part_ref in enumerate((near_ref, near_other_ref, far_ref, far_other_ref)):
         start = count + spot * slots
-        piece = d_table[start : start + slots, :]
-        back[...] = fold(mm_t(piece, send_back))
-        g_send += tm_m(split(part_ref[...]), piece)
-    from_recv = d_table[nodes - count :, :]
+        g_send += tm_m(split(part_ref[...]), d_table[start : start + slots, :])
+
+    grads_ref[0] = fold(g_send[:LANES] + g_send[LANES:])
+    grads_ref[1] = outer(cells_pair, d_table[nodes - count :, :])
+    grads_ref[2] = g_msg[...]
+
+
+def edge_out_kernel(
+    d_table,
+    w_send_ref,
+    w_recv_ref,
+    near_back,
+    near_other_back,
+    far_back,
+    far_other_back,
+    d_cells_ref,
+):
+    count = d_cells_ref.shape[0]
+    slots = near_back.shape[0]
+    send_back = weight_pair_t(w_send_ref[...])
+    for spot, back in enumerate((near_back, near_other_back, far_back, far_other_back)):
+        start = count + spot * slots
+        back[...] = fold(mm_t(d_table[start : start + slots, :], send_back))
     d_cells_ref[...] = fold(
-        mm_t(d_table[:count, :], send_back) + mm_t(from_recv, weight_pair_t(w_recv_ref[...]))
-    )
-
-    def combine(full):
-        return fold(full[:LANES] + full[LANES:])
-
-    grads_ref[0] = combine(g_send)
-    grads_ref[1] = outer(cells_pair, from_recv)
-    grads_ref[2] = combine(g_msg[...])
+        mm_t(d_table[:count, :], send_back)
+        + mm_t(d_table[count + 4 * slots :, :], weight_pair_t(w_recv_ref[...]))
+    )
 
 
 def finish_kernel(
@@ -472,8 +533,9 @@
     near_other_ref,
     far_ref,
     far_other_ref,
-    base_ref,
-    base_after_ref,
+    d_coarse_ref,
+    d_before_ref,
+    d_after_ref,
     sums_ref,
     sums_other_ref,
     send_ref,
@@ -484,14 +546,14 @@
     rows = 2 * coarse_block
     core = place_ref[1]
     count = direct_ref.shape[0]
-    pooled = jnp.concatenate([base_ref[...], base_after_ref[...]], axis=0)
+    pooled = jnp.concatenate([d_before_ref[...], d_after_ref[...]], axis=0) + d_coarse_ref[...]
     pooled = (pooled + sums_ref[...] + sums_other_ref[...]) * scale
     pooled = split(jnp.concatenate([pooled, jnp.zeros((LANES - rows, LANES), F32)], axis=0))
     returned = split(
         jnp.concatenate([near_ref[...], near_other_ref[...], far_ref[...], far_other_ref[...]], axis=0)
     )
-    per = send_ref.shape[0] // 4
-    part = 256
+    per = send_ref.shape[2] // LANES
+    part = 512
 
     def tile(step, carry):
         first = step * part
@@ -499,7 +561,7 @@
         across = []
         for group, place in ((0, core), (0, 1 - core), (1, core), (1, 1 - core)):
             for chunk in range(per):
-                row = send_ref[pl.ds(group * 2 * per + place * per + chunk, 1), :]
+                row = map_row(send_ref, group, place, chunk)
                 across.append(one_hot_columns(row, first, part))
         down = []
         for chunk in range(part // LANES):
@@ -515,17 +577,20 @@
     lax.fori_loop(0, count // part, tile, 0)
 
 
-def call(kernel, outs, scratch, flops, name, *operands):
+def call(kernel, outs, scratch, micros, name, *operands, after=(), limit=16):
     whole = pl.BlockSpec(memory_space=pltpu.VMEM)
     specs = [pl.BlockSpec(memory_space=pltpu.SMEM) if o.ndim == 1 else whole for o in operands]
-    size = sum(o.size * 4 for o in operands) + sum(o.size * 4 for o in outs)
+    specs += [pl.BlockSpec(memory_space=pl.ANY)] * len(after)
+    operands = operands + tuple(after)
+    flops = micros * 1.1e9
+    size = micros * 1e6
     return pl.pallas_call(
         kernel,
         out_shape=outs,
         in_specs=specs,
         out_specs=[whole] * len(outs),
         scratch_shapes=scratch,
-        compiler_params=pltpu.CompilerParams(vmem_limit_bytes=VMEM_LIMIT),
+        compiler_params=pltpu.CompilerParams(vmem_limit_bytes=limit * 1024 * 1024),
         cost_estimate=pl.CostEstimate(flops=int(flops), bytes_accessed=int(size), transcendentals=0),
         name=name,
     )(*operands)
@@ -571,7 +636,7 @@
         return array.reshape(-1, LANES)
 
     send_rows, recv_rows = lanes(senders), lanes(receivers)
-    map_rows, pool_rows = lanes(send_map), lanes(pool_map)
+    pool_rows = lanes(pool_map)
     coarse_send, coarse_recv = lanes(coarse_senders), lanes(coarse_receivers)
 
     def other_core(array):
@@ -588,41 +653,31 @@
     def around(array, by):
         return lax.ppermute(array, "space", [(i, (i + by) % blocks) for i in range(blocks)])
 
-    def everywhere(array):
-        copies = jnp.broadcast_to(array[None], (blocks,) + array.shape)
-        return lax.all_to_all(copies.reshape(-1, latent), "space", 0, 0, tiled=True)
-
+    def exchange(array):
+        pieces = array.reshape(-1, 4, latent)
+        return lax.all_to_all(pieces, "space", 0, 0, tiled=True).reshape(array.shape)
+
+    edge_both = other_core(jnp.concatenate([coarse_send, coarse_recv], axis=0))
+    chunks = coarse_send.shape[0]
+    groups = (blocks * half // LANES) * rows
+    coarse_edges = (coarse_send, edge_both[:chunks], coarse_recv, edge_both[chunks:])
     near, far, pool_part = call(
         functools.partial(pack_kernel, sizes + (pool_scale,)),
         [full(slots, latent), full(slots, latent), full(rows, latent)],
         [],
-        2 * 2 * 2 * slots * count * 256,
+        1,
         "pack",
         place,
         cells,
-        map_rows,
+        send_map,
         pool_rows,
     )
     pooled_own = pool_part[:coarse_block] + around(pool_part[coarse_block:], 1)
     pooled_half = lax.dynamic_slice_in_dim(pooled_own, place[1] * half, half, 0)
-    pooled = everywhere(pooled_half)
+    copies = jnp.broadcast_to(pooled_half[None], (blocks, half, latent))
+    pooled = lax.all_to_all(copies, "space", 0, 0, tiled=True).reshape(-1, latent)
     near, far = along(near, 1), along(far, 2)
     near_other, far_other = other_core(near), other_core(far)
-    edge_both = other_core(jnp.concatenate([coarse_send, coarse_recv], axis=0))
-    chunks = coarse_send.shape[0]
-    groups = (blocks * half // LANES) * rows
-    count_into, count_from = call(
-        functools.partial(count_kernel, sizes),
-        [full(groups, LANES), full(groups, LANES)],
-        [],
-        4 * 2 * groups * LANES * 12 * chunks * LANES,
-        "count",
-        place,
-        coarse_send,
-        edge_both[:chunks],
-        coarse_recv,
-        edge_both[chunks:],
-    )
     pre, hidden, agg = call(
         edge_kernel,
         [full(edges, latent), full(edges, latent), full(count, latent)],
@@ -631,7 +686,7 @@
             pltpu.VMEM((TILE, nodes), BF16),
             pltpu.VMEM((edges, 2 * latent), BF16),
         ],
-        2 * 2 * edges * (nodes + count) * 256,
+        11,
         "edges",
         place,
         cells,
@@ -644,13 +699,24 @@
         w_msg,
         send_rows,
         recv_rows,
+        limit=20,
     )
     agg_other = other_core(agg)
+    (count_into,) = call(
+        functools.partial(count_kernel, sizes, True),
+        [full(groups, LANES)],
+        [],
+        4,
+        "count_into",
+        place,
+        *coarse_edges,
+        after=(agg,),
+    )
     (sums,) = call(
         functools.partial(coarse_sum_kernel, (coarse_block, blocks)),
         [full(2 * rows, latent)],
         [],
-        6 * 2 * rows * blocks * half * latent,
+        1,
         "coarse_sum",
         place,
         count_into,
@@ -668,7 +734,7 @@
             full(4, latent, latent),
         ],
         [square, square, square, pltpu.VMEM((rows, 2 * latent), F32)],
-        2 * 2 * 11 * count * 256 * 256,
+        6,
         "nodes",
         place,
         cells,
@@ -685,11 +751,28 @@
         w_out,
     )
     d_before = around(d_coarse[coarse_block:], 1)
-    base, d_in_half, coarse_grad = call(
+    d_after = around(d_coarse[:coarse_block], -1)
+    d_pre, msg_grad = call(
+        edge_back_kernel,
+        [jax.ShapeDtypeStruct((edges, 2 * latent), BF16), full(latent, latent)],
+        [
+            pltpu.VMEM((count, 2 * latent), BF16),
+            pltpu.VMEM((TILE, count), BF16),
+            square,
+        ],
+        5,
+        "edges_back",
+        w_msg,
+        recv_rows,
+        pre,
+        hidden,
+        d_agg,
+    )
+    d_in, coarse_grad = call(
         functools.partial(coarse_back_kernel, coarse_block),
-        [full(coarse_block, latent), full(half, latent), full(latent, latent)],
+        [full(coarse_block, latent), full(latent, latent)],
         [],
-        1e6,
+        1,
         "coarse_back",
         place,
         d_coarse,
@@ -697,63 +780,89 @@
         coarse_in,
         w_coarse,
     )
-    base_after = around(base, -1)
-    d_in = everywhere(d_in_half)
-    near_back, near_other_back, far_back, far_other_back, d_cells_own, edge_grads = call(
-        edge_back_kernel,
-        [full(slots, latent)] * 4 + [full(count, latent), full(3, latent, latent)],
-        [
-            pltpu.VMEM((count, 2 * latent), BF16),
-            pltpu.VMEM((TILE, count), BF16),
-            pltpu.VMEM((edges, 2 * latent), BF16),
-            pltpu.VMEM((nodes, 2 * latent), BF16),
-            square,
-        ],
-        2 * 2 * edges * (nodes + count) * 256,
-        "edges_back",
+    d_table, edge_grads = call(
+        edge_table_kernel,
+        [jax.ShapeDtypeStruct((nodes, 2 * latent), BF16), full(3, latent, latent)],
+        [],
+        8,
+        "edges_table",
         place,
         cells,
         near,
         near_other,
         far,
         far_other,
+        send_rows,
+        recv_rows,
+        d_pre,
+        msg_grad,
+        after=(d_in, d_after),
+    )
+    near_back, near_other_back, far_back, far_other_back, d_cells_own = call(
+        edge_out_kernel,
+        [full(slots, latent)] * 4 + [full(count, latent)],
+        [],
+        2,
+        "edges_out",
+        d_table,
         w_send,
         w_recv,
-        w_msg,
-        send_rows,
-        recv_rows,
-        pre,
-        hidden,
-        d_agg,
-    )
-    edge_grads = edge_grads + other_core(edge_grads)
-    first = place[1] == 0
-    mine = jnp.where(
-        first, jnp.concatenate([edge_grads, coarse_grad[None]], axis=0), node_grads
-    ).reshape(-1, latent)
-    pieces = lax.all_to_all(mine, "space", 0, 0, tiled=True)
-    reduced = jnp.sum(pieces.reshape(blocks, -1, latent), axis=0) * grad_scale
-    own_grads = everywhere(reduced).reshape(-1, latent, latent)
-    weight_grads = lax.all_gather(own_grads, "coarse", axis=0, tiled=True)
-
+    )
+    (packed,) = call(
+        assemble_kernel,
+        [full(blocks // 2, 24, latent)],
+        [],
+        1,
+        "assemble",
+        place,
+        d_in,
+        edge_grads,
+        other_core(edge_grads),
+        coarse_grad,
+        node_grads,
+    )
     near_back = near_back + other_core(near_other_back)
     far_back = far_back + other_core(far_other_back)
     near_back, far_back = along(near_back, -1), along(far_back, -2)
     d_cells_other = other_core(d_cells_own)
+    (count_from,) = call(
+        functools.partial(count_kernel, sizes, False),
+        [full(groups, LANES)],
+        [],
+        3,
+        "count_from",
+        place,
+        *coarse_edges,
+        after=(packed,),
+    )
+    packed = exchange(packed)
+    (copies,) = call(
+        functools.partial(reduce_kernel, grad_scale),
+        [full(blocks // 2, 8, latent)],
+        [],
+        1,
+        "reduce",
+        packed,
+        after=(count_from, near_back, far_back),
+    )
+    own_grads = exchange(copies).reshape(-1, latent, latent)
+    weight_grads = lax.all_gather(own_grads, "coarse", axis=0, tiled=True)
+
     (back_sums,) = call(
-        functools.partial(coarse_back_sum_kernel, rows),
+        functools.partial(coarse_back_sum_kernel, (coarse_block, blocks)),
         [full(rows, latent)],
-        [],
-        6 * 2 * rows * blocks * half * latent,
+        [pltpu.VMEM((blocks // 2, 16, latent), F32)],
+        1,
         "coarse_back_sum",
+        place,
         count_from,
-        d_in,
+        packed,
     )
     (d_cells,) = call(
         functools.partial(finish_kernel, sizes + (pool_scale,)),
         [full(count, latent)],
         [],
-        2 * 2 * count * 4 * slots * 256,
+        3,
         "finish",
         place,
         d_direct,
@@ -763,11 +872,12 @@
         other_core(near_back),
         far_back,
         other_core(far_back),
-        base,
-        base_after,
+        d_coarse,
+        d_before,
+        d_after,
         back_sums,
         other_core(back_sums),
-        map_rows,
+        send_map,
         pool_rows,
     )
     return d_cells, weight_grads

time: 178 us -> 146 us (0.82)
  the two profiles are of different devices: /device:TPU:25 before, /device:TPU:1 now
where the time goes in v2:
time: 146 us; the launch traced here: 145 us
  starting transfers between devices  60.2 us (41%)
  Pallas kernels  47.1 us (32%)
  waiting for transfers between devices  24.9 us (17%)
  local copies, waits for them, and re-layouts  7.85 us (5%)
  blocking collectives  4.26 us (3%)
    pallas_call x14, Pallas kernels, call(): pl.pallas_call(kernel, out_shape=outs, in_specs=specs, out_specs=[whole]...  47.1 us
    all_to_all x2, starting transfers between devices, exchange(): lax.all_to_all(pieces, 'space', 0, 0, tiled=True).reshape(array.shape)  17.1 us
    ppermute x12, starting transfers between devices, other_core(): return lax.ppermute(array, 'coarse', [(0, 1), (1, 0)])  16 us
    all_to_all x2, waiting for transfers between devices, exchange(): lax.all_to_all(pieces, 'space', 0, 0, tiled=True).reshape(array.shape)  12.9 us
    all_to_all x1, starting transfers between devices, shards(): lax.all_to_all(copies, 'space', 0, 0, tiled=True).reshape(-1, latent)  10.2 us
    ppermute x4, starting transfers between devices, along(): return lax.ppermute(array, ('space', 'coarse'), pairs)  9.33 us
    ppermute x3, starting transfers between devices, around(): lax.ppermute(array, 'space', [(i, (i + by) % blocks) for i in range(block...  7.55 us
    unnamed x51, local copies, waits for them, and re-layouts  7 us
  transfers between devices with their start and end apart: 22, of which 12 were waited for; matrix products, arithmetic and copies ran while one was open for 1% of the time, Pallas kernels for 22%

profile of v2, /device:TPU:1, one launch (start us, length us, event | category | flops | bytes accessed | tf_op | source)
XLA Modules:
  0.0 145.5 jit_solution(7702946878696145194)
XLA Ops:
  4.3 2.5 %collective-permute-start.6 = (f32[16,128]{1,0:T(8,128)S(1)}, f32[16,128]{1,0:T(8,128)S(1)}, u32[]{:S(2)}, u32[]{:S(2)}) collective-permute-start(f32[16,128]{1,0:T(8,128)S(1)} %get-tuple-element.51), channel_id=1, source_target_pairs={{0,2},{2,4},{4,6},{6,8},{8,10},{10,12},{12,14},{14,16},{16,18},{18... | collective-permute-start | bytes 24584 | tf_op jit(solution)/shard_map/ppermute | solution.py:654
  9.5 8.7 %collective-permute-start.5 = (s32[96,128]{1,0:T(8,128)S(1)}, s32[96,128]{1,0:T(8,128)S(1)}, u32[]{:S(2)}, u32[]{:S(2)}) collective-permute-start(s32[96,128]{1,0:T(8,128)S(1)} %pad_add_fusion), channel_id=1, source_target_pairs={{0,1},{1,0},{2,3},{3,2},{4,5},{5,4},{6,7},{7,6},{8,9},{9,8},{10,11... | collective-permute-start | bytes 147464 | tf_op jit(solution)/shard_map/ppermute | solution.py:643
  19.0 10.2 %all-to-all-start = ((f32[128,8,128]{2,1,0:T(8,128)}), f32[128,8,128]{2,1,0:T(8,128)S(1)}, u32[]{:S(2)}, u32[]{:S(2)}) async-start(f32[128,8,128]{2,1,0:T(8,128)} %broadcast_in_dim.2), calls=%async_computation | async-start | bytes 1048576 | tf_op jit(solution)/shard_map/all_to_all | solution.py:678
  31.0 10.0 %edges.1 = (f32[3072,128]{1,0:T(8,128)S(1)}, f32[3072,128]{1,0:T(8,128)S(1)}, f32[1024,128]{1,0:T(8,128)S(1)}) custom-call(s32[2]{0:T(128)S(1)} %pad_add_fusion.1.place_ref, f32[1024,128]{1,0:T(8,128)S(1)} %copy-done.4, f32[256,128]{1,0:T(8,128)S(1)} %collective-permute-done.near_ref, f32[256,128]{1,0:T(8,128)S(1)} %collective-permute-done.1.near_other_ref, ...), custom_call_target="tpu_custom_call" | custom-call | flops 12099999744 | bytes 11000000 | tf_op jit(solution)/shard_map/edges/pallas_call | solution.py:587
  43.5 4.7 %count_into.1.count_ref = f32[256,128]{1,0:T(8,128)S(1)} custom-call(s32[2]{0:T(128)S(1)} %pad_add_fusion.1.place_ref, s32[48,128]{1,0:T(8,128)S(1)} %bitcast.16, s32[48,128]{1,0:T(8,128)S(1)} %get-tuple-element.47.send_other_ref, s32[48,128]{1,0:T(8,128)S(1)} %bitcast.19, s32[48,128]{1,0:T(8,128)S(1)} %get-tuple-element.46.recv_other_ref, ...), custom_call_target="tpu_custom_call" | custom-call | flops 4400000000 | bytes 4000000 | tf_op jit(solution)/shard_map/count_into/pallas_call | solution.py:587
  50.1 1.9 %collective-permute-start.7 = (f32[64,128]{1,0:T(8,128)S(1)}, f32[64,128]{1,0:T(8,128)S(1)}, u32[]{:S(2)}, u32[]{:S(2)}) collective-permute-start(f32[64,128]{1,0:T(8,128)S(1)} %coarse_sum.1.sums_ref), channel_id=1, source_target_pairs={{0,1},{1,0},{2,3},{3,2},{4,5},{5,4},{6,7},{7,6},{8,9},{9,8},{10,11... | collective-permute-start | bytes 98312 | tf_op jit(solution)/shard_map/ppermute | solution.py:643
  53.0 6.3 %nodes.1 = (f32[1024,128]{1,0:T(8,128)S(1)}, f32[1024,128]{1,0:T(8,128)S(1)}, f32[32,128]{1,0:T(8,128)S(1)}, f32[32,128]{1,0:T(8,128)S(1)}, f32[4,128,128]{2,1,0:T(8,128)S(1)}) custom-call(s32[2]{0:T(128)S(1)} %pad_add_fusion.1.place_ref, f32[1024,128]{1,0:T(8,128)S(1)} %copy-done.4, f32[1024,128]{1,0:T(8,128)S(1)} %get-tuple-element.26.rest_0_.agg_ref, ...), custom_call_target="tpu_custom_call" | custom-call | flops 6600000000 | bytes 6000000 | tf_op jit(solution)/shard_map/nodes/pallas_call | solution.py:587
  59.3 5.0 %collective-permute-start.9 = (f32[16,128]{1,0:T(8,128)S(1)}, f32[16,128]{1,0:T(8,128)S(1)}, u32[]{:S(2)}, u32[]{:S(2)}) collective-permute-start(f32[16,128]{1,0:T(8,128)S(1)} %get-tuple-element.48), channel_id=1, source_target_pairs={{0,254},{2,0},{4,2},{6,4},{8,6},{10,8},{12,10},{14,12},{16,14},{18... | collective-permute-start | bytes 24584 | tf_op jit(solution)/shard_map/ppermute | solution.py:654
  64.3 5.4 %edges_back.1 = (bf16[3072,256]{1,0:T(8,128)(2,1)S(1)}, f32[128,128]{1,0:T(8,128)S(1)}) custom-call(f32[128,128]{1,0:T(8,128)S(1)} %copy-done.9, s32[24,128]{1,0:T(8,128)S(1)} %bitcast.24, f32[3072,128]{1,0:T(8,128)S(1)} %copy-done.22, f32[3072,128]{1,0:T(8,128)S(1)} %copy-done.24, f32[1024,128]{1,0:T(8,128)S(1)} %get-tuple-element.31.d_agg_ref), custom_call_target="tpu_custom_call" | custom-call | flops 5500000256 | bytes 5000000 | tf_op jit(solution)/shard_map/edges_back/pallas_call | solution.py:587
  69.7 2.5 %collective-permute-done.8.before_ref.d_before_ref = f32[16,128]{1,0:T(8,128)S(1)} collective-permute-done((f32[16,128]{1,0:T(8,128)S(1)}, f32[16,128]{1,0:T(8,128)S(1)}, u32[]{:S(2)}, u32[]{:S(2)}) %collective-permute-start.8) | collective-permute-done | bytes 8224 | tf_op jit(solution)/shard_map/ppermute | solution.py:654
  73.1 6.5 %edges_table.1 = (bf16[3072,256]{1,0:T(8,128)(2,1)S(1)}, f32[3,128,128]{2,1,0:T(8,128)S(1)}) custom-call(s32[2]{0:T(128)S(1)} %pad_add_fusion.1.place_ref, f32[1024,128]{1,0:T(8,128)S(1)} %copy-done.4, f32[256,128]{1,0:T(8,128)S(1)} %collective-permute-done.near_ref, f32[256,128]{1,0:T(8,128)S(1)} %collective-permute-done.1.near_other_ref, ...), custom_call_target="tpu_custom_call" | custom-call | flops 8800000000 | bytes 8000000 | tf_op jit(solution)/shard_map/edges_table/pallas_call | solution.py:587
  79.7 1.8 %collective-permute-start.17 = (f32[3,128,128]{2,1,0:T(8,128)S(1)}, f32[3,128,128]{2,1,0:T(8,128)S(1)}, u32[]{:S(2)}, u32[]{:S(2)}) collective-permute-start(f32[3,128,128]{2,1,0:T(8,128)S(1)} %get-tuple-element.43.edge_ref), channel_id=1, source_target_pairs={{0,1},{1,0},{2,3},{3,2},{4,5},{5,4},{6,7},{7,6},{8,9},{9,8},{10,11... | collective-permute-start | bytes 589832 | tf_op jit(solution)/shard_map/ppermute | solution.py:643
  82.6 1.5 %assemble.1.rest_0_ = f32[64,24,128]{2,1,0:T(8,128)} custom-call(s32[2]{0:T(128)S(1)} %pad_add_fusion.1.place_ref, f32[16,128]{1,0:T(8,128)S(1)} %get-tuple-element.36.d_in_ref, f32[3,128,128]{2,1,0:T(8,128)S(1)} %get-tuple-element.43.edge_ref, f32[3,128,128]{2,1,0:T(8,128)S(1)} %collective-permute-done.17.edge_other_ref, ...), custom_call_target="tpu_custom_call" | custom-call | flops 1100000000 | bytes 1000000 | tf_op jit(solution)/shard_map/assemble/pallas_call | solution.py:587
  84.1 7.1 %all-to-all-start.1 = ((f32[384,4,128]{2,1,0:T(4,128)}), f32[384,4,128]{2,1,0:T(4,128)S(1)}, u32[]{:S(2)}, u32[]{:S(2)}) async-start(f32[384,4,128]{2,1,0:T(4,128)} %bitcast.8), calls=%async_computation.1 | async-start | bytes 1572864 | tf_op jit(solution)/shard_map/all_to_all | solution.py:658
  94.9 2.8 %collective-permute-start.12 = (f32[256,128]{1,0:T(8,128)S(1)}, f32[256,128]{1,0:T(8,128)S(1)}, u32[]{:S(2)}, u32[]{:S(2)}) collective-permute-start(f32[256,128]{1,0:T(8,128)S(1)} %add.14), channel_id=1, source_target_pairs={{1,3},{2,0},{3,5},{4,2},{5,7},{6,4},{7,9},{8,6},{9,11},{10,8},{11,... | collective-permute-start | bytes 393224 | tf_op jit(solution)/shard_map/ppermute | solution.py:651
  97.7 4.0 %collective-permute-start.15 = (f32[256,128]{1,0:T(8,128)S(1)}, f32[256,128]{1,0:T(8,128)S(1)}, u32[]{:S(2)}, u32[]{:S(2)}) collective-permute-start(f32[256,128]{1,0:T(8,128)S(1)} %add.15), channel_id=1, source_target_pairs={{1,5},{3,7},{4,0},{5,9},{6,2},{7,11},{8,4},{9,13},{10,6},{11,15},{... | collective-permute-start | bytes 393224 | tf_op jit(solution)/shard_map/ppermute | solution.py:651
  101.7 4.7 %count_from.1.count_ref = f32[256,128]{1,0:T(8,128)S(1)} custom-call(s32[2]{0:T(128)S(1)} %pad_add_fusion.1.place_ref, s32[48,128]{1,0:T(8,128)S(1)} %bitcast.17, s32[48,128]{1,0:T(8,128)S(1)} %get-tuple-element.47.send_other_ref, s32[48,128]{1,0:T(8,128)S(1)} %bitcast.20, s32[48,128]{1,0:T(8,128)S(1)} %get-tuple-element.46.recv_other_ref, ...), custom_call_target="tpu_custom_call" | custom-call | flops 3300000000 | bytes 3000000 | tf_op jit(solution)/shard_map/count_from/pallas_call | solution.py:587
  106.4 2.1 %collective-permute-done.12.near_ref = f32[256,128]{1,0:T(8,128)S(1)} collective-permute-done((f32[256,128]{1,0:T(8,128)S(1)}, f32[256,128]{1,0:T(8,128)S(1)}, u32[]{:S(2)}, u32[]{:S(2)}) %collective-permute-start.12) | collective-permute-done | bytes 131104 | tf_op jit(solution)/shard_map/ppermute | solution.py:651
  108.5 2.2 %collective-permute-done.15.far_ref = f32[256,128]{1,0:T(8,128)S(1)} collective-permute-done((f32[256,128]{1,0:T(8,128)S(1)}, f32[256,128]{1,0:T(8,128)S(1)}, u32[]{:S(2)}, u32[]{:S(2)}) %collective-permute-start.15) | collective-permute-done | bytes 131104 | tf_op jit(solution)/shard_map/ppermute | solution.py:651
  110.7 5.4 %all-to-all-done.1 = f32[384,4,128]{2,1,0:T(4,128)S(1)} async-done(((f32[384,4,128]{2,1,0:T(4,128)}), f32[384,4,128]{2,1,0:T(4,128)S(1)}, u32[]{:S(2)}, u32[]{:S(2)}) %all-to-all-start.1) | async-done | bytes 786464 | tf_op jit(solution)/shard_map/all_to_all | solution.py:658
  116.9 10.0 %all-to-all-start.2 = ((f32[128,4,128]{2,1,0:T(4,128)}), f32[128,4,128]{2,1,0:T(4,128)S(1)}, u32[]{:S(2)}, u32[]{:S(2)}) async-start(f32[128,4,128]{2,1,0:T(4,128)} %bitcast.10), calls=%async_computation.2 | async-start | bytes 524288 | tf_op jit(solution)/shard_map/all_to_all | solution.py:658
  130.3 2.6 %finish.1 = f32[1024,128]{1,0:T(8,128)} custom-call(s32[2]{0:T(128)S(1)} %pad_add_fusion.1.place_ref, f32[1024,128]{1,0:T(8,128)S(1)} %get-tuple-element.28.direct_ref, f32[1024,128]{1,0:T(8,128)S(1)} %get-tuple-element.38.own_ref, f32[1024,128]{1,0:T(8,128)S(1)} %collective-permute-done.10.other_ref, f32[256,128]{1,0:T(8,128)S(1)} %collective-permute-done.12.near_ref, ...), custom_call_target="tpu_custom_call" | custom-call | flops 3300000000 | bytes 3000000 | tf_op jit(solution)/shard_map/finish/pallas_call | solution.py:587
  132.9 7.5 %all-to-all-done.2 = f32[128,4,128]{2,1,0:T(4,128)S(1)} async-done(((f32[128,4,128]{2,1,0:T(4,128)}), f32[128,4,128]{2,1,0:T(4,128)S(1)}, u32[]{:S(2)}, u32[]{:S(2)}) %all-to-all-start.2) | async-done | bytes 262176 | tf_op jit(solution)/shard_map/all_to_all | solution.py:658
  140.4 4.3 %all_gather.3 = f32[8,128,128]{2,1,0:T(8,128)S(1)} all-gather(f32[4,128,128]{2,1,0:T(8,128)S(1)} %bitcast.29), channel_id=1, replica_groups=mesh['space'=128,'coarse'=2] {'coarse'}, dimensions={0}, use_global_device_ids=true | all-gather | bytes 786432 | tf_op jit(solution)/shard_map/all_gather | solution.py:849
  (95 shorter events, 24.9 us)
Async XLA Ops:
  4.2 26.8 %copy-start.4 = (f32[1024,128]{1,0:T(8,128)S(1)}, f32[1024,128]{1,0:T(8,128)}, u32[]{:S(2)}) copy-start(f32[1024,128]{1,0:T(8,128)} %cells_ref.7) | copy-start | bytes 1572868
  4.2 26.8 %copy-start.9 = (f32[128,128]{1,0:T(8,128)S(1)}, f32[128,128]{1,0:T(8,128)}, u32[]{:S(2)}) copy-start(f32[128,128]{1,0:T(8,128)} %w_msg_ref.3) | copy-start | bytes 196612
  4.3 13.8 %collective-permute-start.6 = (f32[16,128]{1,0:T(8,128)S(1)}, f32[16,128]{1,0:T(8,128)S(1)}, u32[]{:S(2)}, u32[]{:S(2)}) collective-permute-start(f32[16,128]{1,0:T(8,128)S(1)} %get-tuple-element.51), channel_id=1, source_target_pairs={{0,2},{2,4},{4,6},{6,8},{8,10},{10,12},{12,14},{14,16},{16,18},{18... | collective-permute-start | bytes 24584 | tf_op jit(solution)/shard_map/ppermute | solution.py:654
  6.8 22.4 %collective-permute-start = (f32[256,128]{1,0:T(8,128)S(1)}, f32[256,128]{1,0:T(8,128)S(1)}, u32[]{:S(2)}, u32[]{:S(2)}) collective-permute-start(f32[256,128]{1,0:T(8,128)S(1)} %get-tuple-element.24), channel_id=1, source_target_pairs={{0,2},{2,4},{3,1},{4,6},{5,3},{6,8},{7,5},{8,10},{9,7},{10,12},{11... | collective-permute-start | bytes 393224 | tf_op jit(solution)/shard_map/ppermute | solution.py:651
  8.1 21.5 %collective-permute-start.2 = (f32[256,128]{1,0:T(8,128)S(1)}, f32[256,128]{1,0:T(8,128)S(1)}, u32[]{:S(2)}, u32[]{:S(2)}) collective-permute-start(f32[256,128]{1,0:T(8,128)S(1)} %get-tuple-element.25), channel_id=1, source_target_pairs={{0,4},{2,6},{4,8},{5,1},{6,10},{7,3},{8,12},{9,5},{10,14},{11,7},{... | collective-permute-start | bytes 393224 | tf_op jit(solution)/shard_map/ppermute | solution.py:651
  9.5 20.4 %collective-permute-start.5 = (s32[96,128]{1,0:T(8,128)S(1)}, s32[96,128]{1,0:T(8,128)S(1)}, u32[]{:S(2)}, u32[]{:S(2)}) collective-permute-start(s32[96,128]{1,0:T(8,128)S(1)} %pad_add_fusion), channel_id=1, source_target_pairs={{0,1},{1,0},{2,3},{3,2},{4,5},{5,4},{6,7},{7,6},{8,9},{9,8},{10,11... | collective-permute-start | bytes 147464 | tf_op jit(solution)/shard_map/ppermute | solution.py:643
  19.0 30.1 %all-to-all-start = ((f32[128,8,128]{2,1,0:T(8,128)}), f32[128,8,128]{2,1,0:T(8,128)S(1)}, u32[]{:S(2)}, u32[]{:S(2)}) async-start(f32[128,8,128]{2,1,0:T(8,128)} %broadcast_in_dim.2), calls=%async_computation | async-start | bytes 1048576 | tf_op jit(solution)/shard_map/all_to_all | solution.py:678
  29.2 1.4 collective-permute-start.1
  29.6 1.3 collective-permute-start.3
  43.3 8.8 %collective-permute-start.4 = (f32[1024,128]{1,0:T(8,128)S(1)}, f32[1024,128]{1,0:T(8,128)S(1)}, u32[]{:S(2)}, u32[]{:S(2)}) collective-permute-start(f32[1024,128]{1,0:T(8,128)S(1)} %get-tuple-element.26.rest_0_.agg_ref), channel_id=1, source_target_pairs={{0,1},{1,0},{2,3},{3,2},{4,5},{5,4},{6,7},{7,6},{8,9},{9,8},{10,11... | collective-permute-start | bytes 1572872 | tf_op jit(solution)/shard_map/ppermute | solution.py:643
  50.1 2.8 %collective-permute-start.7 = (f32[64,128]{1,0:T(8,128)S(1)}, f32[64,128]{1,0:T(8,128)S(1)}, u32[]{:S(2)}, u32[]{:S(2)}) collective-permute-start(f32[64,128]{1,0:T(8,128)S(1)} %coarse_sum.1.sums_ref), channel_id=1, source_target_pairs={{0,1},{1,0},{2,3},{3,2},{4,5},{5,4},{6,7},{7,6},{8,9},{9,8},{10,11... | collective-permute-start | bytes 98312 | tf_op jit(solution)/shard_map/ppermute | solution.py:643
  59.3 13.8 %collective-permute-start.9 = (f32[16,128]{1,0:T(8,128)S(1)}, f32[16,128]{1,0:T(8,128)S(1)}, u32[]{:S(2)}, u32[]{:S(2)}) collective-permute-start(f32[16,128]{1,0:T(8,128)S(1)} %get-tuple-element.48), channel_id=1, source_target_pairs={{0,254},{2,0},{4,2},{6,4},{8,6},{10,8},{12,10},{14,12},{16,14},{18... | collective-permute-start | bytes 24584 | tf_op jit(solution)/shard_map/ppermute | solution.py:654
  64.3 7.9 %collective-permute-start.8 = (f32[16,128]{1,0:T(8,128)S(1)}, f32[16,128]{1,0:T(8,128)S(1)}, u32[]{:S(2)}, u32[]{:S(2)}) collective-permute-start(f32[16,128]{1,0:T(8,128)S(1)} %get-tuple-element.49), channel_id=1, source_target_pairs={{0,2},{2,4},{4,6},{6,8},{8,10},{10,12},{12,14},{14,16},{16,18},{18... | collective-permute-start | bytes 24584 | tf_op jit(solution)/shard_map/ppermute | solution.py:654
  79.7 2.9 %collective-permute-start.17 = (f32[3,128,128]{2,1,0:T(8,128)S(1)}, f32[3,128,128]{2,1,0:T(8,128)S(1)}, u32[]{:S(2)}, u32[]{:S(2)}) collective-permute-start(f32[3,128,128]{2,1,0:T(8,128)S(1)} %get-tuple-element.43.edge_ref), channel_id=1, source_target_pairs={{0,1},{1,0},{2,3},{3,2},{4,5},{5,4},{6,7},{7,6},{8,9},{9,8},{10,11... | collective-permute-start | bytes 589832 | tf_op jit(solution)/shard_map/ppermute | solution.py:643
  84.1 32.0 %all-to-all-start.1 = ((f32[384,4,128]{2,1,0:T(4,128)}), f32[384,4,128]{2,1,0:T(4,128)S(1)}, u32[]{:S(2)}, u32[]{:S(2)}) async-start(f32[384,4,128]{2,1,0:T(4,128)} %bitcast.8), calls=%async_computation.1 | async-start | bytes 1572864 | tf_op jit(solution)/shard_map/all_to_all | solution.py:658
  93.1 1.7 %collective-permute-start.11 = (f32[256,128]{1,0:T(8,128)S(1)}, f32[256,128]{1,0:T(8,128)S(1)}, u32[]{:S(2)}, u32[]{:S(2)}) collective-permute-start(f32[256,128]{1,0:T(8,128)S(1)} %get-tuple-element.40), channel_id=1, source_target_pairs={{0,1},{1,0},{2,3},{3,2},{4,5},{5,4},{6,7},{7,6},{8,9},{9,8},{10,11... | collective-permute-start | bytes 393224 | tf_op jit(solution)/shard_map/ppermute | solution.py:643
  93.9 3.8 %collective-permute-start.14 = (f32[256,128]{1,0:T(8,128)S(1)}, f32[256,128]{1,0:T(8,128)S(1)}, u32[]{:S(2)}, u32[]{:S(2)}) collective-permute-start(f32[256,128]{1,0:T(8,128)S(1)} %get-tuple-element.42), channel_id=1, source_target_pairs={{0,1},{1,0},{2,3},{3,2},{4,5},{5,4},{6,7},{7,6},{8,9},{9,8},{10,11... | collective-permute-start | bytes 393224 | tf_op jit(solution)/shard_map/ppermute | solution.py:643
  94.0 35.5 %collective-permute-start.10 = (f32[1024,128]{1,0:T(8,128)S(1)}, f32[1024,128]{1,0:T(8,128)S(1)}, u32[]{:S(2)}, u32[]{:S(2)}) collective-permute-start(f32[1024,128]{1,0:T(8,128)S(1)} %get-tuple-element.38.own_ref), channel_id=1, source_target_pairs={{0,1},{1,0},{2,3},{3,2},{4,5},{5,4},{6,7},{7,6},{8,9},{9,8},{10,11... | collective-permute-start | bytes 1572872 | tf_op jit(solution)/shard_map/ppermute | solution.py:643
  94.9 13.6 %collective-permute-start.12 = (f32[256,128]{1,0:T(8,128)S(1)}, f32[256,128]{1,0:T(8,128)S(1)}, u32[]{:S(2)}, u32[]{:S(2)}) collective-permute-start(f32[256,128]{1,0:T(8,128)S(1)} %add.14), channel_id=1, source_target_pairs={{1,3},{2,0},{3,5},{4,2},{5,7},{6,4},{7,9},{8,6},{9,11},{10,8},{11,... | collective-permute-start | bytes 393224 | tf_op jit(solution)/shard_map/ppermute | solution.py:651
  97.7 13.0 %collective-permute-start.15 = (f32[256,128]{1,0:T(8,128)S(1)}, f32[256,128]{1,0:T(8,128)S(1)}, u32[]{:S(2)}, u32[]{:S(2)}) collective-permute-start(f32[256,128]{1,0:T(8,128)S(1)} %add.15), channel_id=1, source_target_pairs={{1,5},{3,7},{4,0},{5,9},{6,2},{7,11},{8,4},{9,13},{10,6},{11,15},{... | collective-permute-start | bytes 393224 | tf_op jit(solution)/shard_map/ppermute | solution.py:651
  116.9 23.6 %all-to-all-start.2 = ((f32[128,4,128]{2,1,0:T(4,128)}), f32[128,4,128]{2,1,0:T(4,128)S(1)}, u32[]{:S(2)}, u32[]{:S(2)}) async-start(f32[128,4,128]{2,1,0:T(4,128)} %bitcast.10), calls=%async_computation.2 | async-start | bytes 524288 | tf_op jit(solution)/shard_map/all_to_all | solution.py:658
  126.9 2.6 %collective-permute-start.13 = (f32[256,128]{1,0:T(8,128)S(1)}, f32[256,128]{1,0:T(8,128)S(1)}, u32[]{:S(2)}, u32[]{:S(2)}) collective-permute-start(f32[256,128]{1,0:T(8,128)S(1)} %collective-permute-done.12.near_ref), channel_id=1, source_target_pairs={{0,1},{1,0},{2,3},{3,2},{4,5},{5,4},{6,7},{7,6},{8,9},{9,8},{10,11... | collective-permute-start | bytes 393224 | tf_op jit(solution)/shard_map/ppermute | solution.py:643
  127.9 1.6 %collective-permute-start.16 = (f32[256,128]{1,0:T(8,128)S(1)}, f32[256,128]{1,0:T(8,128)S(1)}, u32[]{:S(2)}, u32[]{:S(2)}) collective-permute-start(f32[256,128]{1,0:T(8,128)S(1)} %collective-permute-done.15.far_ref), channel_id=1, source_target_pairs={{0,1},{1,0},{2,3},{3,2},{4,5},{5,4},{6,7},{7,6},{8,9},{9,8},{10,11... | collective-permute-start | bytes 393224 | tf_op jit(solution)/shard_map/ppermute | solution.py:643
  129.1 1.3 collective-permute-start.18
  (23 other events, 189.4 us)

commit v3 on v2

v3 whole, which is shorter than its diff:
```python
import functools

import jax
import jax.numpy as jnp
from jax import lax
from jax.experimental import pallas as pl
from jax.experimental.pallas import tpu as pltpu
from jax.sharding import PartitionSpec as P

EPSILON = 1e-05
LANES = 128
PLANE = ("y", "x")
LINE = ("z",)
SPACE = PLANE + LINE
TILE = 1024
F32 = jnp.float32
BF16 = jnp.bfloat16


def split(values):
    high = values.astype(BF16)
    low = (values - high.astype(F32)).astype(BF16)
    return jnp.concatenate([high, low], axis=1)


def fold(values):
    return values[:, :LANES] + values[:, LANES:]


def weight_pair(weight):
    pair = split(weight)
    return jnp.concatenate([pair, pair], axis=0)


def weight_pair_t(weight):
    high = weight.astype(BF16)
    low = (weight - high.astype(F32)).astype(BF16)
    stacked = jnp.concatenate([high, low], axis=0)
    return jnp.concatenate([stacked, stacked], axis=1)


def mm(left, right):
    return lax.dot_general(left, right, (((1,), (0,)), ((), ())), preferred_element_type=F32)


def mm_t(left, right):
    return lax.dot_general(left, right, (((1,), (1,)), ((), ())), preferred_element_type=F32)


def tm_m(left, right):
    return lax.dot_general(left, right, (((0,), (0,)), ((), ())), preferred_element_type=F32)


def outer(left_pair, right_pair):
    full = tm_m(left_pair, right_pair)
    return fold(full[:LANES] + full[LANES:])


def as_column(row):
    return jnp.transpose(jnp.broadcast_to(row, (LANES, LANES)))


def one_hot_rows(row, count):
    column = jnp.concatenate([as_column(row).astype(jnp.int16)] * (count // LANES), axis=1)
    place = lax.broadcasted_iota(jnp.int16, (LANES, count), 1)
    return jnp.where(column == place, jnp.ones((), BF16), jnp.zeros((), BF16))


def one_hot_columns(row, first, count):
    wide = jnp.broadcast_to(row - first, (16, LANES)).astype(jnp.int16)
    wide = jnp.concatenate([wide] * (count // 16), axis=0)
    place = lax.broadcasted_iota(jnp.int16, (count, LANES), 0)
    return jnp.where(wide == place, jnp.ones((), BF16), jnp.zeros((), BF16))


def norm_parts(values):
    centered = values - jnp.mean(values, axis=-1, keepdims=True)
    variance = jnp.mean(centered * centered, axis=-1, keepdims=True)
    scale = lax.rsqrt(variance + EPSILON)
    return centered * scale, scale


def norm_back(normed, scale, cotangent):
    shared = cotangent - normed * jnp.mean(cotangent * normed, axis=-1, keepdims=True)
    return scale * (shared - jnp.mean(shared, axis=-1, keepdims=True))


def sigmoid(values):
    return 1.0 / (1.0 + jnp.exp(-values))


def silu_slope(values, gate):
    return gate * (1.0 + values * (1.0 - gate))


def relative_pool(row, place, coarse_block, coarse_total):
    shifted = row - place * coarse_block
    return jnp.where(shifted < 0, shifted + coarse_total, shifted)


def own_half(rows, core):
    half = rows.shape[0] // 4
    first = jnp.concatenate([rows[:half], rows[2 * half : 3 * half]], axis=0)
    second = jnp.concatenate([rows[half : 2 * half], rows[3 * half :]], axis=0)
    return jnp.where(core == 0, first, second)


def join_line(parts):
    half = parts.shape[1] // 2
    low, high = parts[:, :half, :], parts[:, half:, :]
    joined = jnp.concatenate([low[:1], low[1:] + high[:-1]], axis=0)
    return jnp.concatenate([joined.reshape(-1, LANES), high[-1]], axis=0)


def join_plane(parts, half):
    body, extra = parts[:, :-half, :], parts[:, -half:, :]
    extra = jnp.concatenate([extra[-1:], extra[:-1]], axis=0)
    body = jnp.concatenate([body[:, :half, :] + extra, body[:, half:, :]], axis=1)
    return body.reshape(-1, LANES)


def map_row(send_ref, group, core, chunk):
    at = slice(chunk * LANES, (chunk + 1) * LANES)
    first, second = send_ref[0, 2 * group : 2 * group + 1, at], send_ref[0, 2 * group + 1 : 2 * group + 2, at]
    return jnp.where(core == 0, first, second)


def pool_kernel(
    sizes, place_ref, cells_hbm, pool_hbm, out_ref, cells, pool, sems
):
    coarse_block, coarse_total, scale = sizes
    loads = [
        pltpu.make_async_copy(cells_hbm, cells, sems.at[0]),
        pltpu.make_async_copy(pool_hbm, pool, sems.at[1]),
    ]
    for load in loads:
        load.start()
    for load in loads:
        load.wait()
    hot = []
    for chunk in range(cells.shape[0] // LANES):
        row = relative_pool(pool[chunk : chunk + 1, :], place_ref[0], coarse_block, coarse_total)
        hot.append(one_hot_columns(row, 0, 2 * coarse_block))
    part = own_half(fold(mm(jnp.concatenate(hot, axis=1), split(cells[...]))) * scale, place_ref[1])
    out_ref[...] = jnp.broadcast_to(part[None], out_ref.shape)


def spread_kernel(parts_ref, count_ref, out_ref):
    rows = join_line(parts_ref[...])
    out_ref[...] = jnp.broadcast_to(rows[None], out_ref.shape)


def halo_kernel(
    place_ref, cells_ref, send_ref, coarse_send_ref, coarse_recv_ref, pool_ref, near_ref, far_ref, edges_ref
):
    core = place_ref[1]
    count = cells_ref.shape[0]
    pair = split(cells_ref[...])
    edges_ref[: coarse_send_ref.shape[0], :] = coarse_send_ref[...]
    edges_ref[coarse_send_ref.shape[0] :, :] = coarse_recv_ref[...]
    for group, out in ((0, near_ref), (1, far_ref)):
        for chunk in range(out.shape[0] // LANES):
            row = map_row(send_ref, group, core, chunk)
            out[chunk * LANES : (chunk + 1) * LANES, :] = fold(mm(one_hot_rows(row, count), pair))


def join_halo_kernel(near_ref, far_ref, spread_ref, out_ref):
    slots = near_ref.shape[0]
    out_ref[:slots, :] = near_ref[...]
    out_ref[slots:, :] = far_ref[...]


def sender_row(row, core, count, slots):
    return jnp.where(row >= count, row ^ (core * slots), row)


def edge_kernel(
    place_ref,
    cells_ref,
    halo_ref,
    halo_other_ref,
    w_send_ref,
    w_recv_ref,
    w_msg_ref,
    send_ref,
    recv_ref,
    pre_hbm,
    agg_ref,
    table,
    hot,
    normed,
    pre_ref,
    sems,
):
    core = place_ref[1]
    count = cells_ref.shape[0]
    slots = halo_ref.shape[0] // 2
    nodes = 2 * count + 4 * slots
    edges = pre_ref.shape[0]
    w_send = weight_pair(w_send_ref[...])
    cells_pair = split(cells_ref[...])
    table[:count, :] = split(fold(mm(cells_pair, w_send)))
    for spot, part in enumerate((halo_ref, halo_other_ref, halo_ref, halo_other_ref)):
        start, at = count + spot * slots, spot // 2 * slots
        table[start : start + slots, :] = split(fold(mm(split(part[at : at + slots, :]), w_send)))
    table[nodes - count :, :] = split(fold(mm(cells_pair, weight_pair(w_recv_ref[...]))))
    w_msg = weight_pair(w_msg_ref[...])
    chunks = TILE // LANES

    def keep(step):
        at = pl.ds(pl.multiple_of(step * TILE, TILE), TILE)
        return pltpu.make_async_copy(pre_ref.at[at], pre_hbm.at[at], sems.at[step])

    def tile(step, carry):
        start = pl.multiple_of(step * TILE, TILE)
        for chunk in range(chunks):
            place = step * chunks + chunk
            row = sender_row(send_ref[pl.ds(place, 1), :], core, count, slots)
            hot[chunk * LANES : (chunk + 1) * LANES, : nodes - count] = one_hot_rows(row, nodes - count)
            row = recv_ref[pl.ds(place, 1), :]
            hot[chunk * LANES : (chunk + 1) * LANES, nodes - count :] = one_hot_rows(row, count)
        pre = fold(mm(hot[...], table[...]))
        pre_ref[pl.ds(start, TILE), :] = pre
        keep(step).start()
        hidden = fold(mm(split(pre * sigmoid(pre)), w_msg))
        normed[pl.ds(start, TILE), :] = split(norm_parts(hidden)[0])
        return carry

    lax.fori_loop(0, edges // TILE, tile, 0)
    part = 512

    def gather_tile(step, carry):
        first = step * part
        across = [
            one_hot_columns(recv_ref[chunk : chunk + 1, :], first, part)
            for chunk in range(edges // LANES)
        ]
        agg_ref[pl.ds(pl.multiple_of(first, part), part), :] = fold(
            mm(jnp.concatenate(across, axis=1), normed[...])
        )
        return carry

    lax.fori_loop(0, count // part, gather_tile, 0)
    for step in range(edges // TILE):
        keep(step).wait()


def count_kernel(
    sizes, into, place_ref, send_ref, send_other_ref, recv_ref, recv_other_ref, *rest
):
    coarse_block, coarse_total = sizes
    count_ref, keys, lows = rest[-3:]
    core = place_ref[1]
    rows = 2 * coarse_block
    half = coarse_block // 2
    own = coarse_total // 2
    groups = count_ref.shape[0]
    chunks = send_ref.shape[0]
    for at, senders, receivers, owner in (
        (0, send_ref, recv_ref, core),
        (chunks, send_other_ref, recv_other_ref, 1 - core),
    ):
        sender, receiver = senders[...], receivers[...] + owner * own
        near, distant = (receiver, sender) if into else (sender, receiver)
        near = relative_pool(near, place_ref[0], coarse_block, coarse_total)
        inside = distant & (coarse_block - 1)
        column = (distant >> (coarse_block.bit_length() - 1)) * half + (inside & (half - 1))
        wanted = (jnp.where(inside >= half, 1, 0) == core) & (near < rows)
        keys[at : at + chunks, :] = jnp.where(
            wanted, (column >> (LANES.bit_length() - 1)) * rows + near, -1
        )
        lows[at : at + chunks, :] = column & (LANES - 1)

    first = [one_hot_columns(keys[at : at + 1, :], 0, groups) for at in range(2 * chunks)]
    second = [one_hot_columns(lows[at : at + 1, :], 0, LANES) for at in range(2 * chunks)]
    count_ref[...] = mm_t(jnp.concatenate(first, axis=1), jnp.concatenate(second, axis=1))


def weigh_counts(count_ref, values_ref, rows):
    total = jnp.zeros((rows, LANES), F32)
    for group in range(count_ref.shape[0] // rows):
        total += jnp.dot(
            count_ref[group * rows : (group + 1) * rows, :],
            values_ref[group * LANES : (group + 1) * LANES, :],
            precision=lax.Precision.HIGHEST,
            preferred_element_type=F32,
        )
    return total


def coarse_sum_kernel(sizes, place_ref, count_ref, parts_ref, sums_ref, values):
    coarse_block, blocks = sizes
    rows = 2 * coarse_block
    half = coarse_block // 2
    place, core = place_ref[0], place_ref[1]
    after = lax.rem(place + 1, blocks)
    values[...] = join_plane(parts_ref[...], half)
    sums_ref[:rows, :] = weigh_counts(count_ref, values, rows)
    sums_ref[rows:, :] = jnp.zeros((rows, LANES), F32)
    for spot, block in ((0, place), (1, after)):
        own = values[pl.ds(pl.multiple_of(block * half, half), half), :]
        sums_ref[pl.ds(pl.multiple_of(rows + spot * coarse_block + core * half, half), half), :] = own


def coarse_back_sum_kernel(sizes, place_ref, count_ref, packed_ref, out_ref, values):
    coarse_block, blocks, share = sizes
    rows = 2 * coarse_block
    half = coarse_block // 2
    place, core = place_ref[0], place_ref[1]
    after = lax.rem(place + 1, blocks)
    plane = packed_ref.shape[0]
    out_ref[: plane * share, :] = packed_ref[:, :share, :].reshape(-1, LANES)
    values[...] = join_plane(packed_ref[:, share:, :], half)
    at = plane * share
    out_ref[at:, :] = weigh_counts(count_ref, values, rows)
    for spot, block in ((0, place), (1, after)):
        own = values[pl.ds(pl.multiple_of(block * half, half), half), :]
        out_ref[pl.ds(pl.multiple_of(at + spot * coarse_block + core * half, half), half), :] += own


def node_kernel(
    sizes,
    place_ref,
    cells_ref,
    agg_ref,
    agg_other_ref,
    sums_ref,
    sums_other_ref,
    upstream_ref,
    pool_ref,
    w_coarse_ref,
    w_self_ref,
    w_agg_ref,
    w_up_ref,
    w_out_ref,
    d_agg_ref,
    d_direct_ref,
    d_coarse_ref,
    g_coarse_ref,
    grads_ref,
    g_self,
    g_agg,
    g_out,
    lifted_back,
):
    coarse_block, coarse_total = sizes
    rows = 2 * coarse_block
    count = cells_ref.shape[0]
    sums = sums_ref[...] + sums_other_ref[...]
    pooled = sums[rows:]
    coarse_in = pooled + sums[:rows]
    coarse_pre = fold(mm(split(coarse_in), weight_pair(w_coarse_ref[...])))
    coarse_gate = sigmoid(coarse_pre)
    coarse_new = pooled + coarse_pre * coarse_gate
    raised = fold(mm(split(coarse_new), weight_pair(w_up_ref[...])))
    raised = split(jnp.concatenate([raised, jnp.zeros((LANES - rows, LANES), F32)], axis=0))
    w_self, w_agg, w_out = w_self_ref[...], w_agg_ref[...], w_out_ref[...]
    self_pair, agg_pair, out_pair = weight_pair(w_self), weight_pair(w_agg), weight_pair(w_out)
    self_back, agg_back, out_back = weight_pair_t(w_self), weight_pair_t(w_agg), weight_pair_t(w_out)
    part = count
    g_self[...] = jnp.zeros_like(g_self)
    g_agg[...] = jnp.zeros_like(g_agg)
    g_out[...] = jnp.zeros_like(g_out)
    lifted_back[...] = jnp.zeros_like(lifted_back)

    def tile(step, carry):
        at = pl.ds(pl.multiple_of(step * part, part), part)
        cells_pair = split(cells_ref[at, :])
        agg_pair_rows = split(agg_ref[at, :] + agg_other_ref[at, :])
        down, across = [], []
        for chunk in range(part // LANES):
            row = pool_ref[pl.ds(step * (part // LANES) + chunk, 1), :]
            row = relative_pool(row, place_ref[0], coarse_block, coarse_total)
            down.append(one_hot_rows(row, LANES))
            across.append(one_hot_columns(row, 0, rows))
        inner = fold(
            mm(cells_pair, self_pair)
            + mm(agg_pair_rows, agg_pair)
            + mm(jnp.concatenate(down, axis=0), raised)
        )
        gate = sigmoid(inner)
        active = split(inner * gate)
        normed, scale = norm_parts(fold(mm(active, out_pair)))
        upstream = upstream_ref[at, :]
        d_hidden = split(norm_back(normed, scale, upstream))
        g_out[...] += tm_m(active, d_hidden)
        d_inner = fold(mm_t(d_hidden, out_back)) * silu_slope(inner, gate)
        d_pair = split(d_inner)
        d_agg_ref[at, :] = fold(mm_t(d_pair, agg_back))
        d_direct_ref[at, :] = upstream + fold(mm_t(d_pair, self_back))
        g_self[...] += tm_m(cells_pair, d_pair)
        g_agg[...] += tm_m(agg_pair_rows, d_pair)
        lifted_back[...] += mm(jnp.concatenate(across, axis=1), d_pair)
        return carry

    lax.fori_loop(0, count // part, tile, 0)

    def combine(full):
        return fold(full[:LANES] + full[LANES:])

    inner_sums = split(fold(lifted_back[...]))
    d_coarse = fold(mm_t(inner_sums, weight_pair_t(w_up_ref[...])))
    d_coarse_ref[:rows, :] = d_coarse
    d_coarse_pre = split(d_coarse * silu_slope(coarse_pre, coarse_gate))
    d_coarse_ref[rows:, :] = fold(mm_t(d_coarse_pre, weight_pair_t(w_coarse_ref[...])))
    g_coarse_ref[...] = outer(split(coarse_in), d_coarse_pre)
    grads_ref[0] = combine(g_self[...])
    grads_ref[1] = combine(g_agg[...])
    grads_ref[2] = outer(split(coarse_new), inner_sums)
    grads_ref[3] = combine(g_out[...])


def line_kernel(
    scale, place_ref, parts_ref, d_coarse_ref, mine_ref, other_ref, count_ref, out_ref, near_ref, far_ref
):
    total = jnp.sum(parts_ref[...], axis=0) * scale
    core = place_ref[1]
    rows = d_coarse_ref.shape[0] // 2
    d_in = own_half(d_coarse_ref[rows:, :], core)
    out_ref[...] = jnp.broadcast_to(jnp.concatenate([total, d_in], axis=0)[None], out_ref.shape)
    slots = far_ref.shape[0]
    near_ref[:slots, :] = mine_ref[:slots, :] + other_ref[:slots, :]
    near_ref[slots:, :] = jnp.where(core == 0, d_coarse_ref[: rows // 2, :], d_coarse_ref[rows // 2 : rows, :])
    far_ref[...] = mine_ref[slots:, :] + other_ref[slots:, :]


def plane_kernel(share, parts_ref, out_ref):
    total = jnp.sum(parts_ref[:, :share, :], axis=0)
    rows = jnp.concatenate([total, join_line(parts_ref[:, share:, :])], axis=0)
    out_ref[...] = jnp.broadcast_to(rows[None], out_ref.shape)


def edge_back_kernel(
    w_msg_ref,
    recv_ref,
    pre_ref,
    d_agg_ref,
    d_pre,
    g_ref,
    d_agg,
    hot,
):
    count = d_agg_ref.shape[0]
    edges = pre_ref.shape[0]
    d_agg[...] = split(d_agg_ref[...])
    for chunk in range(edges // LANES):
        row = recv_ref[chunk : chunk + 1, :]
        hot[chunk * LANES : (chunk + 1) * LANES, :] = one_hot_rows(row, count)
    pre = pre_ref[...]
    gate = sigmoid(pre)
    active = split(pre * gate)
    normed, scale = norm_parts(fold(mm(active, weight_pair(w_msg_ref[...]))))
    d_hidden = split(norm_back(normed, scale, fold(mm(hot[...], d_agg[...]))))
    g_ref[...] = outer(active, d_hidden)
    d_pre[...] = split(fold(mm_t(d_hidden, weight_pair_t(w_msg_ref[...]))) * silu_slope(pre, gate))


def edge_table_kernel(
    place_ref,
    cells_ref,
    halo_ref,
    halo_other_ref,
    w_send_ref,
    w_recv_ref,
    send_ref,
    recv_ref,
    d_pre,
    g_msg,
    direct_ref,
    grads_ref,
    mine_back,
    other_back,
    d_cells_ref,
    d_table,
):
    core = place_ref[1]
    count = cells_ref.shape[0]
    slots = halo_ref.shape[0] // 2
    nodes = 2 * count + 4 * slots
    edges = d_pre.shape[0]
    part = 1024

    def scatter_tile(step, carry):
        first = step * part
        own = first < nodes - count
        across = []
        for chunk in range(edges // LANES):
            sender = sender_row(send_ref[chunk : chunk + 1, :], core, count, slots)
            receiver = recv_ref[chunk : chunk + 1, :] + (nodes - count)
            across.append(one_hot_columns(jnp.where(own, sender, receiver), first, part))
        d_table[pl.ds(pl.multiple_of(first, part), part), :] = split(
            fold(mm(jnp.concatenate(across, axis=1), d_pre[...]))
        )
        return carry

    lax.fori_loop(0, nodes // part, scatter_tile, 0)
    cells_pair = split(cells_ref[...])
    g_send = tm_m(cells_pair, d_table[:count, :])
    for spot, part in enumerate((halo_ref, halo_other_ref, halo_ref, halo_other_ref)):
        start, at = count + spot * slots, spot // 2 * slots
        g_send += tm_m(split(part[at : at + slots, :]), d_table[start : start + slots, :])

    grads_ref[0] = fold(g_send[:LANES] + g_send[LANES:])
    grads_ref[1] = outer(cells_pair, d_table[nodes - count :, :])
    grads_ref[2] = g_msg[...]
    send_back = weight_pair_t(w_send_ref[...])
    for spot, back in enumerate((mine_back, other_back, mine_back, other_back)):
        start = count + spot * slots
        at = spot // 2 * slots
        back[at : at + slots, :] = fold(mm_t(d_table[start : start + slots, :], send_back))
    d_cells = fold(
        mm_t(d_table[:count, :], send_back)
        + mm_t(d_table[nodes - count :, :], weight_pair_t(w_recv_ref[...]))
    )
    d_cells_ref[...] = d_cells + jnp.where(core == 0, direct_ref[...], 0.0)


def gather_back_kernel(sizes, place_ref, own_ref, other_ref, back_ref, back_other_ref, send_ref, out_ref):
    extra, blocks = sizes
    place, core = place_ref[0], place_ref[1]
    count = own_ref.shape[0]
    slots = (back_ref.shape[0] - extra) // 2

    def inside(ref, core):
        edge = jnp.where(core == 0, blocks - 1, 0)
        return jnp.where(place == edge, 0.0, ref[:slots, :])

    returned = split(
        jnp.concatenate(
            [
                inside(back_ref, core),
                inside(back_other_ref, 1 - core),
                back_ref[slots + extra :, :],
                back_other_ref[slots + extra :, :],
            ],
            axis=0,
        )
    )
    part = 512

    def tile(step, carry):
        first = step * part
        at = pl.ds(pl.multiple_of(first, part), part)
        across = []
        for group, place in ((0, core), (0, 1 - core), (1, core), (1, 1 - core)):
            for chunk in range(send_ref.shape[2] // LANES):
                row = map_row(send_ref, group, place, chunk)
                across.append(one_hot_columns(row, first, part))
        added = mm(jnp.concatenate(across, axis=1), returned)
        out_ref[at, :] = own_ref[at, :] + other_ref[at, :] + fold(added)
        return carry

    lax.fori_loop(0, count // part, tile, 0)


def finish_kernel(
    sizes,
    place_ref,
    most_ref,
    d_coarse_ref,
    back_ref,
    back_other_ref,
    mine_ref,
    other_ref,
    pool_ref,
    out_ref,
    grads_ref,
):
    coarse_block, coarse_total, scale = sizes
    rows = 2 * coarse_block
    core = place_ref[1]
    count = most_ref.shape[0]
    weights = mine_ref.shape[0] - rows
    half = grads_ref.shape[0] // 2
    grads_ref[pl.ds(core * half, half)] = mine_ref[:weights, :].reshape(half, LANES, LANES)
    grads_ref[pl.ds((1 - core) * half, half)] = other_ref[:weights, :].reshape(half, LANES, LANES)
    slots = (back_ref.shape[0] - coarse_block) // 2
    at = slice(slots, slots + coarse_block)
    mine, other = back_ref[at, :], back_other_ref[at, :]
    d_before, d_after = jnp.where(core == 0, other, mine), jnp.where(core == 0, mine, other)
    pooled = jnp.concatenate([d_before, d_after], axis=0) + d_coarse_ref[:rows, :]
    pooled = (pooled + mine_ref[weights:, :] + other_ref[weights:, :]) * scale
    pooled = split(jnp.concatenate([pooled, jnp.zeros((LANES - rows, LANES), F32)], axis=0))
    down = []
    for chunk in range(count // LANES):
        row = relative_pool(pool_ref[chunk : chunk + 1, :], place_ref[0], coarse_block, coarse_total)
        down.append(one_hot_rows(row, LANES))
    out_ref[...] = most_ref[...] + fold(mm(jnp.concatenate(down, axis=0), pooled))


MEGABYTES = {
    "pool": 6,
    "halo": 6,
    "count_into": 6,
    "spread": 4,
    "edges": 14,
    "coarse_sum": 4,
    "nodes": 8,
    "edges_back": 14,
    "edges_table": 9,
    "line": 6,
    "plane": 4,
    "gather_back": 8,
    "coarse_back_sum": 6,
    "finish": 6,
    "count_from": 6,
    "join_halo": 4,
}


def call(kernel, outs, scratch, micros, name, *operands, after=(), far=(), far_outs=()):
    whole = pl.BlockSpec(memory_space=pltpu.VMEM)
    outer = pl.BlockSpec(memory_space=pltpu.HBM)
    specs = [pl.BlockSpec(memory_space=pltpu.SMEM) if o.ndim == 1 else whole for o in operands]
    specs = [outer if at in far else spec for at, spec in enumerate(specs)]
    specs += [pl.BlockSpec(memory_space=pl.ANY)] * len(after)
    operands = operands + tuple(after)
    flops = micros * 1.1e9
    size = micros * 1e6
    return pl.pallas_call(
        kernel,
        out_shape=outs,
        in_specs=specs,
        out_specs=[outer if at in far_outs else whole for at in range(len(outs))],
        scratch_shapes=scratch,
        compiler_params=pltpu.CompilerParams(vmem_limit_bytes=MEGABYTES[name] * 1024 * 1024),
        cost_estimate=pl.CostEstimate(flops=int(flops), bytes_accessed=int(size), transcendentals=0),
        name=name,
    )(*operands)


def full(*shape):
    return jax.ShapeDtypeStruct(shape, F32)


def shards(
    cells,
    w_send,
    w_recv,
    w_msg,
    w_coarse,
    w_self,
    w_agg,
    w_up,
    w_out,
    upstream,
    senders,
    receivers,
    send_map,
    pool_map,
    coarse_senders,
    coarse_receivers,
):
    count, latent = cells.shape
    plane, line = lax.axis_size(PLANE), lax.axis_size(LINE)
    blocks = plane * line
    place = jnp.stack([lax.axis_index(SPACE), lax.axis_index("coarse")]).astype(jnp.int32)
    coarse_total = coarse_senders.shape[0] * 2 // 6
    coarse_block = coarse_total // blocks
    rows = 2 * coarse_block
    half = coarse_block // 2
    slots = send_map.shape[2]
    edges = senders.shape[0]
    nodes = 2 * count + 4 * slots
    pool_scale = (coarse_block / count) ** 0.5
    grad_scale = (count * blocks) ** (-0.5)
    sizes = (coarse_block, coarse_total)

    def lanes(array):
        return array.reshape(-1, LANES)

    send_rows, recv_rows = lanes(senders), lanes(receivers)
    pool_rows = lanes(pool_map)
    coarse_send, coarse_recv = lanes(coarse_senders), lanes(coarse_receivers)

    def other_core(array):
        return lax.ppermute(array, "coarse", [(0, 1), (1, 0)])

    def along(array, by, around=False):
        pairs = []
        for block in range(blocks):
            for core, step in ((0, by), (1, -by)):
                if around or 0 <= block + step < blocks:
                    pairs.append((2 * block + core, 2 * ((block + step) % blocks) + core))
        return lax.ppermute(array, SPACE + ("coarse",), pairs)

    def exchange(array, axes):
        return lax.all_to_all(array.reshape(-1, latent), axes, 0, 0, tiled=True)

    chunks = coarse_send.shape[0]
    groups = (blocks * half // LANES) * rows
    edge_keys = pltpu.VMEM((2 * chunks, LANES), jnp.int32)
    (copies,) = call(
        functools.partial(pool_kernel, sizes + (pool_scale,)),
        [full(line, coarse_block, latent)],
        [
            pltpu.VMEM((count, latent), F32),
            pltpu.VMEM((count // LANES, LANES), jnp.int32),
            pltpu.SemaphoreType.DMA((2,)),
        ],
        1,
        "pool",
        place,
        cells,
        pool_rows,
        far=(1, 2),
    )
    parts = exchange(copies, LINE).reshape(line, coarse_block, latent)
    near, far, edge_both = call(
        halo_kernel,
        [
            full(slots, latent),
            full(slots, latent),
            jax.ShapeDtypeStruct((2 * chunks, LANES), jnp.int32),
        ],
        [],
        1,
        "halo",
        place,
        cells,
        send_map,
        coarse_send,
        coarse_recv,
        after=(copies,),
    )
    edge_both = other_core(edge_both)
    coarse_edges = (coarse_send, edge_both[:chunks], coarse_recv, edge_both[chunks:])
    (count_into,) = call(
        functools.partial(count_kernel, sizes, True),
        [full(groups, LANES)],
        [edge_keys, edge_keys],
        3,
        "count_into",
        place,
        *coarse_edges,
    )
    lines = line * half + half
    (copies,) = call(
        spread_kernel,
        [full(plane, lines, latent)],
        [],
        1,
        "spread",
        parts,
        after=(count_into,),
    )
    pooled = exchange(copies, PLANE).reshape(plane, lines, latent)
    (halo,) = call(
        join_halo_kernel,
        [full(2 * slots, latent)],
        [],
        0.5,
        "join_halo",
        along(near, 1),
        along(far, 2),
        after=(copies,),
    )
    halo_other = other_core(halo)
    pre, agg = call(
        edge_kernel,
        [pltpu.HBM((edges, latent), F32), full(count, latent)],
        [
            pltpu.VMEM((nodes, 2 * latent), BF16),
            pltpu.VMEM((TILE, nodes), BF16),
            pltpu.VMEM((edges, 2 * latent), BF16),
            pltpu.VMEM((edges, latent), F32),
            pltpu.SemaphoreType.DMA((edges // TILE,)),
        ],
        3,
        "edges",
        place,
        cells,
        halo,
        halo_other,
        w_send,
        w_recv,
        w_msg,
        send_rows,
        recv_rows,
        far_outs=(0,),
    )
    agg_other = other_core(agg)
    (sums,) = call(
        functools.partial(coarse_sum_kernel, (coarse_block, blocks)),
        [full(2 * rows, latent)],
        [pltpu.VMEM((blocks * half, latent), F32)],
        1,
        "coarse_sum",
        place,
        count_into,
        pooled,
    )
    sums_other = other_core(sums)
    square = pltpu.VMEM((2 * latent, 2 * latent), F32)
    d_agg, d_direct, d_coarse, coarse_grad, node_grads = call(
        functools.partial(node_kernel, sizes),
        [
            full(count, latent),
            full(count, latent),
            full(2 * rows, latent),
            full(latent, latent),
            full(4, latent, latent),
        ],
        [square, square, square, pltpu.VMEM((rows, 2 * latent), F32)],
        6,
        "nodes",
        place,
        cells,
        agg,
        agg_other,
        sums,
        sums_other,
        upstream,
        pool_rows,
        w_coarse,
        w_self,
        w_agg,
        w_up,
        w_out,
    )
    d_pre, msg_grad = call(
        edge_back_kernel,
        [jax.ShapeDtypeStruct((edges, 2 * latent), BF16), full(latent, latent)],
        [
            pltpu.VMEM((count, 2 * latent), BF16),
            pltpu.VMEM((edges, count), BF16),
        ],
        5,
        "edges_back",
        w_msg,
        recv_rows,
        pre,
        d_agg,
    )
    edge_grads, mine_back, other_back, d_cells_own = call(
        edge_table_kernel,
        [
            full(3, latent, latent),
            full(2 * slots, latent),
            full(2 * slots, latent),
            full(count, latent),
        ],
        [pltpu.VMEM((nodes, 2 * latent), BF16)],
        8,
        "edges_table",
        place,
        cells,
        halo,
        halo_other,
        w_send,
        w_recv,
        send_rows,
        recv_rows,
        d_pre,
        msg_grad,
        d_direct,
    )
    edge_grads = edge_grads + other_core(edge_grads)
    mine = jnp.concatenate([edge_grads, coarse_grad[None]], axis=0)
    mine = jnp.where(place[1] == 0, mine, node_grads)
    share = 4 * latent // plane
    parts = exchange(mine, PLANE).reshape(plane, share, latent)
    other_back = other_core(other_back)
    d_cells_other = other_core(d_cells_own)
    (count_from,) = call(
        functools.partial(count_kernel, sizes, False),
        [full(groups, LANES)],
        [edge_keys, edge_keys],
        3,
        "count_from",
        place,
        *coarse_edges,
        after=(mine,),
    )
    copies, near_back, far_back = call(
        functools.partial(line_kernel, grad_scale),
        [
            full(line, share + coarse_block, latent),
            full(slots + coarse_block, latent),
            full(slots, latent),
        ],
        [],
        1,
        "line",
        place,
        parts,
        d_coarse,
        mine_back,
        other_back,
        after=(count_from,),
    )
    back = jnp.concatenate([along(near_back, -1, True), along(far_back, -2)], axis=0)
    back_other = other_core(back)
    parts = exchange(copies, LINE).reshape(line, share + coarse_block, latent)
    (copies,) = call(
        functools.partial(plane_kernel, share),
        [full(plane, share + lines, latent)],
        [],
        1,
        "plane",
        parts,
    )
    packed = exchange(copies, PLANE).reshape(plane, share + lines, latent)
    (most,) = call(
        functools.partial(gather_back_kernel, (coarse_block, blocks)),
        [full(count, latent)],
        [],
        3,
        "gather_back",
        place,
        d_cells_own,
        d_cells_other,
        back,
        back_other,
        send_map,
    )
    (sums,) = call(
        functools.partial(coarse_back_sum_kernel, (coarse_block, blocks, share)),
        [full(4 * latent + rows, latent)],
        [pltpu.VMEM((blocks * half, latent), F32)],
        1,
        "coarse_back_sum",
        place,
        count_from,
        packed,
    )
    return call(
        functools.partial(finish_kernel, sizes + (pool_scale,)),
        [full(count, latent), full(8, latent, latent)],
        [],
        2,
        "finish",
        place,
        most,
        d_coarse,
        back,
        back_other,
        sums,
        other_core(sums),
        pool_rows,
    )


def solution(mesh):
    blocks, cores = mesh.devices.shape
    width = 4
    grid = mesh.devices.reshape(width, width, blocks // (width * width), cores)
    mesh = jax.sharding.Mesh(grid, SPACE + ("coarse",))
    both = SPACE + ("coarse",)
    in_specs = (
        (P(SPACE, None),)
        + (P(),) * 8
        + (P(SPACE, None), P(both), P(both), P(SPACE, None, None), P(SPACE), P("coarse"), P("coarse"))
    )
    out_specs = (P(SPACE, None), P())
    return jax.shard_map(shards, mesh=mesh, in_specs=in_specs, out_specs=out_specs, check_vma=False)
```

time: 146 us -> 127 us (0.87)
  blocking collectives: 4.26 us -> 14.1 us
  starting transfers between devices: 60.2 us -> 50.8 us
  waiting for transfers between devices: 24.9 us -> 15.6 us
  Pallas kernels: 47.1 us -> 40.3 us
  local copies, waits for them, and re-layouts: 7.85 us -> 4.1 us
    all_to_all x0 -> x1, blocking collectives: none -> 14.1 us  [exchange(): return lax.all_to_all(array.reshape(-1, latent), axes, 0, 0, tiled=True)]
    ppermute x7 -> x4, starting transfers between devices: 16.9 us -> 4.33 us  [along(): return lax.ppermute(array, SPACE + ('coarse',), pairs)]
    pallas_call x14 -> x16, Pallas kernels: 47.1 us -> 40.3 us  [call(): pl.pallas_call(kernel, out_shape=outs, in_specs=specs, out_specs=[outer i...]
    ppermute x12 -> x9, starting transfers between devices: 16 us -> 22.5 us  [other_core(): return lax.ppermute(array, 'coarse', [(0, 1), (1, 0)])]
    all_to_all x3 -> x4, waiting for transfers between devices: 13.7 us -> 9.35 us  [exchange(): return lax.all_to_all(array.reshape(-1, latent), axes, 0, 0, tiled=True)]
    all_gather x1 -> x0, blocking collectives: 4.26 us -> none  [shards(): weight_grads = lax.all_gather(own_grads, 'coarse', axis=0, tiled=True)]
    all_to_all x3 -> x4, starting transfers between devices: 27.3 us -> 23.9 us  [exchange(): return lax.all_to_all(array.reshape(-1, latent), axes, 0, 0, tiled=True)]
    unnamed x51 -> x67, local copies, waits for them, and re-layouts: 7 us -> 4.08 us
  transfers between devices with their start and end apart: 22 -> 17, of which waited for: 12 -> 8; matrix products, arithmetic and copies ran while one was open for 1% -> 1% of each run, Pallas kernels for 22% -> 15%
where the time goes in v3:
time: 127 us
  starting transfers between devices  50.8 us (40%)
  Pallas kernels  40.3 us (32%)
  waiting for transfers between devices  15.6 us (12%)
  blocking collectives  14.1 us (11%)
  local copies, waits for them, and re-layouts  4.1 us (3%)
    pallas_call x16, Pallas kernels, call(): pl.pallas_call(kernel, out_shape=outs, in_specs=specs, out_specs=[outer i...  40.3 us
    all_to_all x4, starting transfers between devices, exchange(): return lax.all_to_all(array.reshape(-1, latent), axes, 0, 0, tiled=True)  23.9 us
    ppermute x9, starting transfers between devices, other_core(): return lax.ppermute(array, 'coarse', [(0, 1), (1, 0)])  22.5 us
    all_to_all x1, blocking collectives, exchange(): return lax.all_to_all(array.reshape(-1, latent), axes, 0, 0, tiled=True)  14.1 us
    all_to_all x4, waiting for transfers between devices, exchange(): return lax.all_to_all(array.reshape(-1, latent), axes, 0, 0, tiled=True)  9.35 us
    ppermute x4, waiting for transfers between devices, along(): return lax.ppermute(array, SPACE + ('coarse',), pairs)  4.48 us
    ppermute x4, starting transfers between devices, along(): return lax.ppermute(array, SPACE + ('coarse',), pairs)  4.33 us
    unnamed x67, local copies, waits for them, and re-layouts  4.08 us
  transfers between devices with their start and end apart: 17, of which 8 were waited for; matrix products, arithmetic and copies ran while one was open for 1% of the time, Pallas kernels for 15%

profile of v3, /device:TPU:1, one launch (start us, length us, event | category | flops | bytes accessed | tf_op | source)
XLA Modules:
  0.0 126.8 jit_solution(6692263776605046102)
XLA Ops:
  2.5 1.4 %pool.1.pool_ref = f32[8,16,128]{2,1,0:T(8,128)} custom-call(s32[2]{0:T(128)S(1)} %pad_add_fusion.place_ref, f32[1024,128]{1,0:T(8,128)S(1)} %copy-done.1, s32[8,128]{1,0:T(8,128)S(1)} %bitcast.21), custom_call_target="tpu_custom_call" | custom-call | flops 1100000000 | bytes 1000000 | tf_op jit(solution)/shard_map/pool/pallas_call | solution.py:620
  5.0 3.3 %collective-permute-start.2 = (s32[96,128]{1,0:T(8,128)S(1)}, s32[96,128]{1,0:T(8,128)S(1)}, u32[]{:S(2)}, u32[]{:S(2)}) collective-permute-start(s32[96,128]{1,0:T(8,128)S(1)} %get-tuple-element.23), channel_id=1, source_target_pairs={{0,1},{1,0},{2,3},{3,2},{4,5},{5,4},{6,7},{7,6},{8,9},{9,8},{10,11... | collective-permute-start | bytes 147464 | tf_op jit(solution)/shard_map/ppermute | solution.py:677
  8.3 6.5 %all-to-all-start = ((f32[8,16,128]{2,1,0:T(8,128)}), f32[8,16,128]{2,1,0:T(8,128)S(1)}, u32[]{:S(2)}, u32[]{:S(2)}) async-start(f32[8,16,128]{2,1,0:T(8,128)} %pool.1.pool_ref), calls=%async_computation | async-start | bytes 131072 | tf_op jit(solution)/shard_map/all_to_all | solution.py:688
  16.0 1.3 %collective-permute-start.1 = (f32[256,128]{1,0:T(8,128)S(1)}, f32[256,128]{1,0:T(8,128)S(1)}, u32[]{:S(2)}, u32[]{:S(2)}) collective-permute-start(f32[256,128]{1,0:T(8,128)S(1)} %get-tuple-element.22), channel_id=1, source_target_pairs={{0,4},{2,6},{4,8},{5,1},{6,10},{7,3},{8,12},{9,5},{10,14},{11,7},{... | collective-permute-start | bytes 393224 | tf_op jit(solution)/shard_map/ppermute | solution.py:685
  17.4 2.3 %count_into.1.count_ref = f32[256,128]{1,0:T(8,128)S(1)} custom-call(s32[2]{0:T(128)S(1)} %pad_add_fusion.place_ref, s32[48,128]{1,0:T(8,128)S(1)} %bitcast.11, s32[48,128]{1,0:T(8,128)S(1)} %get-tuple-element.41.send_other_ref, s32[48,128]{1,0:T(8,128)S(1)} %bitcast.14, s32[48,128]{1,0:T(8,128)S(1)} %get-tuple-element.40.recv_other_ref), custom_call_target="tpu_custom_call" | custom-call | flops 3300000000 | bytes 3000000 | tf_op jit(solution)/shard_map/count_into/pallas_call | solution.py:620
  19.7 2.2 %all-to-all-done.parts_ref = f32[8,16,128]{2,1,0:T(8,128)S(1)} async-done(((f32[8,16,128]{2,1,0:T(8,128)}), f32[8,16,128]{2,1,0:T(8,128)S(1)}, u32[]{:S(2)}, u32[]{:S(2)}) %all-to-all-start) | async-done | bytes 65568 | tf_op jit(solution)/shard_map/all_to_all | solution.py:688
  22.8 2.3 %collective-permute-done.1.far_ref = f32[256,128]{1,0:T(8,128)S(1)} collective-permute-done((f32[256,128]{1,0:T(8,128)S(1)}, f32[256,128]{1,0:T(8,128)S(1)}, u32[]{:S(2)}, u32[]{:S(2)}) %collective-permute-start.1) | collective-permute-done | bytes 131104 | tf_op jit(solution)/shard_map/ppermute | solution.py:685
  25.2 1.5 %collective-permute-start.3 = (f32[512,128]{1,0:T(8,128)S(1)}, f32[512,128]{1,0:T(8,128)S(1)}, u32[]{:S(2)}, u32[]{:S(2)}) collective-permute-start(f32[512,128]{1,0:T(8,128)S(1)} %join_halo.1.halo_ref), channel_id=1, source_target_pairs={{0,1},{1,0},{2,3},{3,2},{4,5},{5,4},{6,7},{7,6},{8,9},{9,8},{10,11... | collective-permute-start | bytes 786440 | tf_op jit(solution)/shard_map/ppermute | solution.py:677
  26.7 9.2 %all-to-all-start.1 = ((f32[16,72,128]{2,1,0:T(8,128)}), f32[16,72,128]{2,1,0:T(8,128)S(1)}, u32[]{:S(2)}, u32[]{:S(2)}) async-start(f32[16,72,128]{2,1,0:T(8,128)} %spread.1.spread_ref), calls=%async_computation.1 | async-start | bytes 1179648 | tf_op jit(solution)/shard_map/all_to_all | solution.py:688
  36.0 10.0 %edges.1 = (f32[3072,128]{1,0:T(8,128)}, f32[1024,128]{1,0:T(8,128)S(1)}) custom-call(s32[2]{0:T(128)S(1)} %pad_add_fusion.place_ref, f32[1024,128]{1,0:T(8,128)S(1)} %copy-done.2, f32[512,128]{1,0:T(8,128)S(1)} %join_halo.1.halo_ref, f32[512,128]{1,0:T(8,128)S(1)} %collective-permute-done.3.halo_other_ref, f32[128,128]{1,0:T(8,128)S(1)} %copy-done.10, ...), custom_call_target="tpu_custom_call" | custom-call | flops 3300000000 | bytes 3000000 | tf_op jit(solution)/shard_map/edges/pallas_call | solution.py:620
  50.4 1.7 %collective-permute-start.5 = (f32[64,128]{1,0:T(8,128)S(1)}, f32[64,128]{1,0:T(8,128)S(1)}, u32[]{:S(2)}, u32[]{:S(2)}) collective-permute-start(f32[64,128]{1,0:T(8,128)S(1)} %coarse_sum.1.sums_ref), channel_id=1, source_target_pairs={{0,1},{1,0},{2,3},{3,2},{4,5},{5,4},{6,7},{7,6},{8,9},{9,8},{10,11... | collective-permute-start | bytes 98312 | tf_op jit(solution)/shard_map/ppermute | solution.py:677
  53.0 3.6 %nodes.1 = (f32[1024,128]{1,0:T(8,128)S(1)}, f32[1024,128]{1,0:T(8,128)S(1)}, f32[64,128]{1,0:T(8,128)S(1)}, f32[128,128]{1,0:T(8,128)S(1)}, f32[4,128,128]{2,1,0:T(8,128)S(1)}) custom-call(s32[2]{0:T(128)S(1)} %copy-done.26, f32[1024,128]{1,0:T(8,128)S(1)} %copy-done.2, f32[1024,128]{1,0:T(8,128)S(1)} %get-tuple-element.25.agg_ref, ...), custom_call_target="tpu_custom_call" | custom-call | flops 6600000000 | bytes 6000000 | tf_op jit(solution)/shard_map/nodes/pallas_call | solution.py:620
  57.3 4.5 %edges_back.1 = (bf16[3072,256]{1,0:T(8,128)(2,1)S(1)}, f32[128,128]{1,0:T(8,128)S(1)}) custom-call(f32[128,128]{1,0:T(8,128)S(1)} %copy-done.9, s32[24,128]{1,0:T(8,128)S(1)} %bitcast.19, f32[3072,128]{1,0:T(8,128)S(1)} %copy-done.28, f32[1024,128]{1,0:T(8,128)S(1)} %get-tuple-element.26.d_agg_ref), custom_call_target="tpu_custom_call" | custom-call | flops 5500000256 | bytes 5000000 | tf_op jit(solution)/shard_map/edges_back/pallas_call | solution.py:620
  61.9 7.0 %edges_table.1 = (f32[3,128,128]{2,1,0:T(8,128)S(1)}, f32[512,128]{1,0:T(8,128)S(1)}, f32[512,128]{1,0:T(8,128)S(1)}, f32[1024,128]{1,0:T(8,128)S(1)}) custom-call(s32[2]{0:T(128)S(1)} %copy-done.26, f32[1024,128]{1,0:T(8,128)S(1)} %copy-done.2, f32[512,128]{1,0:T(8,128)S(1)} %join_halo.1.halo_ref, f32[512,128]{1,0:T(8,128)S(1)} %collective-permute-done.3.halo_other_ref, ...), custom_call_target="tpu_custom_call" | custom-call | flops 8800000000 | bytes 8000000 | tf_op jit(solution)/shard_map/edges_table/pallas_call | solution.py:620
  71.1 4.7 %all-to-all-start.2 = ((f32[16,32,128]{2,1,0:T(8,128)}), f32[16,32,128]{2,1,0:T(8,128)S(1)}, u32[]{:S(2)}, u32[]{:S(2)}) async-start(f32[16,32,128]{2,1,0:T(8,128)} %bitcast.8), calls=%async_computation.2 | async-start | bytes 524288 | tf_op jit(solution)/shard_map/all_to_all | solution.py:688
  75.8 2.3 %count_from.1.count_ref = f32[256,128]{1,0:T(8,128)S(1)} custom-call(s32[2]{0:T(128)S(1)} %copy-done.27, s32[48,128]{1,0:T(8,128)S(1)} %bitcast.12, s32[48,128]{1,0:T(8,128)S(1)} %get-tuple-element.41.send_other_ref, s32[48,128]{1,0:T(8,128)S(1)} %bitcast.15, s32[48,128]{1,0:T(8,128)S(1)} %get-tuple-element.40.recv_other_ref, ...), custom_call_target="tpu_custom_call" | custom-call | flops 3300000000 | bytes 3000000 | tf_op jit(solution)/shard_map/count_from/pallas_call | solution.py:620
  78.2 6.0 %all-to-all-done.2.parts_ref = f32[16,32,128]{2,1,0:T(8,128)S(1)} async-done(((f32[16,32,128]{2,1,0:T(8,128)}), f32[16,32,128]{2,1,0:T(8,128)S(1)}, u32[]{:S(2)}, u32[]{:S(2)}) %all-to-all-start.2) | async-done | bytes 262176 | tf_op jit(solution)/shard_map/all_to_all | solution.py:688
  84.8 14.1 %all_to_all.33.parts_ref = f32[8,48,128]{2,1,0:T(8,128)S(1)} all-to-all(f32[8,48,128]{2,1,0:T(8,128)S(1)} %get-tuple-element.39), channel_id=1, replica_groups=mesh['y'=4,'x'=4,'z'=8,'coarse'=2] {'z'}, dimensions={0} | all-to-all | bytes 393216 | tf_op jit(solution)/shard_map/all_to_all | solution.py:688
  99.8 3.6 %all-to-all-start.4 = ((f32[16,104,128]{2,1,0:T(8,128)}), f32[16,104,128]{2,1,0:T(8,128)S(1)}, u32[]{:S(2)}, u32[]{:S(2)}) async-start(f32[16,104,128]{2,1,0:T(8,128)} %plane.1), calls=%async_computation.4 | async-start | bytes 1703936 | tf_op jit(solution)/shard_map/all_to_all | solution.py:688
  103.9 7.4 %collective-permute-start.6 = (f32[1024,128]{1,0:T(8,128)S(1)}, f32[1024,128]{1,0:T(8,128)S(1)}, u32[]{:S(2)}, u32[]{:S(2)}) collective-permute-start(f32[1024,128]{1,0:T(8,128)S(1)} %get-tuple-element.30.own_ref), channel_id=1, source_target_pairs={{0,1},{1,0},{2,3},{3,2},{4,5},{5,4},{6,7},{7,6},{8,9},{9,8},{10,11... | collective-permute-start | bytes 1572872 | tf_op jit(solution)/shard_map/ppermute | solution.py:677
  114.8 4.4 %collective-permute-start.11 = (f32[528,128]{1,0:T(8,128)S(1)}, f32[528,128]{1,0:T(8,128)S(1)}, u32[]{:S(2)}, u32[]{:S(2)}) collective-permute-start(f32[528,128]{1,0:T(8,128)S(1)} %constant_dynamic-update-slice_fusion.back_ref), channel_id=1, source_target_pairs={{0,1},{1,0},{2,3},{3,2},{4,5},{5,4},{6,7},{7,6},{8,9},{9,8},{10,11... | collective-permute-start | bytes 811016 | tf_op jit(solution)/shard_map/ppermute | solution.py:677
  120.2 3.2 %collective-permute-start.12 = (f32[544,128]{1,0:T(8,128)S(1)}, f32[544,128]{1,0:T(8,128)S(1)}, u32[]{:S(2)}, u32[]{:S(2)}) collective-permute-start(f32[544,128]{1,0:T(8,128)S(1)} %coarse_back_sum.1.mine_ref), channel_id=1, source_target_pairs={{0,1},{1,0},{2,3},{3,2},{4,5},{5,4},{6,7},{7,6},{8,9},{9,8},{10,11... | collective-permute-start | bytes 835592 | tf_op jit(solution)/shard_map/ppermute | solution.py:677
  123.5 1.5 %gather_back.1.most_ref = f32[1024,128]{1,0:T(8,128)S(1)} custom-call(s32[2]{0:T(128)S(1)} %copy-done.27, f32[1024,128]{1,0:T(8,128)S(1)} %get-tuple-element.30.own_ref, f32[1024,128]{1,0:T(8,128)S(1)} %collective-permute-done.6.other_ref, f32[528,128]{1,0:T(8,128)S(1)} %constant_dynamic-update-slice_fusion.back_ref, ...), custom_call_target="tpu_custom_call" | custom-call | flops 3300000000 | bytes 3000000 | tf_op jit(solution)/shard_map/gather_back/pallas_call | solution.py:620
  125.0 1.8 %finish.1 = (f32[1024,128]{1,0:T(8,128)}, f32[8,128,128]{2,1,0:T(8,128)}) custom-call(s32[2]{0:T(128)S(1)} %copy-done.27, f32[1024,128]{1,0:T(8,128)S(1)} %gather_back.1.most_ref, f32[64,128]{1,0:T(8,128)S(1)} %copy-done.32, f32[528,128]{1,0:T(8,128)S(1)} %constant_dynamic-update-slice_fusion.back_ref, ...), custom_call_target="tpu_custom_call" | custom-call | flops 2200000000 | bytes 2000000 | tf_op jit(solution)/shard_map/finish/pallas_call | solution.py:620
  (99 shorter events, 19.8 us)
Async XLA Ops:
  0.7 35.2 %copy-start.24 = (s32[2]{0:T(128)}, s32[2]{0:T(128)S(1)}, u32[]{:S(2)}) copy-start(s32[2]{0:T(128)S(1)} %pad_add_fusion.place_ref) | copy-start | bytes 28
  5.0 12.4 %collective-permute-start.2 = (s32[96,128]{1,0:T(8,128)S(1)}, s32[96,128]{1,0:T(8,128)S(1)}, u32[]{:S(2)}, u32[]{:S(2)}) collective-permute-start(s32[96,128]{1,0:T(8,128)S(1)} %get-tuple-element.23), channel_id=1, source_target_pairs={{0,1},{1,0},{2,3},{3,2},{4,5},{5,4},{6,7},{7,6},{8,9},{9,8},{10,11... | collective-permute-start | bytes 147464 | tf_op jit(solution)/shard_map/ppermute | solution.py:677
  8.3 13.6 %all-to-all-start = ((f32[8,16,128]{2,1,0:T(8,128)}), f32[8,16,128]{2,1,0:T(8,128)S(1)}, u32[]{:S(2)}, u32[]{:S(2)}) async-start(f32[8,16,128]{2,1,0:T(8,128)} %pool.1.pool_ref), calls=%async_computation | async-start | bytes 131072 | tf_op jit(solution)/shard_map/all_to_all | solution.py:688
  14.8 8.1 %collective-permute-start = (f32[256,128]{1,0:T(8,128)S(1)}, f32[256,128]{1,0:T(8,128)S(1)}, u32[]{:S(2)}, u32[]{:S(2)}) collective-permute-start(f32[256,128]{1,0:T(8,128)S(1)} %get-tuple-element.21), channel_id=1, source_target_pairs={{0,2},{2,4},{3,1},{4,6},{5,3},{6,8},{7,5},{8,10},{9,7},{10,12},{11... | collective-permute-start | bytes 393224 | tf_op jit(solution)/shard_map/ppermute | solution.py:685
  16.0 9.1 %collective-permute-start.1 = (f32[256,128]{1,0:T(8,128)S(1)}, f32[256,128]{1,0:T(8,128)S(1)}, u32[]{:S(2)}, u32[]{:S(2)}) collective-permute-start(f32[256,128]{1,0:T(8,128)S(1)} %get-tuple-element.22), channel_id=1, source_target_pairs={{0,4},{2,6},{4,8},{5,1},{6,10},{7,3},{8,12},{9,5},{10,14},{11,7},{... | collective-permute-start | bytes 393224 | tf_op jit(solution)/shard_map/ppermute | solution.py:685
  22.8 13.2 %copy-start.2 = (f32[1024,128]{1,0:T(8,128)S(1)}, f32[1024,128]{1,0:T(8,128)}, u32[]{:S(2)}) copy-start(f32[1024,128]{1,0:T(8,128)} %cells_ref.7) | copy-start | bytes 1572868
  22.8 13.2 %copy-start.8 = (f32[128,128]{1,0:T(8,128)S(1)}, f32[128,128]{1,0:T(8,128)}, u32[]{:S(2)}) copy-start(f32[128,128]{1,0:T(8,128)} %w_msg_ref.3) | copy-start | bytes 196612
  22.8 13.2 %copy-start.10 = (f32[128,128]{1,0:T(8,128)S(1)}, f32[128,128]{1,0:T(8,128)}, u32[]{:S(2)}) copy-start(f32[128,128]{1,0:T(8,128)} %w_send_ref.3) | copy-start | bytes 196612
  22.8 13.2 %copy-start.12 = (f32[128,128]{1,0:T(8,128)S(1)}, f32[128,128]{1,0:T(8,128)}, u32[]{:S(2)}) copy-start(f32[128,128]{1,0:T(8,128)} %w_recv_ref.3) | copy-start | bytes 196612
  22.8 13.2 %copy-start.17 = (s32[3072]{0:T(1024)S(1)}, s32[3072]{0:T(1024)}, u32[]{:S(2)}) copy-start(s32[3072]{0:T(1024)} %param.26) | copy-start | bytes 36868
  22.8 13.2 %copy-start.19 = (s32[3072]{0:T(1024)S(1)}, s32[3072]{0:T(1024)}, u32[]{:S(2)}) copy-start(s32[3072]{0:T(1024)} %param.27) | copy-start | bytes 36868
  25.2 10.8 %collective-permute-start.3 = (f32[512,128]{1,0:T(8,128)S(1)}, f32[512,128]{1,0:T(8,128)S(1)}, u32[]{:S(2)}, u32[]{:S(2)}) collective-permute-start(f32[512,128]{1,0:T(8,128)S(1)} %join_halo.1.halo_ref), channel_id=1, source_target_pairs={{0,1},{1,0},{2,3},{3,2},{4,5},{5,4},{6,7},{7,6},{8,9},{9,8},{10,11... | collective-permute-start | bytes 786440 | tf_op jit(solution)/shard_map/ppermute | solution.py:677
  26.7 21.0 %all-to-all-start.1 = ((f32[16,72,128]{2,1,0:T(8,128)}), f32[16,72,128]{2,1,0:T(8,128)S(1)}, u32[]{:S(2)}, u32[]{:S(2)}) async-start(f32[16,72,128]{2,1,0:T(8,128)} %spread.1.spread_ref), calls=%async_computation.1 | async-start | bytes 1179648 | tf_op jit(solution)/shard_map/all_to_all | solution.py:688
  46.1 6.9 %collective-permute-start.4 = (f32[1024,128]{1,0:T(8,128)S(1)}, f32[1024,128]{1,0:T(8,128)S(1)}, u32[]{:S(2)}, u32[]{:S(2)}) collective-permute-start(f32[1024,128]{1,0:T(8,128)S(1)} %get-tuple-element.25.agg_ref), channel_id=1, source_target_pairs={{0,1},{1,0},{2,3},{3,2},{4,5},{5,4},{6,7},{7,6},{8,9},{9,8},{10,11... | collective-permute-start | bytes 1572872 | tf_op jit(solution)/shard_map/ppermute | solution.py:677
  50.4 2.6 %collective-permute-start.5 = (f32[64,128]{1,0:T(8,128)S(1)}, f32[64,128]{1,0:T(8,128)S(1)}, u32[]{:S(2)}, u32[]{:S(2)}) collective-permute-start(f32[64,128]{1,0:T(8,128)S(1)} %coarse_sum.1.sums_ref), channel_id=1, source_target_pairs={{0,1},{1,0},{2,3},{3,2},{4,5},{5,4},{6,7},{7,6},{8,9},{9,8},{10,11... | collective-permute-start | bytes 98312 | tf_op jit(solution)/shard_map/ppermute | solution.py:677
  68.8 1.5 %collective-permute-start.7 = (f32[3,128,128]{2,1,0:T(8,128)S(1)}, f32[3,128,128]{2,1,0:T(8,128)S(1)}, u32[]{:S(2)}, u32[]{:S(2)}) collective-permute-start(f32[3,128,128]{2,1,0:T(8,128)S(1)} %get-tuple-element.31), channel_id=1, source_target_pairs={{0,1},{1,0},{2,3},{3,2},{4,5},{5,4},{6,7},{7,6},{8,9},{9,8},{10,11... | collective-permute-start | bytes 589832 | tf_op jit(solution)/shard_map/ppermute | solution.py:677
  69.3 8.9 %collective-permute-start.8 = (f32[512,128]{1,0:T(8,128)S(1)}, f32[512,128]{1,0:T(8,128)S(1)}, u32[]{:S(2)}, u32[]{:S(2)}) collective-permute-start(f32[512,128]{1,0:T(8,128)S(1)} %get-tuple-element.36), channel_id=1, source_target_pairs={{0,1},{1,0},{2,3},{3,2},{4,5},{5,4},{6,7},{7,6},{8,9},{9,8},{10,11... | collective-permute-start | bytes 786440 | tf_op jit(solution)/shard_map/ppermute | solution.py:677
  71.1 13.0 %all-to-all-start.2 = ((f32[16,32,128]{2,1,0:T(8,128)}), f32[16,32,128]{2,1,0:T(8,128)S(1)}, u32[]{:S(2)}, u32[]{:S(2)}) async-start(f32[16,32,128]{2,1,0:T(8,128)} %bitcast.8), calls=%async_computation.2 | async-start | bytes 524288 | tf_op jit(solution)/shard_map/all_to_all | solution.py:688
  99.8 19.3 %all-to-all-start.4 = ((f32[16,104,128]{2,1,0:T(8,128)}), f32[16,104,128]{2,1,0:T(8,128)S(1)}, u32[]{:S(2)}, u32[]{:S(2)}) async-start(f32[16,104,128]{2,1,0:T(8,128)} %plane.1), calls=%async_computation.4 | async-start | bytes 1703936 | tf_op jit(solution)/shard_map/all_to_all | solution.py:688
  103.5 10.3 %collective-permute-start.9 = (f32[272,128]{1,0:T(8,128)S(1)}, f32[272,128]{1,0:T(8,128)S(1)}, u32[]{:S(2)}, u32[]{:S(2)}) collective-permute-start(f32[272,128]{1,0:T(8,128)S(1)} %get-tuple-element.37), channel_id=1, source_target_pairs={{0,254},{1,3},{2,0},{3,5},{4,2},{5,7},{6,4},{7,9},{8,6},{9,11},{10... | collective-permute-start | bytes 417800 | tf_op jit(solution)/shard_map/ppermute | solution.py:685
  103.9 19.5 %collective-permute-start.6 = (f32[1024,128]{1,0:T(8,128)S(1)}, f32[1024,128]{1,0:T(8,128)S(1)}, u32[]{:S(2)}, u32[]{:S(2)}) collective-permute-start(f32[1024,128]{1,0:T(8,128)S(1)} %get-tuple-element.30.own_ref), channel_id=1, source_target_pairs={{0,1},{1,0},{2,3},{3,2},{4,5},{5,4},{6,7},{7,6},{8,9},{9,8},{10,11... | collective-permute-start | bytes 1572872 | tf_op jit(solution)/shard_map/ppermute | solution.py:677
  111.3 3.5 %collective-permute-start.10 = (f32[256,128]{1,0:T(8,128)S(1)}, f32[256,128]{1,0:T(8,128)S(1)}, u32[]{:S(2)}, u32[]{:S(2)}) collective-permute-start(f32[256,128]{1,0:T(8,128)S(1)} %get-tuple-element.38), channel_id=1, source_target_pairs={{1,5},{3,7},{4,0},{5,9},{6,2},{7,11},{8,4},{9,13},{10,6},{11,15},{... | collective-permute-start | bytes 393224 | tf_op jit(solution)/shard_map/ppermute | solution.py:685
  114.8 8.7 %collective-permute-start.11 = (f32[528,128]{1,0:T(8,128)S(1)}, f32[528,128]{1,0:T(8,128)S(1)}, u32[]{:S(2)}, u32[]{:S(2)}) collective-permute-start(f32[528,128]{1,0:T(8,128)S(1)} %constant_dynamic-update-slice_fusion.back_ref), channel_id=1, source_target_pairs={{0,1},{1,0},{2,3},{3,2},{4,5},{5,4},{6,7},{7,6},{8,9},{9,8},{10,11... | collective-permute-start | bytes 811016 | tf_op jit(solution)/shard_map/ppermute | solution.py:677
  120.2 4.7 %collective-permute-start.12 = (f32[544,128]{1,0:T(8,128)S(1)}, f32[544,128]{1,0:T(8,128)S(1)}, u32[]{:S(2)}, u32[]{:S(2)}) collective-permute-start(f32[544,128]{1,0:T(8,128)S(1)} %coarse_back_sum.1.mine_ref), channel_id=1, source_target_pairs={{0,1},{1,0},{2,3},{3,2},{4,5},{5,4},{6,7},{7,6},{8,9},{9,8},{10,11... | collective-permute-start | bytes 835592 | tf_op jit(solution)/shard_map/ppermute | solution.py:677
  (26 other events, 117.0 us)

commit v4 on v3

--- a/solution.py
+++ b/solution.py
@@ -151,7 +151,7 @@
 
 
 def halo_kernel(
-    place_ref, cells_ref, send_ref, coarse_send_ref, coarse_recv_ref, pool_ref, near_ref, far_ref, edges_ref
+    place_ref, cells_ref, send_ref, coarse_send_ref, coarse_recv_ref, pool_ref, far_ref, near_ref, edges_ref
 ):
     core = place_ref[1]
     count = cells_ref.shape[0]
@@ -164,7 +164,7 @@
             out[chunk * LANES : (chunk + 1) * LANES, :] = fold(mm(one_hot_rows(row, count), pair))
 
 
-def join_halo_kernel(near_ref, far_ref, spread_ref, out_ref):
+def join_halo_kernel(far_ref, near_ref, spread_ref, out_ref):
     slots = near_ref.shape[0]
     out_ref[:slots, :] = near_ref[...]
     out_ref[slots:, :] = far_ref[...]
@@ -302,7 +302,7 @@
         sums_ref[pl.ds(pl.multiple_of(rows + spot * coarse_block + core * half, half), half), :] = own
 
 
-def coarse_back_sum_kernel(sizes, place_ref, count_ref, packed_ref, out_ref, values):
+def coarse_back_sum_kernel(sizes, place_ref, count_ref, packed_ref, most_ref, out_ref, values):
     coarse_block, blocks, share = sizes
     rows = 2 * coarse_block
     half = coarse_block // 2
@@ -411,7 +411,7 @@
 
 
 def line_kernel(
-    scale, place_ref, parts_ref, d_coarse_ref, mine_ref, other_ref, count_ref, out_ref, near_ref, far_ref
+    scale, place_ref, parts_ref, d_coarse_ref, mine_ref, other_ref, count_ref, out_ref, far_ref, near_ref
 ):
     total = jnp.sum(parts_ref[...], axis=0) * scale
     core = place_ref[1]
@@ -706,7 +706,7 @@
         far=(1, 2),
     )
     parts = exchange(copies, LINE).reshape(line, coarse_block, latent)
-    near, far, edge_both = call(
+    far, near, edge_both = call(
         halo_kernel,
         [
             full(slots, latent),
@@ -751,8 +751,8 @@
         [],
         0.5,
         "join_halo",
+        along(far, 2),
         along(near, 1),
-        along(far, 2),
         after=(copies,),
     )
     halo_other = other_core(halo)
@@ -872,12 +872,12 @@
         *coarse_edges,
         after=(mine,),
     )
-    copies, near_back, far_back = call(
+    copies, far_back, near_back = call(
         functools.partial(line_kernel, grad_scale),
         [
             full(line, share + coarse_block, latent),
+            full(slots, latent),
             full(slots + coarse_block, latent),
-            full(slots, latent),
         ],
         [],
         1,
@@ -889,7 +889,8 @@
         other_back,
         after=(count_from,),
     )
-    back = jnp.concatenate([along(near_back, -1, True), along(far_back, -2)], axis=0)
+    far_back = along(far_back, -2)
+    back = jnp.concatenate([along(near_back, -1, True), far_back], axis=0)
     back_other = other_core(back)
     parts = exchange(copies, LINE).reshape(line, share + coarse_block, latent)
     (copies,) = call(
@@ -923,6 +924,7 @@
         place,
         count_from,
         packed,
+        after=(most,),
     )
     return call(
         functools.partial(finish_kernel, sizes + (pool_scale,)),

time: 127 us -> 124 us (0.976)
  blocking collectives: 14.1 us -> 0 us
  starting transfers between devices: 50.8 us -> 56.4 us
  waiting for transfers between devices: 15.6 us -> 20 us
    all_to_all x1 -> x0, blocking collectives: 14.1 us -> none  [exchange(): return lax.all_to_all(array.reshape(-1, latent), axes, 0, 0, tiled=True)]
    all_to_all x4 -> x5, waiting for transfers between devices: 9.35 us -> 15.2 us  [exchange(): return lax.all_to_all(array.reshape(-1, latent), axes, 0, 0, tiled=True)]
    all_to_all x4 -> x5, starting transfers between devices: 23.9 us -> 28.4 us  [exchange(): return lax.all_to_all(array.reshape(-1, latent), axes, 0, 0, tiled=True)]
    ppermute x4, waiting for transfers between devices: 4.48 us -> 0.59 us  [along(): return lax.ppermute(array, SPACE + ('coarse',), pairs)]
    ppermute x9, waiting for transfers between devices: 1.81 us -> 4.16 us  [other_core(): return lax.ppermute(array, 'coarse', [(0, 1), (1, 0)])]
  transfers between devices with their start and end apart: 17 -> 18, of which waited for: 8 -> 10; matrix products, arithmetic and copies ran while one was open for 1% -> 1% of each run, Pallas kernels for 15% -> 16%
where the time goes in v4:
time: 124 us; the launch traced here: 123 us
  starting transfers between devices  56.4 us (45%)
  Pallas kernels  40.9 us (33%)
  waiting for transfers between devices  20 us (16%)
  local copies, waits for them, and re-layouts  3.99 us (3%)
    pallas_call x16, Pallas kernels, call(): pl.pallas_call(kernel, out_shape=outs, in_specs=specs, out_specs=[outer i...  40.9 us
    all_to_all x5, starting transfers between devices, exchange(): return lax.all_to_all(array.reshape(-1, latent), axes, 0, 0, tiled=True)  28.4 us
    ppermute x9, starting transfers between devices, other_core(): return lax.ppermute(array, 'coarse', [(0, 1), (1, 0)])  22.6 us
    all_to_all x5, waiting for transfers between devices, exchange(): return lax.all_to_all(array.reshape(-1, latent), axes, 0, 0, tiled=True)  15.2 us
    ppermute x4, starting transfers between devices, along(): return lax.ppermute(array, SPACE + ('coarse',), pairs)  5.32 us
    ppermute x9, waiting for transfers between devices, other_core(): return lax.ppermute(array, 'coarse', [(0, 1), (1, 0)])  4.16 us
    unnamed x67, local copies, waits for them, and re-layouts  3.98 us
  transfers between devices with their start and end apart: 18, of which 10 were waited for; matrix products, arithmetic and copies ran while one was open for 1% of the time, Pallas kernels for 16%

profile of v4, /device:TPU:1, one launch (start us, length us, event | category | flops | bytes accessed | tf_op | source)
XLA Modules:
  0.0 123.2 jit_solution(15965682885150479519)
XLA Ops:
  5.0 3.3 %collective-permute-start.2 = (s32[96,128]{1,0:T(8,128)S(1)}, s32[96,128]{1,0:T(8,128)S(1)}, u32[]{:S(2)}, u32[]{:S(2)}) collective-permute-start(s32[96,128]{1,0:T(8,128)S(1)} %get-tuple-element.23), channel_id=1, source_target_pairs={{0,1},{1,0},{2,3},{3,2},{4,5},{5,4},{6,7},{7,6},{8,9},{9,8},{10,11... | collective-permute-start | bytes 147464 | tf_op jit(solution)/shard_map/ppermute | solution.py:677
  8.3 6.5 %all-to-all-start = ((f32[8,16,128]{2,1,0:T(8,128)}), f32[8,16,128]{2,1,0:T(8,128)S(1)}, u32[]{:S(2)}, u32[]{:S(2)}) async-start(f32[8,16,128]{2,1,0:T(8,128)} %pool.1.pool_ref), calls=%async_computation | async-start | bytes 131072 | tf_op jit(solution)/shard_map/all_to_all | solution.py:688
  17.4 2.3 %count_into.1.count_ref = f32[256,128]{1,0:T(8,128)S(1)} custom-call(s32[2]{0:T(128)S(1)} %pad_add_fusion.place_ref, s32[48,128]{1,0:T(8,128)S(1)} %bitcast.11, s32[48,128]{1,0:T(8,128)S(1)} %get-tuple-element.41.send_other_ref, s32[48,128]{1,0:T(8,128)S(1)} %bitcast.14, s32[48,128]{1,0:T(8,128)S(1)} %get-tuple-element.40.recv_other_ref), custom_call_target="tpu_custom_call" | custom-call | flops 3300000000 | bytes 3000000 | tf_op jit(solution)/shard_map/count_into/pallas_call | solution.py:620
  19.7 2.2 %all-to-all-done.parts_ref = f32[8,16,128]{2,1,0:T(8,128)S(1)} async-done(((f32[8,16,128]{2,1,0:T(8,128)}), f32[8,16,128]{2,1,0:T(8,128)S(1)}, u32[]{:S(2)}, u32[]{:S(2)}) %all-to-all-start) | async-done | bytes 65568 | tf_op jit(solution)/shard_map/all_to_all | solution.py:688
  23.4 3.3 %collective-permute-start.3 = (f32[512,128]{1,0:T(8,128)S(1)}, f32[512,128]{1,0:T(8,128)S(1)}, u32[]{:S(2)}, u32[]{:S(2)}) collective-permute-start(f32[512,128]{1,0:T(8,128)S(1)} %join_halo.1.halo_ref), channel_id=1, source_target_pairs={{0,1},{1,0},{2,3},{3,2},{4,5},{5,4},{6,7},{7,6},{8,9},{9,8},{10,11... | collective-permute-start | bytes 786440 | tf_op jit(solution)/shard_map/ppermute | solution.py:677
  26.7 9.0 %all-to-all-start.1 = ((f32[16,72,128]{2,1,0:T(8,128)}), f32[16,72,128]{2,1,0:T(8,128)S(1)}, u32[]{:S(2)}, u32[]{:S(2)}) async-start(f32[16,72,128]{2,1,0:T(8,128)} %spread.1.spread_ref), calls=%async_computation.1 | async-start | bytes 1179648 | tf_op jit(solution)/shard_map/all_to_all | solution.py:688
  35.8 10.0 %edges.1 = (f32[3072,128]{1,0:T(8,128)}, f32[1024,128]{1,0:T(8,128)S(1)}) custom-call(s32[2]{0:T(128)S(1)} %pad_add_fusion.place_ref, f32[1024,128]{1,0:T(8,128)S(1)} %copy-done.2, f32[512,128]{1,0:T(8,128)S(1)} %join_halo.1.halo_ref, f32[512,128]{1,0:T(8,128)S(1)} %collective-permute-done.3.halo_other_ref, f32[128,128]{1,0:T(8,128)S(1)} %copy-done.10, ...), custom_call_target="tpu_custom_call" | custom-call | flops 3300000000 | bytes 3000000 | tf_op jit(solution)/shard_map/edges/pallas_call | solution.py:620
  50.1 1.7 %collective-permute-start.5 = (f32[64,128]{1,0:T(8,128)S(1)}, f32[64,128]{1,0:T(8,128)S(1)}, u32[]{:S(2)}, u32[]{:S(2)}) collective-permute-start(f32[64,128]{1,0:T(8,128)S(1)} %coarse_sum.1.sums_ref), channel_id=1, source_target_pairs={{0,1},{1,0},{2,3},{3,2},{4,5},{5,4},{6,7},{7,6},{8,9},{9,8},{10,11... | collective-permute-start | bytes 98312 | tf_op jit(solution)/shard_map/ppermute | solution.py:677
  52.7 3.6 %nodes.1 = (f32[1024,128]{1,0:T(8,128)S(1)}, f32[1024,128]{1,0:T(8,128)S(1)}, f32[64,128]{1,0:T(8,128)S(1)}, f32[128,128]{1,0:T(8,128)S(1)}, f32[4,128,128]{2,1,0:T(8,128)S(1)}) custom-call(s32[2]{0:T(128)S(1)} %copy-done.26, f32[1024,128]{1,0:T(8,128)S(1)} %copy-done.2, f32[1024,128]{1,0:T(8,128)S(1)} %get-tuple-element.25.agg_ref, ...), custom_call_target="tpu_custom_call" | custom-call | flops 6600000000 | bytes 6000000 | tf_op jit(solution)/shard_map/nodes/pallas_call | solution.py:620
  57.0 4.5 %edges_back.1 = (bf16[3072,256]{1,0:T(8,128)(2,1)S(1)}, f32[128,128]{1,0:T(8,128)S(1)}) custom-call(f32[128,128]{1,0:T(8,128)S(1)} %copy-done.9, s32[24,128]{1,0:T(8,128)S(1)} %bitcast.19, f32[3072,128]{1,0:T(8,128)S(1)} %copy-done.28, f32[1024,128]{1,0:T(8,128)S(1)} %get-tuple-element.26.d_agg_ref), custom_call_target="tpu_custom_call" | custom-call | flops 5500000256 | bytes 5000000 | tf_op jit(solution)/shard_map/edges_back/pallas_call | solution.py:620
  61.5 7.0 %edges_table.1 = (f32[3,128,128]{2,1,0:T(8,128)S(1)}, f32[512,128]{1,0:T(8,128)S(1)}, f32[512,128]{1,0:T(8,128)S(1)}, f32[1024,128]{1,0:T(8,128)S(1)}) custom-call(s32[2]{0:T(128)S(1)} %copy-done.26, f32[1024,128]{1,0:T(8,128)S(1)} %copy-done.2, f32[512,128]{1,0:T(8,128)S(1)} %join_halo.1.halo_ref, f32[512,128]{1,0:T(8,128)S(1)} %collective-permute-done.3.halo_other_ref, ...), custom_call_target="tpu_custom_call" | custom-call | flops 8800000000 | bytes 8000000 | tf_op jit(solution)/shard_map/edges_table/pallas_call | solution.py:620
  70.8 4.7 %all-to-all-start.2 = ((f32[16,32,128]{2,1,0:T(8,128)}), f32[16,32,128]{2,1,0:T(8,128)S(1)}, u32[]{:S(2)}, u32[]{:S(2)}) async-start(f32[16,32,128]{2,1,0:T(8,128)} %bitcast.8), calls=%async_computation.2 | async-start | bytes 524288 | tf_op jit(solution)/shard_map/all_to_all | solution.py:688
  75.5 2.3 %count_from.1.count_ref = f32[256,128]{1,0:T(8,128)S(1)} custom-call(s32[2]{0:T(128)S(1)} %copy-done.27, s32[48,128]{1,0:T(8,128)S(1)} %bitcast.12, s32[48,128]{1,0:T(8,128)S(1)} %get-tuple-element.41.send_other_ref, s32[48,128]{1,0:T(8,128)S(1)} %bitcast.15, s32[48,128]{1,0:T(8,128)S(1)} %get-tuple-element.40.recv_other_ref, ...), custom_call_target="tpu_custom_call" | custom-call | flops 3300000000 | bytes 3000000 | tf_op jit(solution)/shard_map/count_from/pallas_call | solution.py:620
  77.9 6.0 %all-to-all-done.2.parts_ref = f32[16,32,128]{2,1,0:T(8,128)S(1)} async-done(((f32[16,32,128]{2,1,0:T(8,128)}), f32[16,32,128]{2,1,0:T(8,128)S(1)}, u32[]{:S(2)}, u32[]{:S(2)}) %all-to-all-start.2) | async-done | bytes 262176 | tf_op jit(solution)/shard_map/all_to_all | solution.py:688
  85.1 4.7 %all-to-all-start.3 = ((f32[8,48,128]{2,1,0:T(8,128)}), f32[8,48,128]{2,1,0:T(8,128)S(1)}, u32[]{:S(2)}, u32[]{:S(2)}) async-start(f32[8,48,128]{2,1,0:T(8,128)} %get-tuple-element.39), calls=%async_computation.3 | async-start | bytes 393216 | tf_op jit(solution)/shard_map/all_to_all | solution.py:688
  89.8 1.5 %collective-permute-start.9 = (f32[272,128]{1,0:T(8,128)S(1)}, f32[272,128]{1,0:T(8,128)S(1)}, u32[]{:S(2)}, u32[]{:S(2)}) collective-permute-start(f32[272,128]{1,0:T(8,128)S(1)} %get-tuple-element.37), channel_id=1, source_target_pairs={{0,254},{1,3},{2,0},{3,5},{4,2},{5,7},{6,4},{7,9},{8,6},{9,11},{10... | collective-permute-start | bytes 417800 | tf_op jit(solution)/shard_map/ppermute | solution.py:685
  91.3 4.0 %collective-permute-start.6 = (f32[1024,128]{1,0:T(8,128)S(1)}, f32[1024,128]{1,0:T(8,128)S(1)}, u32[]{:S(2)}, u32[]{:S(2)}) collective-permute-start(f32[1024,128]{1,0:T(8,128)S(1)} %get-tuple-element.30.own_ref), channel_id=1, source_target_pairs={{0,1},{1,0},{2,3},{3,2},{4,5},{5,4},{6,7},{7,6},{8,9},{9,8},{10,11... | collective-permute-start | bytes 1572872 | tf_op jit(solution)/shard_map/ppermute | solution.py:677
  96.5 1.7 %all-to-all-done.3.parts_ref = f32[8,48,128]{2,1,0:T(8,128)S(1)} async-done(((f32[8,48,128]{2,1,0:T(8,128)}), f32[8,48,128]{2,1,0:T(8,128)S(1)}, u32[]{:S(2)}, u32[]{:S(2)}) %all-to-all-start.3) | async-done | bytes 196640 | tf_op jit(solution)/shard_map/all_to_all | solution.py:688
  99.3 3.6 %all-to-all-start.4 = ((f32[16,104,128]{2,1,0:T(8,128)}), f32[16,104,128]{2,1,0:T(8,128)S(1)}, u32[]{:S(2)}, u32[]{:S(2)}) async-start(f32[16,104,128]{2,1,0:T(8,128)} %plane.1), calls=%async_computation.4 | async-start | bytes 1703936 | tf_op jit(solution)/shard_map/all_to_all | solution.py:688
  102.9 4.2 %collective-permute-start.11 = (f32[528,128]{1,0:T(8,128)S(1)}, f32[528,128]{1,0:T(8,128)S(1)}, u32[]{:S(2)}, u32[]{:S(2)}) collective-permute-start(f32[528,128]{1,0:T(8,128)S(1)} %constant_dynamic-update-slice_fusion.back_ref), channel_id=1, source_target_pairs={{0,1},{1,0},{2,3},{3,2},{4,5},{5,4},{6,7},{7,6},{8,9},{9,8},{10,11... | collective-permute-start | bytes 811016 | tf_op jit(solution)/shard_map/ppermute | solution.py:677
  108.3 1.5 %gather_back.1.most_ref = f32[1024,128]{1,0:T(8,128)S(1)} custom-call(s32[2]{0:T(128)S(1)} %copy-done.27, f32[1024,128]{1,0:T(8,128)S(1)} %get-tuple-element.30.own_ref, f32[1024,128]{1,0:T(8,128)S(1)} %collective-permute-done.6.other_ref, f32[528,128]{1,0:T(8,128)S(1)} %constant_dynamic-update-slice_fusion.back_ref, ...), custom_call_target="tpu_custom_call" | custom-call | flops 3300000000 | bytes 3000000 | tf_op jit(solution)/shard_map/gather_back/pallas_call | solution.py:620
  109.8 4.1 %all-to-all-done.4.packed_ref = f32[16,104,128]{2,1,0:T(8,128)S(1)} async-done(((f32[16,104,128]{2,1,0:T(8,128)}), f32[16,104,128]{2,1,0:T(8,128)S(1)}, u32[]{:S(2)}, u32[]{:S(2)}) %all-to-all-start.4) | async-done | bytes 852000 | tf_op jit(solution)/shard_map/all_to_all | solution.py:688
  115.0 5.2 %collective-permute-start.12 = (f32[544,128]{1,0:T(8,128)S(1)}, f32[544,128]{1,0:T(8,128)S(1)}, u32[]{:S(2)}, u32[]{:S(2)}) collective-permute-start(f32[544,128]{1,0:T(8,128)S(1)} %coarse_back_sum.1.mine_ref), channel_id=1, source_target_pairs={{0,1},{1,0},{2,3},{3,2},{4,5},{5,4},{6,7},{7,6},{8,9},{9,8},{10,11... | collective-permute-start | bytes 835592 | tf_op jit(solution)/shard_map/ppermute | solution.py:677
  121.4 1.8 %finish.1 = (f32[1024,128]{1,0:T(8,128)}, f32[8,128,128]{2,1,0:T(8,128)}) custom-call(s32[2]{0:T(128)S(1)} %copy-done.27, f32[1024,128]{1,0:T(8,128)S(1)} %gather_back.1.most_ref, f32[64,128]{1,0:T(8,128)S(1)} %copy-done.32, f32[528,128]{1,0:T(8,128)S(1)} %constant_dynamic-update-slice_fusion.back_ref, ...), custom_call_target="tpu_custom_call" | custom-call | flops 2200000000 | bytes 2000000 | tf_op jit(solution)/shard_map/finish/pallas_call | solution.py:620
  (100 shorter events, 23.4 us)
Async XLA Ops:
  0.7 35.0 %copy-start.24 = (s32[2]{0:T(128)}, s32[2]{0:T(128)S(1)}, u32[]{:S(2)}) copy-start(s32[2]{0:T(128)S(1)} %pad_add_fusion.place_ref) | copy-start | bytes 28
  5.0 12.4 %collective-permute-start.2 = (s32[96,128]{1,0:T(8,128)S(1)}, s32[96,128]{1,0:T(8,128)S(1)}, u32[]{:S(2)}, u32[]{:S(2)}) collective-permute-start(s32[96,128]{1,0:T(8,128)S(1)} %get-tuple-element.23), channel_id=1, source_target_pairs={{0,1},{1,0},{2,3},{3,2},{4,5},{5,4},{6,7},{7,6},{8,9},{9,8},{10,11... | collective-permute-start | bytes 147464 | tf_op jit(solution)/shard_map/ppermute | solution.py:677
  8.3 13.6 %all-to-all-start = ((f32[8,16,128]{2,1,0:T(8,128)}), f32[8,16,128]{2,1,0:T(8,128)S(1)}, u32[]{:S(2)}, u32[]{:S(2)}) async-start(f32[8,16,128]{2,1,0:T(8,128)} %pool.1.pool_ref), calls=%async_computation | async-start | bytes 131072 | tf_op jit(solution)/shard_map/all_to_all | solution.py:688
  14.8 8.6 %collective-permute-start = (f32[256,128]{1,0:T(8,128)S(1)}, f32[256,128]{1,0:T(8,128)S(1)}, u32[]{:S(2)}, u32[]{:S(2)}) collective-permute-start(f32[256,128]{1,0:T(8,128)S(1)} %get-tuple-element.21), channel_id=1, source_target_pairs={{0,4},{2,6},{4,8},{5,1},{6,10},{7,3},{8,12},{9,5},{10,14},{11,7},{... | collective-permute-start | bytes 393224 | tf_op jit(solution)/shard_map/ppermute | solution.py:685
  16.0 7.3 %collective-permute-start.1 = (f32[256,128]{1,0:T(8,128)S(1)}, f32[256,128]{1,0:T(8,128)S(1)}, u32[]{:S(2)}, u32[]{:S(2)}) collective-permute-start(f32[256,128]{1,0:T(8,128)S(1)} %get-tuple-element.22), channel_id=1, source_target_pairs={{0,2},{2,4},{3,1},{4,6},{5,3},{6,8},{7,5},{8,10},{9,7},{10,12},{11... | collective-permute-start | bytes 393224 | tf_op jit(solution)/shard_map/ppermute | solution.py:685
  22.8 13.0 %copy-start.8 = (f32[128,128]{1,0:T(8,128)S(1)}, f32[128,128]{1,0:T(8,128)}, u32[]{:S(2)}) copy-start(f32[128,128]{1,0:T(8,128)} %w_msg_ref.3) | copy-start | bytes 196612
  22.8 13.0 %copy-start.10 = (f32[128,128]{1,0:T(8,128)S(1)}, f32[128,128]{1,0:T(8,128)}, u32[]{:S(2)}) copy-start(f32[128,128]{1,0:T(8,128)} %w_send_ref.3) | copy-start | bytes 196612
  22.8 13.0 %copy-start.12 = (f32[128,128]{1,0:T(8,128)S(1)}, f32[128,128]{1,0:T(8,128)}, u32[]{:S(2)}) copy-start(f32[128,128]{1,0:T(8,128)} %w_recv_ref.3) | copy-start | bytes 196612
  22.8 13.0 %copy-start.17 = (s32[3072]{0:T(1024)S(1)}, s32[3072]{0:T(1024)}, u32[]{:S(2)}) copy-start(s32[3072]{0:T(1024)} %param.26) | copy-start | bytes 36868
  22.8 13.0 %copy-start.19 = (s32[3072]{0:T(1024)S(1)}, s32[3072]{0:T(1024)}, u32[]{:S(2)}) copy-start(s32[3072]{0:T(1024)} %param.27) | copy-start | bytes 36868
  23.4 12.3 %collective-permute-start.3 = (f32[512,128]{1,0:T(8,128)S(1)}, f32[512,128]{1,0:T(8,128)S(1)}, u32[]{:S(2)}, u32[]{:S(2)}) collective-permute-start(f32[512,128]{1,0:T(8,128)S(1)} %join_halo.1.halo_ref), channel_id=1, source_target_pairs={{0,1},{1,0},{2,3},{3,2},{4,5},{5,4},{6,7},{7,6},{8,9},{9,8},{10,11... | collective-permute-start | bytes 786440 | tf_op jit(solution)/shard_map/ppermute | solution.py:677
  26.7 20.8 %all-to-all-start.1 = ((f32[16,72,128]{2,1,0:T(8,128)}), f32[16,72,128]{2,1,0:T(8,128)S(1)}, u32[]{:S(2)}, u32[]{:S(2)}) async-start(f32[16,72,128]{2,1,0:T(8,128)} %spread.1.spread_ref), calls=%async_computation.1 | async-start | bytes 1179648 | tf_op jit(solution)/shard_map/all_to_all | solution.py:688
  45.9 6.8 %collective-permute-start.4 = (f32[1024,128]{1,0:T(8,128)S(1)}, f32[1024,128]{1,0:T(8,128)S(1)}, u32[]{:S(2)}, u32[]{:S(2)}) collective-permute-start(f32[1024,128]{1,0:T(8,128)S(1)} %get-tuple-element.25.agg_ref), channel_id=1, source_target_pairs={{0,1},{1,0},{2,3},{3,2},{4,5},{5,4},{6,7},{7,6},{8,9},{9,8},{10,11... | collective-permute-start | bytes 1572872 | tf_op jit(solution)/shard_map/ppermute | solution.py:677
  50.1 2.6 %collective-permute-start.5 = (f32[64,128]{1,0:T(8,128)S(1)}, f32[64,128]{1,0:T(8,128)S(1)}, u32[]{:S(2)}, u32[]{:S(2)}) collective-permute-start(f32[64,128]{1,0:T(8,128)S(1)} %coarse_sum.1.sums_ref), channel_id=1, source_target_pairs={{0,1},{1,0},{2,3},{3,2},{4,5},{5,4},{6,7},{7,6},{8,9},{9,8},{10,11... | collective-permute-start | bytes 98312 | tf_op jit(solution)/shard_map/ppermute | solution.py:677
  68.5 1.5 %collective-permute-start.7 = (f32[3,128,128]{2,1,0:T(8,128)S(1)}, f32[3,128,128]{2,1,0:T(8,128)S(1)}, u32[]{:S(2)}, u32[]{:S(2)}) collective-permute-start(f32[3,128,128]{2,1,0:T(8,128)S(1)} %get-tuple-element.31), channel_id=1, source_target_pairs={{0,1},{1,0},{2,3},{3,2},{4,5},{5,4},{6,7},{7,6},{8,9},{9,8},{10,11... | collective-permute-start | bytes 589832 | tf_op jit(solution)/shard_map/ppermute | solution.py:677
  69.0 8.9 %collective-permute-start.8 = (f32[512,128]{1,0:T(8,128)S(1)}, f32[512,128]{1,0:T(8,128)S(1)}, u32[]{:S(2)}, u32[]{:S(2)}) collective-permute-start(f32[512,128]{1,0:T(8,128)S(1)} %get-tuple-element.36), channel_id=1, source_target_pairs={{0,1},{1,0},{2,3},{3,2},{4,5},{5,4},{6,7},{7,6},{8,9},{9,8},{10,11... | collective-permute-start | bytes 786440 | tf_op jit(solution)/shard_map/ppermute | solution.py:677
  70.8 13.0 %all-to-all-start.2 = ((f32[16,32,128]{2,1,0:T(8,128)}), f32[16,32,128]{2,1,0:T(8,128)S(1)}, u32[]{:S(2)}, u32[]{:S(2)}) async-start(f32[16,32,128]{2,1,0:T(8,128)} %bitcast.8), calls=%async_computation.2 | async-start | bytes 524288 | tf_op jit(solution)/shard_map/all_to_all | solution.py:688
  85.1 13.1 %all-to-all-start.3 = ((f32[8,48,128]{2,1,0:T(8,128)}), f32[8,48,128]{2,1,0:T(8,128)S(1)}, u32[]{:S(2)}, u32[]{:S(2)}) async-start(f32[8,48,128]{2,1,0:T(8,128)} %get-tuple-element.39), calls=%async_computation.3 | async-start | bytes 393216 | tf_op jit(solution)/shard_map/all_to_all | solution.py:688
  89.8 13.1 %collective-permute-start.9 = (f32[272,128]{1,0:T(8,128)S(1)}, f32[272,128]{1,0:T(8,128)S(1)}, u32[]{:S(2)}, u32[]{:S(2)}) collective-permute-start(f32[272,128]{1,0:T(8,128)S(1)} %get-tuple-element.37), channel_id=1, source_target_pairs={{0,254},{1,3},{2,0},{3,5},{4,2},{5,7},{6,4},{7,9},{8,6},{9,11},{10... | collective-permute-start | bytes 417800 | tf_op jit(solution)/shard_map/ppermute | solution.py:685
  91.3 15.9 %collective-permute-start.6 = (f32[1024,128]{1,0:T(8,128)S(1)}, f32[1024,128]{1,0:T(8,128)S(1)}, u32[]{:S(2)}, u32[]{:S(2)}) collective-permute-start(f32[1024,128]{1,0:T(8,128)S(1)} %get-tuple-element.30.own_ref), channel_id=1, source_target_pairs={{0,1},{1,0},{2,3},{3,2},{4,5},{5,4},{6,7},{7,6},{8,9},{9,8},{10,11... | collective-permute-start | bytes 1572872 | tf_op jit(solution)/shard_map/ppermute | solution.py:677
  95.2 7.7 %collective-permute-start.10 = (f32[256,128]{1,0:T(8,128)S(1)}, f32[256,128]{1,0:T(8,128)S(1)}, u32[]{:S(2)}, u32[]{:S(2)}) collective-permute-start(f32[256,128]{1,0:T(8,128)S(1)} %get-tuple-element.38), channel_id=1, source_target_pairs={{1,5},{3,7},{4,0},{5,9},{6,2},{7,11},{8,4},{9,13},{10,6},{11,15},{... | collective-permute-start | bytes 393224 | tf_op jit(solution)/shard_map/ppermute | solution.py:685
  99.3 14.7 %all-to-all-start.4 = ((f32[16,104,128]{2,1,0:T(8,128)}), f32[16,104,128]{2,1,0:T(8,128)S(1)}, u32[]{:S(2)}, u32[]{:S(2)}) async-start(f32[16,104,128]{2,1,0:T(8,128)} %plane.1), calls=%async_computation.4 | async-start | bytes 1703936 | tf_op jit(solution)/shard_map/all_to_all | solution.py:688
  102.9 5.3 %collective-permute-start.11 = (f32[528,128]{1,0:T(8,128)S(1)}, f32[528,128]{1,0:T(8,128)S(1)}, u32[]{:S(2)}, u32[]{:S(2)}) collective-permute-start(f32[528,128]{1,0:T(8,128)S(1)} %constant_dynamic-update-slice_fusion.back_ref), channel_id=1, source_target_pairs={{0,1},{1,0},{2,3},{3,2},{4,5},{5,4},{6,7},{7,6},{8,9},{9,8},{10,11... | collective-permute-start | bytes 811016 | tf_op jit(solution)/shard_map/ppermute | solution.py:677
  115.0 6.4 %collective-permute-start.12 = (f32[544,128]{1,0:T(8,128)S(1)}, f32[544,128]{1,0:T(8,128)S(1)}, u32[]{:S(2)}, u32[]{:S(2)}) collective-permute-start(f32[544,128]{1,0:T(8,128)S(1)} %coarse_back_sum.1.mine_ref), channel_id=1, source_target_pairs={{0,1},{1,0},{2,3},{3,2},{4,5},{5,4},{6,7},{7,6},{8,9},{9,8},{10,11... | collective-permute-start | bytes 835592 | tf_op jit(solution)/shard_map/ppermute | solution.py:677
  (27 other events, 129.2 us)

commit v5 on v4

--- a/solution.py
+++ b/solution.py
@@ -125,22 +125,11 @@
     return jnp.where(core == 0, first, second)
 
 
-def pool_kernel(
-    sizes, place_ref, cells_hbm, pool_hbm, out_ref, cells, pool, sems
-):
-    coarse_block, coarse_total, scale = sizes
-    loads = [
-        pltpu.make_async_copy(cells_hbm, cells, sems.at[0]),
-        pltpu.make_async_copy(pool_hbm, pool, sems.at[1]),
-    ]
-    for load in loads:
-        load.start()
-    for load in loads:
-        load.wait()
+def pool_kernel(sizes, place_ref, cells, pool, out_ref):
+    coarse_block, scale = sizes
     hot = []
     for chunk in range(cells.shape[0] // LANES):
-        row = relative_pool(pool[chunk : chunk + 1, :], place_ref[0], coarse_block, coarse_total)
-        hot.append(one_hot_columns(row, 0, 2 * coarse_block))
+        hot.append(one_hot_columns(pool[chunk : chunk + 1, :], 0, 2 * coarse_block))
     part = own_half(fold(mm(jnp.concatenate(hot, axis=1), split(cells[...]))) * scale, place_ref[1])
     out_ref[...] = jnp.broadcast_to(part[None], out_ref.shape)
 
@@ -370,7 +359,6 @@
         down, across = [], []
         for chunk in range(part // LANES):
             row = pool_ref[pl.ds(step * (part // LANES) + chunk, 1), :]
-            row = relative_pool(row, place_ref[0], coarse_block, coarse_total)
             down.append(one_hot_rows(row, LANES))
             across.append(one_hot_columns(row, 0, rows))
         inner = fold(
@@ -583,7 +571,7 @@
     pooled = split(jnp.concatenate([pooled, jnp.zeros((LANES - rows, LANES), F32)], axis=0))
     down = []
     for chunk in range(count // LANES):
-        row = relative_pool(pool_ref[chunk : chunk + 1, :], place_ref[0], coarse_block, coarse_total)
+        row = pool_ref[chunk : chunk + 1, :]
         down.append(one_hot_rows(row, LANES))
     out_ref[...] = most_ref[...] + fold(mm(jnp.concatenate(down, axis=0), pooled))
 
@@ -670,7 +658,7 @@
         return array.reshape(-1, LANES)
 
     send_rows, recv_rows = lanes(senders), lanes(receivers)
-    pool_rows = lanes(pool_map)
+    pool_rows = lanes(relative_pool(pool_map, place[0], coarse_block, coarse_total))
     coarse_send, coarse_recv = lanes(coarse_senders), lanes(coarse_receivers)
 
     def other_core(array):
@@ -691,19 +679,14 @@
     groups = (blocks * half // LANES) * rows
     edge_keys = pltpu.VMEM((2 * chunks, LANES), jnp.int32)
     (copies,) = call(
-        functools.partial(pool_kernel, sizes + (pool_scale,)),
+        functools.partial(pool_kernel, (coarse_block, pool_scale)),
         [full(line, coarse_block, latent)],
-        [
-            pltpu.VMEM((count, latent), F32),
-            pltpu.VMEM((count // LANES, LANES), jnp.int32),
-            pltpu.SemaphoreType.DMA((2,)),
-        ],
+        [],
         1,
         "pool",
         place,
         cells,
         pool_rows,
-        far=(1, 2),
     )
     parts = exchange(copies, LINE).reshape(line, coarse_block, latent)
     far, near, edge_both = call(

time: 124 us -> 124 us (level)
    unnamed x67 -> x63, local copies, waits for them, and re-layouts: 3.98 us -> 3.39 us
where the time goes in v5:
time: 124 us; the launch traced here: 123 us
  starting transfers between devices  56.4 us (45%)
  Pallas kernels  40.9 us (33%)
  waiting for transfers between devices  19.9 us (16%)
  local copies, waits for them, and re-layouts  3.41 us (3%)
  other arithmetic  1.53 us (1%)
    pallas_call x16, Pallas kernels, call(): pl.pallas_call(kernel, out_shape=outs, in_specs=specs, out_specs=[outer i...  40.9 us
    all_to_all x5, starting transfers between devices, exchange(): return lax.all_to_all(array.reshape(-1, latent), axes, 0, 0, tiled=True)  28.4 us
    ppermute x9, starting transfers between devices, other_core(): return lax.ppermute(array, 'coarse', [(0, 1), (1, 0)])  22.6 us
    all_to_all x5, waiting for transfers between devices, exchange(): return lax.all_to_all(array.reshape(-1, latent), axes, 0, 0, tiled=True)  15.2 us
    ppermute x4, starting transfers between devices, along(): return lax.ppermute(array, SPACE + ('coarse',), pairs)  5.32 us
    ppermute x9, waiting for transfers between devices, other_core(): return lax.ppermute(array, 'coarse', [(0, 1), (1, 0)])  4.16 us
    unnamed x63, local copies, waits for them, and re-layouts  3.39 us
  transfers between devices with their start and end apart: 18, of which 10 were waited for; matrix products, arithmetic and copies ran while one was open for 1% of the time, Pallas kernels for 16%

profile of v5, /device:TPU:1, one launch (start us, length us, event | category | flops | bytes accessed | tf_op | source)
XLA Modules:
  0.0 123.3 jit_solution(9578367786964822802)
XLA Ops:
  4.9 3.3 %collective-permute-start.2 = (s32[96,128]{1,0:T(8,128)S(1)}, s32[96,128]{1,0:T(8,128)S(1)}, u32[]{:S(2)}, u32[]{:S(2)}) collective-permute-start(s32[96,128]{1,0:T(8,128)S(1)} %get-tuple-element.23), channel_id=1, source_target_pairs={{0,1},{1,0},{2,3},{3,2},{4,5},{5,4},{6,7},{7,6},{8,9},{9,8},{10,11... | collective-permute-start | bytes 147464 | tf_op jit(solution)/shard_map/ppermute | solution.py:665
  8.2 6.5 %all-to-all-start = ((f32[8,16,128]{2,1,0:T(8,128)}), f32[8,16,128]{2,1,0:T(8,128)S(1)}, u32[]{:S(2)}, u32[]{:S(2)}) async-start(f32[8,16,128]{2,1,0:T(8,128)} %pool.1.pool_ref), calls=%async_computation | async-start | bytes 131072 | tf_op jit(solution)/shard_map/all_to_all | solution.py:676
  17.3 2.3 %count_into.1.count_ref = f32[256,128]{1,0:T(8,128)S(1)} custom-call(s32[2]{0:T(128)S(1)} %pad_add_fusion.place_ref, s32[48,128]{1,0:T(8,128)S(1)} %bitcast.12, s32[48,128]{1,0:T(8,128)S(1)} %get-tuple-element.41.send_other_ref, s32[48,128]{1,0:T(8,128)S(1)} %bitcast.15, s32[48,128]{1,0:T(8,128)S(1)} %get-tuple-element.40.recv_other_ref), custom_call_target="tpu_custom_call" | custom-call | flops 3300000000 | bytes 3000000 | tf_op jit(solution)/shard_map/count_into/pallas_call | solution.py:608
  19.6 2.2 %all-to-all-done.parts_ref = f32[8,16,128]{2,1,0:T(8,128)S(1)} async-done(((f32[8,16,128]{2,1,0:T(8,128)}), f32[8,16,128]{2,1,0:T(8,128)S(1)}, u32[]{:S(2)}, u32[]{:S(2)}) %all-to-all-start) | async-done | bytes 65568 | tf_op jit(solution)/shard_map/all_to_all | solution.py:676
  23.3 3.3 %collective-permute-start.3 = (f32[512,128]{1,0:T(8,128)S(1)}, f32[512,128]{1,0:T(8,128)S(1)}, u32[]{:S(2)}, u32[]{:S(2)}) collective-permute-start(f32[512,128]{1,0:T(8,128)S(1)} %join_halo.1.halo_ref), channel_id=1, source_target_pairs={{0,1},{1,0},{2,3},{3,2},{4,5},{5,4},{6,7},{7,6},{8,9},{9,8},{10,11... | collective-permute-start | bytes 786440 | tf_op jit(solution)/shard_map/ppermute | solution.py:665
  26.6 9.0 %all-to-all-start.1 = ((f32[16,72,128]{2,1,0:T(8,128)}), f32[16,72,128]{2,1,0:T(8,128)S(1)}, u32[]{:S(2)}, u32[]{:S(2)}) async-start(f32[16,72,128]{2,1,0:T(8,128)} %spread.1.spread_ref), calls=%async_computation.1 | async-start | bytes 1179648 | tf_op jit(solution)/shard_map/all_to_all | solution.py:676
  35.7 10.0 %edges.1 = (f32[3072,128]{1,0:T(8,128)}, f32[1024,128]{1,0:T(8,128)S(1)}) custom-call(s32[2]{0:T(128)S(1)} %pad_add_fusion.place_ref, f32[1024,128]{1,0:T(8,128)S(1)} %copy-done.2, f32[512,128]{1,0:T(8,128)S(1)} %join_halo.1.halo_ref, f32[512,128]{1,0:T(8,128)S(1)} %collective-permute-done.3.halo_other_ref, f32[128,128]{1,0:T(8,128)S(1)} %copy-done.10, ...), custom_call_target="tpu_custom_call" | custom-call | flops 3300000000 | bytes 3000000 | tf_op jit(solution)/shard_map/edges/pallas_call | solution.py:608
  50.1 1.7 %collective-permute-start.5 = (f32[64,128]{1,0:T(8,128)S(1)}, f32[64,128]{1,0:T(8,128)S(1)}, u32[]{:S(2)}, u32[]{:S(2)}) collective-permute-start(f32[64,128]{1,0:T(8,128)S(1)} %coarse_sum.1.sums_ref), channel_id=1, source_target_pairs={{0,1},{1,0},{2,3},{3,2},{4,5},{5,4},{6,7},{7,6},{8,9},{9,8},{10,11... | collective-permute-start | bytes 98312 | tf_op jit(solution)/shard_map/ppermute | solution.py:665
  52.7 3.7 %nodes.1 = (f32[1024,128]{1,0:T(8,128)S(1)}, f32[1024,128]{1,0:T(8,128)S(1)}, f32[64,128]{1,0:T(8,128)S(1)}, f32[128,128]{1,0:T(8,128)S(1)}, f32[4,128,128]{2,1,0:T(8,128)S(1)}) custom-call(s32[2]{0:T(128)S(1)} %copy-done.24, f32[1024,128]{1,0:T(8,128)S(1)} %copy-done.2, f32[1024,128]{1,0:T(8,128)S(1)} %get-tuple-element.25.agg_ref, ...), custom_call_target="tpu_custom_call" | custom-call | flops 6600000000 | bytes 6000000 | tf_op jit(solution)/shard_map/nodes/pallas_call | solution.py:608
  57.0 4.5 %edges_back.1 = (bf16[3072,256]{1,0:T(8,128)(2,1)S(1)}, f32[128,128]{1,0:T(8,128)S(1)}) custom-call(f32[128,128]{1,0:T(8,128)S(1)} %copy-done.9, s32[24,128]{1,0:T(8,128)S(1)} %bitcast.20, f32[3072,128]{1,0:T(8,128)S(1)} %copy-done.26, f32[1024,128]{1,0:T(8,128)S(1)} %get-tuple-element.26.d_agg_ref), custom_call_target="tpu_custom_call" | custom-call | flops 5500000256 | bytes 5000000 | tf_op jit(solution)/shard_map/edges_back/pallas_call | solution.py:608
  61.6 7.0 %edges_table.1 = (f32[3,128,128]{2,1,0:T(8,128)S(1)}, f32[512,128]{1,0:T(8,128)S(1)}, f32[512,128]{1,0:T(8,128)S(1)}, f32[1024,128]{1,0:T(8,128)S(1)}) custom-call(s32[2]{0:T(128)S(1)} %copy-done.24, f32[1024,128]{1,0:T(8,128)S(1)} %copy-done.2, f32[512,128]{1,0:T(8,128)S(1)} %join_halo.1.halo_ref, f32[512,128]{1,0:T(8,128)S(1)} %collective-permute-done.3.halo_other_ref, ...), custom_call_target="tpu_custom_call" | custom-call | flops 8800000000 | bytes 8000000 | tf_op jit(solution)/shard_map/edges_table/pallas_call | solution.py:608
  70.9 4.6 %all-to-all-start.2 = ((f32[16,32,128]{2,1,0:T(8,128)}), f32[16,32,128]{2,1,0:T(8,128)S(1)}, u32[]{:S(2)}, u32[]{:S(2)}) async-start(f32[16,32,128]{2,1,0:T(8,128)} %bitcast.8), calls=%async_computation.2 | async-start | bytes 524288 | tf_op jit(solution)/shard_map/all_to_all | solution.py:676
  75.6 2.3 %count_from.1.count_ref = f32[256,128]{1,0:T(8,128)S(1)} custom-call(s32[2]{0:T(128)S(1)} %copy-done.25, s32[48,128]{1,0:T(8,128)S(1)} %bitcast.13, s32[48,128]{1,0:T(8,128)S(1)} %get-tuple-element.41.send_other_ref, s32[48,128]{1,0:T(8,128)S(1)} %bitcast.16, s32[48,128]{1,0:T(8,128)S(1)} %get-tuple-element.40.recv_other_ref, ...), custom_call_target="tpu_custom_call" | custom-call | flops 3300000000 | bytes 3000000 | tf_op jit(solution)/shard_map/count_from/pallas_call | solution.py:608
  77.9 6.0 %all-to-all-done.2.parts_ref = f32[16,32,128]{2,1,0:T(8,128)S(1)} async-done(((f32[16,32,128]{2,1,0:T(8,128)}), f32[16,32,128]{2,1,0:T(8,128)S(1)}, u32[]{:S(2)}, u32[]{:S(2)}) %all-to-all-start.2) | async-done | bytes 262176 | tf_op jit(solution)/shard_map/all_to_all | solution.py:676
  85.2 4.7 %all-to-all-start.3 = ((f32[8,48,128]{2,1,0:T(8,128)}), f32[8,48,128]{2,1,0:T(8,128)S(1)}, u32[]{:S(2)}, u32[]{:S(2)}) async-start(f32[8,48,128]{2,1,0:T(8,128)} %get-tuple-element.39), calls=%async_computation.3 | async-start | bytes 393216 | tf_op jit(solution)/shard_map/all_to_all | solution.py:676
  89.9 1.5 %collective-permute-start.9 = (f32[272,128]{1,0:T(8,128)S(1)}, f32[272,128]{1,0:T(8,128)S(1)}, u32[]{:S(2)}, u32[]{:S(2)}) collective-permute-start(f32[272,128]{1,0:T(8,128)S(1)} %get-tuple-element.37), channel_id=1, source_target_pairs={{0,254},{1,3},{2,0},{3,5},{4,2},{5,7},{6,4},{7,9},{8,6},{9,11},{10... | collective-permute-start | bytes 417800 | tf_op jit(solution)/shard_map/ppermute | solution.py:673
  91.3 4.0 %collective-permute-start.6 = (f32[1024,128]{1,0:T(8,128)S(1)}, f32[1024,128]{1,0:T(8,128)S(1)}, u32[]{:S(2)}, u32[]{:S(2)}) collective-permute-start(f32[1024,128]{1,0:T(8,128)S(1)} %get-tuple-element.30.own_ref), channel_id=1, source_target_pairs={{0,1},{1,0},{2,3},{3,2},{4,5},{5,4},{6,7},{7,6},{8,9},{9,8},{10,11... | collective-permute-start | bytes 1572872 | tf_op jit(solution)/shard_map/ppermute | solution.py:665
  96.6 1.7 %all-to-all-done.3.parts_ref = f32[8,48,128]{2,1,0:T(8,128)S(1)} async-done(((f32[8,48,128]{2,1,0:T(8,128)}), f32[8,48,128]{2,1,0:T(8,128)S(1)}, u32[]{:S(2)}, u32[]{:S(2)}) %all-to-all-start.3) | async-done | bytes 196640 | tf_op jit(solution)/shard_map/all_to_all | solution.py:676
  99.3 3.6 %all-to-all-start.4 = ((f32[16,104,128]{2,1,0:T(8,128)}), f32[16,104,128]{2,1,0:T(8,128)S(1)}, u32[]{:S(2)}, u32[]{:S(2)}) async-start(f32[16,104,128]{2,1,0:T(8,128)} %plane.1), calls=%async_computation.4 | async-start | bytes 1703936 | tf_op jit(solution)/shard_map/all_to_all | solution.py:676
  103.0 4.2 %collective-permute-start.11 = (f32[528,128]{1,0:T(8,128)S(1)}, f32[528,128]{1,0:T(8,128)S(1)}, u32[]{:S(2)}, u32[]{:S(2)}) collective-permute-start(f32[528,128]{1,0:T(8,128)S(1)} %constant_dynamic-update-slice_fusion.back_ref), channel_id=1, source_target_pairs={{0,1},{1,0},{2,3},{3,2},{4,5},{5,4},{6,7},{7,6},{8,9},{9,8},{10,11... | collective-permute-start | bytes 811016 | tf_op jit(solution)/shard_map/ppermute | solution.py:665
  108.4 1.5 %gather_back.1.most_ref = f32[1024,128]{1,0:T(8,128)S(1)} custom-call(s32[2]{0:T(128)S(1)} %copy-done.25, f32[1024,128]{1,0:T(8,128)S(1)} %get-tuple-element.30.own_ref, f32[1024,128]{1,0:T(8,128)S(1)} %collective-permute-done.6.other_ref, f32[528,128]{1,0:T(8,128)S(1)} %constant_dynamic-update-slice_fusion.back_ref, ...), custom_call_target="tpu_custom_call" | custom-call | flops 3300000000 | bytes 3000000 | tf_op jit(solution)/shard_map/gather_back/pallas_call | solution.py:608
  109.9 4.1 %all-to-all-done.4.packed_ref = f32[16,104,128]{2,1,0:T(8,128)S(1)} async-done(((f32[16,104,128]{2,1,0:T(8,128)}), f32[16,104,128]{2,1,0:T(8,128)S(1)}, u32[]{:S(2)}, u32[]{:S(2)}) %all-to-all-start.4) | async-done | bytes 852000 | tf_op jit(solution)/shard_map/all_to_all | solution.py:676
  115.1 5.2 %collective-permute-start.12 = (f32[544,128]{1,0:T(8,128)S(1)}, f32[544,128]{1,0:T(8,128)S(1)}, u32[]{:S(2)}, u32[]{:S(2)}) collective-permute-start(f32[544,128]{1,0:T(8,128)S(1)} %coarse_back_sum.1.mine_ref), channel_id=1, source_target_pairs={{0,1},{1,0},{2,3},{3,2},{4,5},{5,4},{6,7},{7,6},{8,9},{9,8},{10,11... | collective-permute-start | bytes 835592 | tf_op jit(solution)/shard_map/ppermute | solution.py:665
  121.5 1.8 %finish.1 = (f32[1024,128]{1,0:T(8,128)}, f32[8,128,128]{2,1,0:T(8,128)}) custom-call(s32[2]{0:T(128)S(1)} %copy-done.25, f32[1024,128]{1,0:T(8,128)S(1)} %gather_back.1.most_ref, f32[64,128]{1,0:T(8,128)S(1)} %copy-done.30, f32[528,128]{1,0:T(8,128)S(1)} %constant_dynamic-update-slice_fusion.back_ref, ...), custom_call_target="tpu_custom_call" | custom-call | flops 2200000000 | bytes 2000000 | tf_op jit(solution)/shard_map/finish/pallas_call | solution.py:608
  (97 shorter events, 23.5 us)
Async XLA Ops:
  0.7 34.9 %copy-start.22 = (s32[2]{0:T(128)}, s32[2]{0:T(128)S(1)}, u32[]{:S(2)}) copy-start(s32[2]{0:T(128)S(1)} %pad_add_fusion.place_ref) | copy-start | bytes 28
  4.9 12.4 %collective-permute-start.2 = (s32[96,128]{1,0:T(8,128)S(1)}, s32[96,128]{1,0:T(8,128)S(1)}, u32[]{:S(2)}, u32[]{:S(2)}) collective-permute-start(s32[96,128]{1,0:T(8,128)S(1)} %get-tuple-element.23), channel_id=1, source_target_pairs={{0,1},{1,0},{2,3},{3,2},{4,5},{5,4},{6,7},{7,6},{8,9},{9,8},{10,11... | collective-permute-start | bytes 147464 | tf_op jit(solution)/shard_map/ppermute | solution.py:665
  8.2 13.6 %all-to-all-start = ((f32[8,16,128]{2,1,0:T(8,128)}), f32[8,16,128]{2,1,0:T(8,128)S(1)}, u32[]{:S(2)}, u32[]{:S(2)}) async-start(f32[8,16,128]{2,1,0:T(8,128)} %pool.1.pool_ref), calls=%async_computation | async-start | bytes 131072 | tf_op jit(solution)/shard_map/all_to_all | solution.py:676
  14.7 8.6 %collective-permute-start = (f32[256,128]{1,0:T(8,128)S(1)}, f32[256,128]{1,0:T(8,128)S(1)}, u32[]{:S(2)}, u32[]{:S(2)}) collective-permute-start(f32[256,128]{1,0:T(8,128)S(1)} %get-tuple-element.21), channel_id=1, source_target_pairs={{0,4},{2,6},{4,8},{5,1},{6,10},{7,3},{8,12},{9,5},{10,14},{11,7},{... | collective-permute-start | bytes 393224 | tf_op jit(solution)/shard_map/ppermute | solution.py:673
  16.0 7.3 %collective-permute-start.1 = (f32[256,128]{1,0:T(8,128)S(1)}, f32[256,128]{1,0:T(8,128)S(1)}, u32[]{:S(2)}, u32[]{:S(2)}) collective-permute-start(f32[256,128]{1,0:T(8,128)S(1)} %get-tuple-element.22), channel_id=1, source_target_pairs={{0,2},{2,4},{3,1},{4,6},{5,3},{6,8},{7,5},{8,10},{9,7},{10,12},{11... | collective-permute-start | bytes 393224 | tf_op jit(solution)/shard_map/ppermute | solution.py:673
  22.7 13.0 %copy-start.8 = (f32[128,128]{1,0:T(8,128)S(1)}, f32[128,128]{1,0:T(8,128)}, u32[]{:S(2)}) copy-start(f32[128,128]{1,0:T(8,128)} %w_msg_ref.3) | copy-start | bytes 196612
  22.7 13.0 %copy-start.10 = (f32[128,128]{1,0:T(8,128)S(1)}, f32[128,128]{1,0:T(8,128)}, u32[]{:S(2)}) copy-start(f32[128,128]{1,0:T(8,128)} %w_send_ref.3) | copy-start | bytes 196612
  22.7 13.0 %copy-start.12 = (f32[128,128]{1,0:T(8,128)S(1)}, f32[128,128]{1,0:T(8,128)}, u32[]{:S(2)}) copy-start(f32[128,128]{1,0:T(8,128)} %w_recv_ref.3) | copy-start | bytes 196612
  22.7 13.0 %copy-start.17 = (s32[3072]{0:T(1024)S(1)}, s32[3072]{0:T(1024)}, u32[]{:S(2)}) copy-start(s32[3072]{0:T(1024)} %param.26) | copy-start | bytes 36868
  22.7 13.0 %copy-start.19 = (s32[3072]{0:T(1024)S(1)}, s32[3072]{0:T(1024)}, u32[]{:S(2)}) copy-start(s32[3072]{0:T(1024)} %param.27) | copy-start | bytes 36868
  23.3 12.3 %collective-permute-start.3 = (f32[512,128]{1,0:T(8,128)S(1)}, f32[512,128]{1,0:T(8,128)S(1)}, u32[]{:S(2)}, u32[]{:S(2)}) collective-permute-start(f32[512,128]{1,0:T(8,128)S(1)} %join_halo.1.halo_ref), channel_id=1, source_target_pairs={{0,1},{1,0},{2,3},{3,2},{4,5},{5,4},{6,7},{7,6},{8,9},{9,8},{10,11... | collective-permute-start | bytes 786440 | tf_op jit(solution)/shard_map/ppermute | solution.py:665
  26.6 20.8 %all-to-all-start.1 = ((f32[16,72,128]{2,1,0:T(8,128)}), f32[16,72,128]{2,1,0:T(8,128)S(1)}, u32[]{:S(2)}, u32[]{:S(2)}) async-start(f32[16,72,128]{2,1,0:T(8,128)} %spread.1.spread_ref), calls=%async_computation.1 | async-start | bytes 1179648 | tf_op jit(solution)/shard_map/all_to_all | solution.py:676
  45.8 6.9 %collective-permute-start.4 = (f32[1024,128]{1,0:T(8,128)S(1)}, f32[1024,128]{1,0:T(8,128)S(1)}, u32[]{:S(2)}, u32[]{:S(2)}) collective-permute-start(f32[1024,128]{1,0:T(8,128)S(1)} %get-tuple-element.25.agg_ref), channel_id=1, source_target_pairs={{0,1},{1,0},{2,3},{3,2},{4,5},{5,4},{6,7},{7,6},{8,9},{9,8},{10,11... | collective-permute-start | bytes 1572872 | tf_op jit(solution)/shard_map/ppermute | solution.py:665
  50.1 2.6 %collective-permute-start.5 = (f32[64,128]{1,0:T(8,128)S(1)}, f32[64,128]{1,0:T(8,128)S(1)}, u32[]{:S(2)}, u32[]{:S(2)}) collective-permute-start(f32[64,128]{1,0:T(8,128)S(1)} %coarse_sum.1.sums_ref), channel_id=1, source_target_pairs={{0,1},{1,0},{2,3},{3,2},{4,5},{5,4},{6,7},{7,6},{8,9},{9,8},{10,11... | collective-permute-start | bytes 98312 | tf_op jit(solution)/shard_map/ppermute | solution.py:665
  68.6 1.5 %collective-permute-start.7 = (f32[3,128,128]{2,1,0:T(8,128)S(1)}, f32[3,128,128]{2,1,0:T(8,128)S(1)}, u32[]{:S(2)}, u32[]{:S(2)}) collective-permute-start(f32[3,128,128]{2,1,0:T(8,128)S(1)} %get-tuple-element.31), channel_id=1, source_target_pairs={{0,1},{1,0},{2,3},{3,2},{4,5},{5,4},{6,7},{7,6},{8,9},{9,8},{10,11... | collective-permute-start | bytes 589832 | tf_op jit(solution)/shard_map/ppermute | solution.py:665
  69.0 8.9 %collective-permute-start.8 = (f32[512,128]{1,0:T(8,128)S(1)}, f32[512,128]{1,0:T(8,128)S(1)}, u32[]{:S(2)}, u32[]{:S(2)}) collective-permute-start(f32[512,128]{1,0:T(8,128)S(1)} %get-tuple-element.36), channel_id=1, source_target_pairs={{0,1},{1,0},{2,3},{3,2},{4,5},{5,4},{6,7},{7,6},{8,9},{9,8},{10,11... | collective-permute-start | bytes 786440 | tf_op jit(solution)/shard_map/ppermute | solution.py:665
  70.9 13.0 %all-to-all-start.2 = ((f32[16,32,128]{2,1,0:T(8,128)}), f32[16,32,128]{2,1,0:T(8,128)S(1)}, u32[]{:S(2)}, u32[]{:S(2)}) async-start(f32[16,32,128]{2,1,0:T(8,128)} %bitcast.8), calls=%async_computation.2 | async-start | bytes 524288 | tf_op jit(solution)/shard_map/all_to_all | solution.py:676
  85.2 13.2 %all-to-all-start.3 = ((f32[8,48,128]{2,1,0:T(8,128)}), f32[8,48,128]{2,1,0:T(8,128)S(1)}, u32[]{:S(2)}, u32[]{:S(2)}) async-start(f32[8,48,128]{2,1,0:T(8,128)} %get-tuple-element.39), calls=%async_computation.3 | async-start | bytes 393216 | tf_op jit(solution)/shard_map/all_to_all | solution.py:676
  89.9 13.1 %collective-permute-start.9 = (f32[272,128]{1,0:T(8,128)S(1)}, f32[272,128]{1,0:T(8,128)S(1)}, u32[]{:S(2)}, u32[]{:S(2)}) collective-permute-start(f32[272,128]{1,0:T(8,128)S(1)} %get-tuple-element.37), channel_id=1, source_target_pairs={{0,254},{1,3},{2,0},{3,5},{4,2},{5,7},{6,4},{7,9},{8,6},{9,11},{10... | collective-permute-start | bytes 417800 | tf_op jit(solution)/shard_map/ppermute | solution.py:673
  91.3 15.9 %collective-permute-start.6 = (f32[1024,128]{1,0:T(8,128)S(1)}, f32[1024,128]{1,0:T(8,128)S(1)}, u32[]{:S(2)}, u32[]{:S(2)}) collective-permute-start(f32[1024,128]{1,0:T(8,128)S(1)} %get-tuple-element.30.own_ref), channel_id=1, source_target_pairs={{0,1},{1,0},{2,3},{3,2},{4,5},{5,4},{6,7},{7,6},{8,9},{9,8},{10,11... | collective-permute-start | bytes 1572872 | tf_op jit(solution)/shard_map/ppermute | solution.py:665
  95.3 7.7 %collective-permute-start.10 = (f32[256,128]{1,0:T(8,128)S(1)}, f32[256,128]{1,0:T(8,128)S(1)}, u32[]{:S(2)}, u32[]{:S(2)}) collective-permute-start(f32[256,128]{1,0:T(8,128)S(1)} %get-tuple-element.38), channel_id=1, source_target_pairs={{1,5},{3,7},{4,0},{5,9},{6,2},{7,11},{8,4},{9,13},{10,6},{11,15},{... | collective-permute-start | bytes 393224 | tf_op jit(solution)/shard_map/ppermute | solution.py:673
  99.3 14.7 %all-to-all-start.4 = ((f32[16,104,128]{2,1,0:T(8,128)}), f32[16,104,128]{2,1,0:T(8,128)S(1)}, u32[]{:S(2)}, u32[]{:S(2)}) async-start(f32[16,104,128]{2,1,0:T(8,128)} %plane.1), calls=%async_computation.4 | async-start | bytes 1703936 | tf_op jit(solution)/shard_map/all_to_all | solution.py:676
  103.0 5.3 %collective-permute-start.11 = (f32[528,128]{1,0:T(8,128)S(1)}, f32[528,128]{1,0:T(8,128)S(1)}, u32[]{:S(2)}, u32[]{:S(2)}) collective-permute-start(f32[528,128]{1,0:T(8,128)S(1)} %constant_dynamic-update-slice_fusion.back_ref), channel_id=1, source_target_pairs={{0,1},{1,0},{2,3},{3,2},{4,5},{5,4},{6,7},{7,6},{8,9},{9,8},{10,11... | collective-permute-start | bytes 811016 | tf_op jit(solution)/shard_map/ppermute | solution.py:665
  115.1 6.4 %collective-permute-start.12 = (f32[544,128]{1,0:T(8,128)S(1)}, f32[544,128]{1,0:T(8,128)S(1)}, u32[]{:S(2)}, u32[]{:S(2)}) collective-permute-start(f32[544,128]{1,0:T(8,128)S(1)} %coarse_back_sum.1.mine_ref), channel_id=1, source_target_pairs={{0,1},{1,0},{2,3},{3,2},{4,5},{5,4},{6,7},{7,6},{8,9},{9,8},{10,11... | collective-permute-start | bytes 835592 | tf_op jit(solution)/shard_map/ppermute | solution.py:665
  (25 other events, 122.1 us)
